TPU v7x, 32 devices: a whole 2x2x4 slice. The times are simulated.
32 devices in a mesh: batch: 8 (over y, x, core), seq: 4 (over z).
Axes of the slice: x: 2, y: 2, z: 4, core: 2. Of those that a mesh axis runs over, the one named last changes fastest.
Arguments:
- inputs: bfloat16 [16, 1024, 1152], P('batch', 'seq'), may hold values from -6 to 6
- conds: bfloat16 [16, 1152], P('batch'), may hold values from -6 to 6
- heights: int32 [16], P('batch'), may hold values from 16 to 32, as said below
- widths: int32 [16], P('batch'), may hold values from 12 to 32, as said below
- qkv_weight: bfloat16 [1152, 3456], P('batch'), may hold values from -0.1875 to 0.1875
- qv_bias: bfloat16 [2304], P('batch'), may hold values from -1.796875 to 1.796875
- out_weight: bfloat16 [1152, 1152], P('batch'), may hold values from -1.5 to 1.5
- out_bias: bfloat16 [1152], P('batch'), may hold values from -1.796875 to 1.796875
- up_weight: bfloat16 [1152, 4608], P('batch'), may hold values from -0.1875 to 0.1875
- up_bias: bfloat16 [4608], P('batch'), may hold values from -1.796875 to 1.796875
- down_weight: bfloat16 [4608, 1152], P('batch'), may hold values from -0.09375 to 0.09375
- down_bias: bfloat16 [1152], P('batch'), may hold values from -1.796875 to 1.796875
- mod_weight: bfloat16 [1152, 6912], P('batch'), may hold values from -0.1875 to 0.1875
- mod_bias: bfloat16 [6912], P('batch'), may hold values from -3 to 3
- cotangent: bfloat16 [16, 1024, 1152], P('batch', 'seq'), may hold values from -6 to 6
Outputs:
- output: bfloat16 [16, 1024, 1152], P('batch', 'seq')
- input_grad: float32 [16, 1024, 1152], P('batch', 'seq')
- cond_grad: float32 [16, 1152], P('batch')
- qkv_weight_grad: float32 [1152, 3456], P('batch')
- qv_bias_grad: float32 [2304], P('batch')
- out_weight_grad: float32 [1152, 1152], P('batch')
- out_bias_grad: float32 [1152], P('batch')
- up_weight_grad: float32 [1152, 4608], P('batch')
- up_bias_grad: float32 [4608], P('batch')
- down_weight_grad: float32 [4608, 1152], P('batch')
- down_bias_grad: float32 [1152], P('batch')
- mod_weight_grad: float32 [1152, 6912], P('batch')
- mod_bias_grad: float32 [6912], P('batch')
Inputs may be any that keep to these rules, and one draw needn't show every extreme that they name: In each aligned group of 2 samples, one sample drawn from the seed has heights = 32. The sample drawn from the seed also has widths = 32.
All inputs are finite; a program needn't handle non-finite values.
Results may differ from a plain program's by a relative error of at most 0.012.
The roundings to bfloat16 on the way count: a program that leaves them out, or rounds other values in their place, can miss the bound.
Values may be sent and summed in bfloat16 or wider, within the bound.
No kernel may reach another device: no remote copies, remote signals or barrier semaphores. Data moves between devices by JAX's collectives and lax.ppermute only.
A program may use at most 320 MiB of HBM per device.

v0:
```python
import jax
import jax.numpy as jnp
from jax import lax
from jax.sharding import PartitionSpec as P

HEADS = 16
HEAD = 72


def norm_forward(values):
    centre = values - jnp.mean(values, axis=-1, keepdims=True)
    factor = lax.rsqrt(jnp.mean(centre * centre, axis=-1, keepdims=True) + 1e-06)
    return (centre * factor, factor)


def norm_back(grad, normed, factor):
    return factor * (
        grad
        - jnp.mean(grad, axis=-1, keepdims=True)
        - normed * jnp.mean(grad * normed, axis=-1, keepdims=True)
    )


def paired(array):
    return array.reshape((-1, 2) + array.shape[1:])


def unpaired(array):
    return array.reshape((-1,) + array.shape[2:])


def split_heads(array):
    return array.reshape(array.shape[0], array.shape[1], HEADS, HEAD)


def masked_scores(query, whole_key, key_valid):
    scores = jnp.einsum(
        "bqhd,bkhd->bhqk",
        split_heads(query),
        split_heads(whole_key),
        preferred_element_type=jnp.float32,
    ) * HEAD ** (-0.5)
    return jnp.where(key_valid[:, None, None, :], scores, -1000000000.0)


def attend(pieces):
    query, whole_key, whole_value, key_valid = pieces
    scores = masked_scores(query, whole_key, key_valid)
    peak = jnp.max(scores, axis=-1, keepdims=True)
    expo = jnp.exp(scores - peak)
    total = jnp.sum(expo, axis=-1, keepdims=True)
    probs = (expo / total).astype(jnp.bfloat16)
    attended = jnp.einsum(
        "bhqk,bkhd->bqhd", probs, split_heads(whole_value), preferred_element_type=jnp.float32
    )
    attended = attended.reshape(query.shape).astype(jnp.bfloat16)
    return (attended, peak + jnp.log(total))


def attend_back(pieces):
    query, whole_key, whole_value, key_valid, logsum, d_attended = pieces
    scores = masked_scores(query, whole_key, key_valid)
    exact = jnp.exp(scores - logsum)
    probs = exact.astype(jnp.bfloat16)
    d_heads = split_heads(d_attended)
    d_value = jnp.einsum("bhqk,bqhd->bkhd", probs, d_heads, preferred_element_type=jnp.float32)
    d_probs = jnp.einsum(
        "bqhd,bkhd->bhqk", d_heads, split_heads(whole_value), preferred_element_type=jnp.float32
    )
    centred = jnp.sum(exact * d_probs, axis=-1, keepdims=True)
    d_scores = (exact * (d_probs - centred)).astype(jnp.bfloat16)
    d_query = jnp.einsum(
        "bhqk,bkhd->bqhd", d_scores, split_heads(whole_key), preferred_element_type=jnp.float32
    ) * HEAD ** (-0.5)
    d_key = jnp.einsum(
        "bhqk,bqhd->bkhd", d_scores, split_heads(query), preferred_element_type=jnp.float32
    ) * HEAD ** (-0.5)
    return (
        d_query.reshape(query.shape),
        d_key.reshape(whole_key.shape),
        d_value.reshape(whole_value.shape),
    )


def body(
    inputs,
    conds,
    heights,
    widths,
    qkv_weight,
    qv_bias,
    out_weight,
    out_bias,
    up_weight,
    up_bias,
    down_weight,
    down_bias,
    mod_weight,
    mod_bias,
    cotangent,
):
    gathered = (
        lax.all_gather(qkv_weight, "batch", axis=0, tiled=True),
        lax.all_gather(qv_bias, "batch", axis=0, tiled=True),
        lax.all_gather(out_weight, "batch", axis=0, tiled=True),
        lax.all_gather(out_bias, "batch", axis=0, tiled=True),
        lax.all_gather(up_weight, "batch", axis=0, tiled=True),
        lax.all_gather(up_bias, "batch", axis=0, tiled=True),
        lax.all_gather(down_weight, "batch", axis=0, tiled=True),
        lax.all_gather(down_bias, "batch", axis=0, tiled=True),
        lax.all_gather(mod_weight, "batch", axis=0, tiled=True),
        lax.all_gather(mod_bias, "batch", axis=0, tiled=True),
    )
    (
        qkv_matrix,
        qv_offset,
        out_matrix,
        out_offset,
        up_matrix,
        up_offset,
        down_matrix,
        down_offset,
        mod_matrix,
        mod_offset,
    ) = gathered
    samples = inputs.shape[0]
    slot_dev = inputs.shape[1]
    width = inputs.shape[2]
    total_slots = slot_dev * lax.axis_size("seq")
    key_valid = jnp.arange(total_slots, dtype=jnp.int32)[None, :] < (heights * widths)[:, None]
    cond_single = conds.astype(jnp.float32)
    silu_cond = jax.nn.silu(cond_single).astype(jnp.bfloat16)
    modulation = jnp.dot(
        silu_cond, mod_matrix, preferred_element_type=jnp.float32
    ) + mod_offset.astype(jnp.float32)
    shift1, scale1, gate1, shift2, scale2, gate2 = jnp.split(modulation[:, None, :], 6, axis=-1)
    tokens = inputs.astype(jnp.float32)
    normed, factor = norm_forward(tokens)
    moved = (normed * (1.0 + scale1) + shift1).astype(jnp.bfloat16).reshape(-1, width)
    qv_single = qv_offset.astype(jnp.float32)
    offsets = jnp.concatenate(
        [qv_single[:width], jnp.zeros((width,), jnp.float32), qv_single[width:]]
    )
    qkv = (jnp.dot(moved, qkv_matrix, preferred_element_type=jnp.float32) + offsets).astype(
        jnp.bfloat16
    )
    qkv = qkv.reshape(samples, slot_dev, 3 * width)
    query = qkv[:, :, :width]
    key = qkv[:, :, width : 2 * width]
    value = qkv[:, :, 2 * width :]
    whole_key, whole_value = (
        lax.all_gather(key, "seq", axis=1, tiled=True),
        lax.all_gather(value, "seq", axis=1, tiled=True),
    )
    attended, logsum = lax.map(
        attend, (paired(query), paired(whole_key), paired(whole_value), paired(key_valid))
    )
    attended = unpaired(attended).reshape(-1, width)
    projected = (
        jnp.dot(attended, out_matrix, preferred_element_type=jnp.float32)
        + out_offset.astype(jnp.float32)
    ).reshape(samples, slot_dev, width)
    middle = tokens + gate1 * projected
    normed2, factor2 = norm_forward(middle)
    moved2 = (normed2 * (1.0 + scale2) + shift2).astype(jnp.bfloat16).reshape(-1, width)
    upper = jnp.dot(moved2, up_matrix, preferred_element_type=jnp.float32) + up_offset.astype(
        jnp.float32
    )
    gelu_value, gelu_pull = jax.vjp(lambda u: jax.nn.gelu(u, approximate=True), upper)
    act = gelu_value.astype(jnp.bfloat16)
    lowered = (
        jnp.dot(act, down_matrix, preferred_element_type=jnp.float32)
        + down_offset.astype(jnp.float32)
    ).reshape(samples, slot_dev, width)
    output = (middle + gate2 * lowered).astype(jnp.bfloat16)
    upstream = cotangent.astype(jnp.float32)
    d_gate2 = jnp.sum(upstream * lowered, axis=1)
    d_lowered = (gate2 * upstream).astype(jnp.bfloat16).reshape(-1, width)
    down_grad = jnp.einsum("rf,rd->fd", act, d_lowered, preferred_element_type=jnp.float32)
    down_offset_grad = jnp.sum(d_lowered.astype(jnp.float32), axis=0)
    d_act = jnp.einsum("rd,fd->rf", d_lowered, down_matrix, preferred_element_type=jnp.float32)
    d_upper = gelu_pull(d_act)[0].astype(jnp.bfloat16)
    up_grad = jnp.einsum("rd,rf->df", moved2, d_upper, preferred_element_type=jnp.float32)
    up_offset_grad = jnp.sum(d_upper.astype(jnp.float32), axis=0)
    d_moved2 = jnp.einsum(
        "rf,df->rd", d_upper, up_matrix, preferred_element_type=jnp.float32
    ).reshape(samples, slot_dev, width)
    d_shift2 = jnp.sum(d_moved2, axis=1)
    d_scale2 = jnp.sum(d_moved2 * normed2, axis=1)
    d_middle = upstream + norm_back(d_moved2 * (1.0 + scale2), normed2, factor2)
    d_gate1 = jnp.sum(d_middle * projected, axis=1)
    d_projected = (gate1 * d_middle).astype(jnp.bfloat16).reshape(-1, width)
    out_grad = jnp.einsum("rc,rd->cd", attended, d_projected, preferred_element_type=jnp.float32)
    out_offset_grad = jnp.sum(d_projected.astype(jnp.float32), axis=0)
    d_attended = jnp.einsum(
        "rd,cd->rc", d_projected, out_matrix, preferred_element_type=jnp.float32
    ).astype(jnp.bfloat16)
    d_attended = d_attended.reshape(samples, slot_dev, width)
    d_query, d_key_whole, d_value_whole = lax.map(
        attend_back,
        (
            paired(query),
            paired(whole_key),
            paired(whole_value),
            paired(key_valid),
            logsum,
            paired(d_attended),
        ),
    )
    d_key, d_value = (
        lax.psum_scatter(unpaired(d_key_whole), "seq", scatter_dimension=1, tiled=True),
        lax.psum_scatter(unpaired(d_value_whole), "seq", scatter_dimension=1, tiled=True),
    )
    d_qkv = (
        jnp.concatenate([unpaired(d_query), d_key, d_value], axis=-1)
        .astype(jnp.bfloat16)
        .reshape(-1, 3 * width)
    )
    qkv_grad = jnp.einsum("rd,re->de", moved, d_qkv, preferred_element_type=jnp.float32)
    column_sums = jnp.sum(d_qkv.astype(jnp.float32), axis=0)
    qv_offset_grad = jnp.concatenate([column_sums[:width], column_sums[2 * width :]])
    d_moved = jnp.einsum(
        "re,de->rd", d_qkv, qkv_matrix, preferred_element_type=jnp.float32
    ).reshape(samples, slot_dev, width)
    d_shift1 = jnp.sum(d_moved, axis=1)
    d_scale1 = jnp.sum(d_moved * normed, axis=1)
    input_grad = d_middle + norm_back(d_moved * (1.0 + scale1), normed, factor)
    partial_mod = jnp.concatenate(
        [d_shift1, d_scale1, d_gate1, d_shift2, d_scale2, d_gate2], axis=-1
    )
    d_modulation = lax.psum(partial_mod, "seq").astype(jnp.bfloat16)
    leading = (lax.axis_index("seq") == 0).astype(jnp.float32)
    mod_grad = (
        jnp.einsum("sd,se->de", silu_cond, d_modulation, preferred_element_type=jnp.float32)
        * leading
    )
    mod_offset_grad = jnp.sum(d_modulation.astype(jnp.float32), axis=0) * leading
    d_silu = jnp.einsum("se,de->sd", d_modulation, mod_matrix, preferred_element_type=jnp.float32)
    cond_grad = jax.vjp(jax.nn.silu, cond_single)[1](d_silu)[0]
    shards = (
        lax.psum_scatter(qkv_grad, "batch", scatter_dimension=0, tiled=True),
        lax.psum_scatter(qv_offset_grad, "batch", scatter_dimension=0, tiled=True),
        lax.psum_scatter(out_grad, "batch", scatter_dimension=0, tiled=True),
        lax.psum_scatter(out_offset_grad, "batch", scatter_dimension=0, tiled=True),
        lax.psum_scatter(up_grad, "batch", scatter_dimension=0, tiled=True),
        lax.psum_scatter(up_offset_grad, "batch", scatter_dimension=0, tiled=True),
        lax.psum_scatter(down_grad, "batch", scatter_dimension=0, tiled=True),
        lax.psum_scatter(down_offset_grad, "batch", scatter_dimension=0, tiled=True),
        lax.psum_scatter(mod_grad, "batch", scatter_dimension=0, tiled=True),
        lax.psum_scatter(mod_offset_grad, "batch", scatter_dimension=0, tiled=True),
    )
    summed = lax.psum(tuple(shards), "seq")
    return (
        output,
        input_grad,
        cond_grad,
        summed[0],
        summed[1],
        summed[2],
        summed[3],
        summed[4],
        summed[5],
        summed[6],
        summed[7],
        summed[8],
        summed[9],
    )


def solution(mesh):
    in_specs = (
        P("batch", "seq", None),
        P("batch", None),
        P("batch"),
        P("batch"),
        P("batch", None),
        P("batch"),
        P("batch", None),
        P("batch"),
        P("batch", None),
        P("batch"),
        P("batch", None),
        P("batch"),
        P("batch", None),
        P("batch"),
        P("batch", "seq", None),
    )
    out_specs = (
        P("batch", "seq", None),
        P("batch", "seq", None),
        P("batch", None),
        P("batch", None),
        P("batch"),
        P("batch", None),
        P("batch"),
        P("batch", None),
        P("batch"),
        P("batch", None),
        P("batch"),
        P("batch", None),
        P("batch"),
    )
    return jax.shard_map(body, mesh=mesh, in_specs=in_specs, out_specs=out_specs, check_vma=False)
```

profile of v0, /device:TPU:0, one launch (start us, length us, event | category | flops | bytes accessed | tf_op | source)
XLA Modules:
  0.0 2011.4 jit_solution(10382252398066105498)
XLA Ops:
  13.3 26.9 %all-reduce.13 = (bf16[6912]{0:T(1024)(128)(2,1)S(1)}, bf16[2304]{0:T(1024)(128)(2,1)S(1)}, bf16[1152]{0:T(1024)(128)(2,1)S(1)}, bf16[1152]{0:T(1024)(128)(2,1)S(1)}, bf16[4608]{0:T(1024)(128)(2,1)}) all-reduce(bf16[6912]{0:T(1024)(128)(2,1)S(1)} %dynamic-update-slice, ...), channel_id=1, replica_groups=mesh['batch'=8,'seq'=4] {'batch'}, use_global_device_ids=true, to_apply=%add | all-reduce | flops 16128 | bytes 64512
  41.0 58.4 %all-gather.8.cloned.1.call-done = bf16[1152,6912]{1,0:T(8,128)(2,1)} async-done(((bf16[144,6912]{1,0:T(8,128)(2,1)}), bf16[1152,6912]{1,0:T(8,128)(2,1)}) %all-gather.8.cloned.1.call-update) | async-done | bytes 15925264 | tf_op jit(solution)/shard_map/all_gather | solution.py:111
  99.4 7.7 fusion.15
  108.3 45.6 %all-gather.10.cloned.1.call-done = bf16[1152,3456]{1,0:T(8,128)(2,1)} async-done(((bf16[144,3456]{1,0:T(8,128)(2,1)}), bf16[1152,3456]{1,0:T(8,128)(2,1)}) %all-gather.10.cloned.1.call-update) | async-done | bytes 7962640 | tf_op jit(solution)/shard_map/all_gather | solution.py:103
  153.9 8.3 add_convert_fusion
  162.3 1.8 fusion.58
  168.7 84.9 %all-gather.14.cloned.1.call-done = bf16[2,1024,1152]{2,1,0:T(8,128)(2,1)} async-done(((bf16[2,256,1152]{2,1,0:T(8,128)(2,1)}), bf16[2,1024,1152]{2,1,0:T(8,128)(2,1)}) %all-gather.14.cloned.1.call-update) | async-done | bytes 4718608 | tf_op jit(solution)/shard_map/all_gather | solution.py:152
  253.7 6.6 copy.67
  260.3 83.3 %all-gather.12.cloned.1.call-done = bf16[2,1024,1152]{2,1,0:T(8,128)(2,1)} async-done(((bf16[2,256,1152]{2,1,0:T(8,128)(2,1)}), bf16[2,1024,1152]{2,1,0:T(8,128)(2,1)}) %all-gather.12.cloned.1.call-update) | async-done | bytes 4718608 | tf_op jit(solution)/shard_map/all_gather | solution.py:153
  343.6 6.6 copy.65
  350.2 16.9 fusion.62
  367.1 14.4 fusion
  381.6 16.6 fusion.34
  398.2 1.2 copy.68
  399.8 3.6 convolution_add_fusion.2
  406.1 2.6 convert_reduce_fusion.3
  408.7 30.9 %all-gather.18.cloned.1.call-done = bf16[1152,4608]{1,0:T(8,128)(2,1)} async-done(((bf16[144,4608]{1,0:T(8,128)(2,1)}), bf16[1152,4608]{1,0:T(8,128)(2,1)}) %all-gather.18.cloned.1.call-update) | async-done | bytes 10616848 | tf_op jit(solution)/shard_map/all_gather | solution.py:107
  439.6 11.5 fusion.63
  451.1 54.2 %all-gather.20.cloned.1.call-done = bf16[4608,1152]{1,0:T(8,128)(2,1)} async-done(((bf16[576,1152]{1,0:T(8,128)(2,1)}), bf16[4608,1152]{1,0:T(8,128)(2,1)}) %all-gather.20.cloned.1.call-update) | async-done | bytes 10616848 | tf_op jit(solution)/shard_map/all_gather | solution.py:109
  505.3 16.7 convert_reduce_fusion
  522.0 12.3 fusion.32
  534.9 1.3 div.52
  536.2 3.8 fusion.33
  540.1 13.0 convolution_add_fusion.1
  553.2 3.6 convert_reduce_fusion.4
  557.8 1.9 convolution_convert_fusion
  559.7 3.7 reshape.252
  563.4 1.6 copy.70
  565.0 17.3 fusion.2
  582.3 9.7 copy.73
  592.0 24.4 %multiply_reduce_fusion = (f32[2,16,256]{2,1,0:T(8,128)S(1)}, f32[2,16,256,1024]{3,2,1,0:T(8,128)}) fusion(f32[2,16,256,1024]{3,2,1,0:T(8,128)} %get-tuple-element.120, f32[2,16,256]{2,1,0:T(8,128)S(1)} %copy-done.21, bf16[2,256,16,72]{1,3,2,0:T(8,128)(2,1)S(1)} %copy.70, bf16[2,1024,16,72]{1,3,2,0:T(8,128)(2,1)} %bitcast.114), kind=kOutput, calls=%fused_computation.1 | convolution fusion | flops 1233117184 | bytes 73072640 | tf_op jit(solution)/shard_map/while/body/eval_jaxpr/bqhd,bkhd->bhqk/dot_general | solution.py:67
  616.4 28.1 %multiply_convert_fusion = bf16[2,16,256,1024]{3,2,1,0:T(8,128)(2,1)} fusion(f32[2,16,256,1024]{3,2,1,0:T(8,128)} %get-tuple-element.124, f32[2,16,256,1024]{3,2,1,0:T(8,128)} %get-tuple-element.120, f32[2,16,256]{2,1,0:T(8,128)S(1)} %get-tuple-element.123, f32[2,16,256]{2,1,0:T(8,128)S(1)} %copy-done.21), kind=kLoop, calls=%fused_computation | loop fusion | flops 33554432 | bytes 83951616 | tf_op jit(solution)/shard_map/while/body/eval_jaxpr/convert_element_type | solution.py:71
  644.6 12.4 broadcast_multiply_fusion
  657.0 9.7 copy.71
  668.3 4.0 convolution_bitcast_fusion.1
  673.6 14.5 fusion.54
  689.4 12.3 fusion.64
  701.8 10.1 multiply_convert_fusion.2
  712.6 40.8 %reduce-scatter.10.cloned.1.call-done = f32[2,256,1152]{2,1,0:T(8,128)} async-done(((f32[2,1024,1152]{2,1,0:T(8,128)}), f32[2,256,1152]{2,1,0:T(8,128)}) %reduce-scatter.10.cloned.1.call-update) | async-done | bytes 2359312 | tf_op jit(solution)/shard_map/reduce_scatter | solution.py:212
  753.4 1.8 convert.18
  755.2 162.7 %reduce-scatter.8.cloned.1.call-done = f32[2,256,1152]{2,1,0:T(8,128)} async-done(((f32[2,1024,1152]{2,1,0:T(8,128)}), f32[2,256,1152]{2,1,0:T(8,128)}) %reduce-scatter.8.cloned.1.call-update) | async-done | bytes 2359312 | tf_op jit(solution)/shard_map/reduce_scatter | solution.py:211
  917.9 1.9 convert.17
  920.9 8.2 convolution_bitcast_fusion
  930.5 10.5 fusion.28
  942.3 2.5 multiply_reduce_fusion.1
  947.2 19.8 psum.77
  967.0 13.5 convolution_multiply_fusion
  980.7 139.5 %reduce-scatter.18.cloned.1.call-done = f32[576,1152]{1,0:T(8,128)} async-done(((f32[4608,1152]{1,0:T(8,128)}), f32[576,1152]{1,0:T(8,128)}) %reduce-scatter.18.cloned.1.call-update) | async-done | bytes 2654224 | tf_op jit(solution)/shard_map/reduce_scatter | solution.py:247
  1120.2 141.1 %reduce-scatter.16.cloned.1.call-done = f32[144,4608]{1,0:T(8,128)} async-done(((f32[1152,4608]{1,0:T(8,128)}), f32[144,4608]{1,0:T(8,128)}) %reduce-scatter.16.cloned.1.call-update) | async-done | bytes 2654224 | tf_op jit(solution)/shard_map/reduce_scatter | solution.py:245
  1261.3 116.9 %reduce-scatter.12.cloned.1.call-done = f32[144,3456]{1,0:T(8,128)} async-done(((f32[1152,3456]{1,0:T(8,128)}), f32[144,3456]{1,0:T(8,128)}) %reduce-scatter.12.cloned.1.call-update) | async-done | bytes 1990672 | tf_op jit(solution)/shard_map/reduce_scatter | solution.py:241
  1378.2 202.0 %reduce-scatter.20.cloned.1.call-done = f32[144,6912]{1,0:T(8,128)} async-done(((f32[1152,6912]{1,0:T(8,128)}), f32[144,6912]{1,0:T(8,128)}) %reduce-scatter.20.cloned.1.call-update) | async-done | bytes 3981328 | tf_op jit(solution)/shard_map/reduce_scatter | solution.py:249
  1582.7 1.2 copy.76
  1584.3 1.4 copy.78
  1585.7 1.4 copy.77
  1587.1 2.2 convert_reduce_fusion.1
  1589.5 25.6 %all-reduce.10 = (f32[2304]{0:T(1024)S(1)}, f32[1152]{0:T(1024)S(1)}, f32[4608]{0:T(1024)S(1)}, f32[1152]{0:T(1024)S(1)}, f32[6912]{0:T(1024)S(1)}) all-reduce(f32[2304]{0:T(1024)S(1)} %pad_maximum_fusion.4, f32[1152]{0:T(1024)S(1)} %copy-done.48, f32[4608]{0:T(1024)S(1)} %copy-done.55, ...), channel_id=5, replica_groups=mesh['batch'=8,'seq'=4] {'batch'}, use_global_device_ids=true, to_apply=%region_23.24.clone | all-reduce | flops 16128 | bytes 129024
  1615.5 21.5 %all-reduce.11 = (f32[288]{0:T(512)}, f32[144]{0:T(256)}, f32[576]{0:T(1024)}, f32[144]{0:T(256)}, f32[864]{0:T(1024)}) all-reduce(f32[288]{0:T(512)S(1)} %dynamic-slice.11, f32[144]{0:T(256)S(1)} %dynamic-slice.13, f32[576]{0:T(1024)S(1)} %dynamic-slice.15, f32[144]{0:T(256)S(1)} %dynamic-slice.17, ...), channel_id=1, replica_groups=mesh['batch'=8,'seq'=4] {'seq'}, use_global_device_ids=true, to_apply=%region_24.25 | all-reduce | flops 2016 | bytes 16128 | tf_op jit(solution)/shard_map/psum | solution.py:252
  1637.1 10.5 fusion.40
  1647.6 345.2 %all-reduce.16.cloned.1.call-done = (f32[144,3456]{1,0:T(8,128)}, f32[144,1152]{1,0:T(8,128)}, f32[144,4608]{1,0:T(8,128)}, f32[576,1152]{1,0:T(8,128)}, f32[144,6912]{1,0:T(8,128)}) async-done(((f32[144,3456]{1,0:T(8,128)}, f32[144,1152]{1,0:T(8,128)}, f32[144,4608]{1,0:T(8,128)}, f32[576,1152]{1,0:T(8,128)}, f32[144,6912]{1,0:T(8,128)}), (f32[144,3456]{1,0:T(8,128)}, f32[144,1152]{1,0:T(8,128)}, ...) | async-done | bytes 11943952 | tf_op jit(solution)/shard_map/psum | solution.py:252
  1992.7 3.1 copy.99
  1996.7 1.5 copy.101
  1999.4 1.5 copy.102
  2000.9 1.6 copy-done.17
  2002.5 1.9 copy.103
  (224 shorter events, 28.3 us)
Async XLA Ops:
  7.2 4.8 copy-start.65
  7.2 5.1 copy-start.66
  7.2 5.3 copy-start.64
  7.2 5.6 copy-start.62
  7.2 5.8 copy-start.63
  7.2 33.0 %copy-start = (bf16[2,256,1152]{2,1,0:T(8,128)(2,1)S(1)}, bf16[2,256,1152]{2,1,0:T(8,128)(2,1)}, u32[]{:S(2)}) copy-start(bf16[2,256,1152]{2,1,0:T(8,128)(2,1)} %param.15) | copy-start | bytes 3538948
  7.3 92.1 %copy-start.41 = (bf16[2,1152]{1,0:T(2,128)(2,1)S(1)}, bf16[2,1152]{1,0:T(2,128)(2,1)}, u32[]{:S(2)}) copy-start(bf16[2,1152]{1,0:T(2,128)(2,1)} %param.16) | copy-start | bytes 13828
  7.3 92.1 %all-gather.8.cloned.1.call-start = ((), (), s32[]{:S(2)}) async-start(), calls=%async_computation.7 | async-start | bytes 17915904 | tf_op jit(solution)/shard_map/all_gather | solution.py:111
  8.0 145.9 %all-gather.10.cloned.1.call-start = ((), (), s32[]{:S(2)}) async-start(), calls=%async_computation.8 | async-start | bytes 8957952 | tf_op jit(solution)/shard_map/all_gather | solution.py:103
  8.8 244.9 %all-gather.14.cloned.1.call-start = ((), (), s32[]{:S(2)}) async-start(), calls=%async_computation.10 | async-start | bytes 5898240 | tf_op jit(solution)/shard_map/all_gather | solution.py:152
  40.5 67.2 %copy-start.49 = (f32[2,256]{1,0:T(2,128)}, f32[2,256]{1,0:T(2,128)S(1)}, u32[]{:S(2)}) copy-start(f32[2,256]{1,0:T(2,128)S(1)} %broadcast_multiply_fusion.7) | copy-start | bytes 6148
  40.9 66.8 %copy-start.56 = (f32[2,256]{1,0:T(2,128)}, f32[2,256]{1,0:T(2,128)S(1)}, u32[]{:S(2)}) copy-start(f32[2,256]{1,0:T(2,128)S(1)} %add_rsqrt_fusion.1) | copy-start | bytes 6148
  107.7 54.5 %copy-start.35 = (f32[2,1152]{1,0:T(2,128)}, f32[2,1152]{1,0:T(2,128)S(1)}, u32[]{:S(2)}) copy-start(f32[2,1152]{1,0:T(2,128)S(1)} %get-tuple-element.111) | copy-start | bytes 27652
  108.2 54.0 %copy-start.11 = (bf16[2,256,1152]{2,1,0:T(8,128)(2,1)}, bf16[2,256,1152]{2,1,0:T(8,128)(2,1)S(1)}, u32[]{:S(2)}) copy-start(bf16[2,256,1152]{2,1,0:T(8,128)(2,1)S(1)} %fusion.23) | copy-start | bytes 3538948
  164.1 3.3 copy-start.58
  164.1 4.0 copy-start.67
  164.1 4.0 copy-start.68
  164.1 179.5 %all-gather.12.cloned.1.call-start = ((), (), s32[]{:S(2)}) async-start(), calls=%async_computation.9 | async-start | bytes 5898240 | tf_op jit(solution)/shard_map/all_gather | solution.py:153
  164.7 235.1 %all-gather.16.cloned.1.call-start = ((), (), s32[]{:S(2)}) async-start(), calls=%async_computation.11 | async-start | bytes 2985984 | tf_op jit(solution)/shard_map/all_gather | solution.py:105
  165.3 274.4 %all-gather.18.cloned.1.call-start = ((), (), s32[]{:S(2)}) async-start(), calls=%async_computation.12 | async-start | bytes 11943936 | tf_op jit(solution)/shard_map/all_gather | solution.py:107
  165.8 339.5 %all-gather.20.cloned.1.call-start = ((), (), s32[]{:S(2)}) async-start(), calls=%async_computation.13 | async-start | bytes 11943936 | tf_op jit(solution)/shard_map/all_gather | solution.py:109
  166.6 586.8 %reduce-scatter.10.cloned.1.call-start = ((), (), s32[]{:S(2)}) async-start(), calls=%async_computation.15 | async-start | bytes 11796480 | tf_op jit(solution)/shard_map/reduce_scatter | solution.py:212
  168.7 181.5 %copy-start.5 = (bf16[2,256,1152]{1,2,0:T(8,128)(2,1)}, bf16[2,256,1152]{1,2,0:T(8,128)(2,1)S(1)}, u32[]{:S(2)}) copy-start(bf16[2,256,1152]{1,2,0:T(8,128)(2,1)S(1)} %copy.66) | copy-start | bytes 3538948
  367.1 14.4 copy-start.30
  381.6 16.6 copy-start.33
  399.7 3.7 copy-start.37
  403.4 2.4 copy-start.32
  403.5 2.4 copy-start.39
  403.5 2.4 copy-start.46
  522.0 12.3 copy-start.13
  536.2 3.9 copy-start.53
  536.2 3.9 copy-start.60
  540.1 13.1 copy-start.4
  540.1 13.1 copy-start.38
  540.1 13.1 copy-start.40
  540.1 13.1 copy-start.52
  540.1 13.1 copy-start.59
  553.2 4.6 copy-start.20
  559.7 5.3 copy-start.21
  592.0 326.0 %reduce-scatter.8.cloned.1.call-start = ((), (), s32[]{:S(2)}) async-start(), calls=%async_computation.14 | async-start | bytes 11796480 | tf_op jit(solution)/shard_map/reduce_scatter | solution.py:211
  616.4 28.1 %copy-start.6 = (bf16[2,256,1152]{1,2,0:T(8,128)(2,1)S(1)}, bf16[2,256,1152]{1,2,0:T(8,128)(2,1)}, u32[]{:S(2)}) copy-start(bf16[2,256,1152]{1,2,0:T(8,128)(2,1)} %copy-done.5) | copy-start | bytes 3538948
  666.7 313.9 %reduce-scatter.14.cloned.1.call-start = ((), (), s32[]{:S(2)}) async-start(), calls=%async_computation.17 | async-start | bytes 5971968 | tf_op jit(solution)/shard_map/reduce_scatter | solution.py:243
  672.4 447.8 %reduce-scatter.18.cloned.1.call-start = ((), (), s32[]{:S(2)}) async-start(), calls=%async_computation.19 | async-start | bytes 23887872 | tf_op jit(solution)/shard_map/reduce_scatter | solution.py:247
  688.2 573.1 %reduce-scatter.16.cloned.1.call-start = ((), (), s32[]{:S(2)}) async-start(), calls=%async_computation.18 | async-start | bytes 23887872 | tf_op jit(solution)/shard_map/reduce_scatter | solution.py:245
  701.7 676.4 %reduce-scatter.12.cloned.1.call-start = ((), (), s32[]{:S(2)}) async-start(), calls=%async_computation.16 | async-start | bytes 17915904 | tf_op jit(solution)/shard_map/reduce_scatter | solution.py:241
  712.6 207.2 %copy-start.10 = (bf16[2,256,1152]{2,1,0:T(8,128)(2,1)}, bf16[2,256,1152]{2,1,0:T(8,128)(2,1)S(1)}, u32[]{:S(2)}) copy-start(bf16[2,256,1152]{2,1,0:T(8,128)(2,1)S(1)} %copy.74) | copy-start | bytes 3538948
  917.9 2.9 copy-start.12
  929.1 651.1 %reduce-scatter.20.cloned.1.call-start = ((), (), s32[]{:S(2)}) async-start(), calls=%async_computation.20 | async-start | bytes 35831808 | tf_op jit(solution)/shard_map/reduce_scatter | solution.py:249
  930.5 11.8 copy-start.3
  930.5 11.8 copy-start.9
  930.5 11.7 copy-start.57
  942.2 3.1 copy-start.44
  942.2 3.7 copy-start.43
  942.3 4.3 copy-start.45
  967.0 13.5 copy-start.28
  980.6 1012.1 %all-reduce.16.cloned.1.call-start = ((), (), s32[]{:S(2)}) async-start(), calls=%async_computation.21 | async-start | bytes 23887872 | tf_op jit(solution)/shard_map/psum | solution.py:252
  1585.7 3.8 copy-start.47
  1585.7 51.4 %copy-start.42 = (bf16[2,1152]{1,0:T(2,128)(2,1)S(1)}, bf16[2,1152]{1,0:T(2,128)(2,1)}, u32[]{:S(2)}) copy-start(bf16[2,1152]{1,0:T(2,128)(2,1)} %param.16) | copy-start | bytes 13828
  1587.1 2.4 copy-start.48
  1587.1 2.4 copy-start.55
  1992.7 3.1 copy-start.27
  1992.7 4.0 copy-start.19
  1996.7 2.7 copy-start.18
  1999.4 3.1 copy-start.17
  (20 other events, 28.2 us)
Sparse Core Ops, SparseCore 0:
  10.0 89.3 all-gather.7
  101.3 52.5 all-gather.9
  164.2 89.4 all-gather.13
  255.7 87.8 all-gather.11
  345.3 28.6 all-gather.15
  375.8 63.8 all-gather.17
  441.5 63.8 all-gather.19
  592.1 161.2 reduce-scatter.9
  755.8 162.1 reduce-scatter.7
  921.2 57.7 reduce-scatter.13
  983.1 137.0 reduce-scatter.17
  1124.1 137.1 reduce-scatter.15
  1265.3 112.7 reduce-scatter.11
  1381.7 198.4 reduce-scatter.19
  1583.5 409.2 all-reduce.15
where the time goes:
time: 2020 us; the launch traced here: 2010 us
  waiting for transfers between devices  1510 us (75%)
  matrix products  246 us (12%)
  blocking collectives  93.9 us (5%)
  local copies, waits for them, and re-layouts  74.1 us (4%)
  other arithmetic  66.3 us (3%)
  between operations  20.4 us (1%)
    psum x1, waiting for transfers between devices, body(): summed = lax.psum(tuple(shards), 'seq')  345 us
    reduce_scatter x1, waiting for transfers between devices, body(): lax.psum_scatter(mod_grad, 'batch', scatter_dimension=0, tiled=True)  202 us
    reduce_scatter x1, waiting for transfers between devices, body(): lax.psum_scatter(unpaired(d_key_whole), 'seq', scatter_dimension=1, tiled...  163 us
    reduce_scatter x1, waiting for transfers between devices, body(): lax.psum_scatter(up_grad, 'batch', scatter_dimension=0, tiled=True)  141 us
    reduce_scatter x1, waiting for transfers between devices, body(): lax.psum_scatter(down_grad, 'batch', scatter_dimension=0, tiled=True)  140 us
    reduce_scatter x1, waiting for transfers between devices, body(): lax.psum_scatter(qkv_grad, 'batch', scatter_dimension=0, tiled=True)  117 us
    all_gather x1, waiting for transfers between devices, body(): lax.all_gather(key, 'seq', axis=1, tiled=True)  84.9 us
    all_gather x1, waiting for transfers between devices, body(): lax.all_gather(value, 'seq', axis=1, tiled=True)  83.3 us
  transfers between devices with their start and end apart: 15, of which 13 were waited for; matrix products, arithmetic and copies ran while one was open for 13% of the time, Pallas kernels for 0%

commit v1 on v0

v1 whole, which is shorter than its diff:
```python
import functools

import jax
import jax.numpy as jnp
from jax import lax
from jax.experimental import pallas as pl
from jax.experimental.pallas import tpu as pltpu
from jax.sharding import PartitionSpec as P

HEADS = 16
HEAD = 72
SCALE = HEAD ** (-0.5)
f32 = jnp.float32
bf16 = jnp.bfloat16
NT = (((1,), (1,)), ((), ()))
TN = (((0,), (0,)), ((), ()))


def dot(a, b, dims=(((1,), (0,)), ((), ()))):
    return lax.dot_general(a, b, dims, preferred_element_type=f32)


def attend_kernel(heads, limits, mine, theirs, out_mine, out_theirs, lse, qs, ks, vs, os, ls):
    half = mine.shape[0]
    total = 2 * half
    chunks = limits.shape[0]
    chunk = total // chunks
    wide = heads * HEAD
    lane = lax.broadcasted_iota(jnp.int32, (1, chunk), 1)
    valid = jnp.concatenate([lane < limits[i] for i in range(chunks)], axis=1)
    block = 256
    for h in range(heads):
        lo = h * HEAD
        for part, ref in ((0, mine), (1, theirs)):
            rows = slice(part * half, (part + 1) * half)
            qs[rows, :] = ref[:, lo : lo + HEAD]
            ks[rows, :] = ref[:, wide + lo : wide + lo + HEAD]
            vs[rows, :] = ref[:, 2 * wide + lo : 2 * wide + lo + HEAD]

        def step(i, carry):
            at = pl.ds(pl.multiple_of(i * block, block), block)
            scores = dot(qs[at, :], ks[...], NT) * SCALE
            scores = jnp.where(valid, scores, -1000000000.0)
            peak = jnp.max(scores, axis=1, keepdims=True)
            expo = jnp.exp(scores - peak)
            summed = jnp.sum(expo, axis=1, keepdims=True)
            probs = (expo * (1.0 / summed)).astype(bf16)
            os[at, :] = dot(probs, vs[...]).astype(bf16)
            ls[at, :] = peak + jnp.log(summed)
            return carry

        lax.fori_loop(0, total // block, step, 0)
        out_mine[:, lo : lo + HEAD] = os[:half, :]
        out_theirs[:, lo : lo + HEAD] = os[half:, :]
        lse[h : h + 1, :] = jnp.transpose(ls[...])


def attend(limits, mine, theirs):
    half, wide3 = mine.shape
    wide = wide3 // 3
    heads = wide // HEAD
    total = 2 * half
    return pl.pallas_call(
        functools.partial(attend_kernel, heads),
        out_shape=(
            jax.ShapeDtypeStruct((half, wide), bf16),
            jax.ShapeDtypeStruct((half, wide), bf16),
            jax.ShapeDtypeStruct((heads, total), f32),
        ),
        in_specs=[
            pl.BlockSpec(memory_space=pltpu.SMEM),
            pl.BlockSpec(memory_space=pltpu.VMEM),
            pl.BlockSpec(memory_space=pltpu.VMEM),
        ],
        out_specs=(pl.BlockSpec(memory_space=pltpu.VMEM),) * 3,
        scratch_shapes=[
            pltpu.VMEM((total, HEAD), bf16),
            pltpu.VMEM((total, HEAD), bf16),
            pltpu.VMEM((total, HEAD), bf16),
            pltpu.VMEM((total, HEAD), bf16),
            pltpu.VMEM((total, 1), f32),
        ],
        compiler_params=pltpu.CompilerParams(vmem_limit_bytes=40 * 2**20),
        cost_estimate=pl.CostEstimate(
            flops=4 * heads * total * total * 128,
            bytes_accessed=8 * total * wide,
            transcendentals=heads * total * total,
        ),
    )(limits, mine, theirs)


def back_kernel(heads, limits, mine, theirs, d_mine, d_theirs, lse, out_mine, out_theirs, qs, ks, vs, ds, dq, dk, dv):
    half = mine.shape[0]
    total = 2 * half
    chunks = limits.shape[0]
    chunk = total // chunks
    wide = heads * HEAD
    sub = lax.broadcasted_iota(jnp.int32, (chunk, 1), 0)
    valid = jnp.concatenate([sub < limits[i] for i in range(chunks)], axis=0)
    block = 256
    for h in range(heads):
        lo = h * HEAD
        for part, ref, d_ref in ((0, mine, d_mine), (1, theirs, d_theirs)):
            rows = slice(part * half, (part + 1) * half)
            qs[rows, :] = ref[:, lo : lo + HEAD]
            ks[rows, :] = ref[:, wide + lo : wide + lo + HEAD]
            vs[rows, :] = ref[:, 2 * wide + lo : 2 * wide + lo + HEAD]
            ds[rows, :] = d_ref[:, lo : lo + HEAD]
        dk[...] = jnp.zeros_like(dk)
        dv[...] = jnp.zeros_like(dv)

        def step(i, carry):
            at = pl.ds(pl.multiple_of(i * block, block), block)
            query = qs[at, :]
            d_out = ds[at, :]
            scores = dot(ks[...], query, NT) * SCALE - lse[h : h + 1, at]
            exact = jnp.where(valid, jnp.exp(jnp.where(valid, scores, -1000000000.0)), 0.0)
            d_probs = dot(vs[...], d_out, NT)
            dv[...] += dot(exact.astype(bf16), d_out)
            product = exact * d_probs
            centred = jnp.sum(product, axis=0, keepdims=True)
            d_scores = (product - exact * centred).astype(bf16)
            dk[...] += dot(d_scores, query)
            dq[at, :] = (dot(d_scores, ks[...], TN) * SCALE).astype(bf16)
            return carry

        lax.fori_loop(0, total // block, step, 0)
        for part, ref in ((0, out_mine), (1, out_theirs)):
            rows = slice(part * half, (part + 1) * half)
            ref[:, lo : lo + HEAD] = dq[rows, :]
            ref[:, wide + lo : wide + lo + HEAD] = (dk[rows, :] * SCALE).astype(bf16)
            ref[:, 2 * wide + lo : 2 * wide + lo + HEAD] = dv[rows, :].astype(bf16)


def attend_back(limits, mine, theirs, d_mine, d_theirs, lse):
    half, wide3 = mine.shape
    wide = wide3 // 3
    heads = wide // HEAD
    total = 2 * half
    return pl.pallas_call(
        functools.partial(back_kernel, heads),
        out_shape=(
            jax.ShapeDtypeStruct((half, wide3), bf16),
            jax.ShapeDtypeStruct((half, wide3), bf16),
        ),
        in_specs=[pl.BlockSpec(memory_space=pltpu.SMEM)] + [pl.BlockSpec(memory_space=pltpu.VMEM)] * 5,
        out_specs=(pl.BlockSpec(memory_space=pltpu.VMEM),) * 2,
        scratch_shapes=[
            pltpu.VMEM((total, HEAD), bf16),
            pltpu.VMEM((total, HEAD), bf16),
            pltpu.VMEM((total, HEAD), bf16),
            pltpu.VMEM((total, HEAD), bf16),
            pltpu.VMEM((total, HEAD), bf16),
            pltpu.VMEM((total, HEAD), f32),
            pltpu.VMEM((total, HEAD), f32),
        ],
        compiler_params=pltpu.CompilerParams(vmem_limit_bytes=40 * 2**20),
        cost_estimate=pl.CostEstimate(
            flops=10 * heads * total * total * 128,
            bytes_accessed=16 * total * wide,
            transcendentals=heads * total * total,
        ),
    )(limits, mine, theirs, d_mine, d_theirs, lse)


def pair_swap(array):
    size = lax.axis_size("batch")
    return lax.ppermute(array, "batch", [(i, i ^ 1) for i in range(size)])


def deal_pairs(turn, back=False):
    pairs = []
    seq = lax.axis_size("seq")
    for b in range(lax.axis_size("batch")):
        for s in range(seq):
            j = (s ^ turn) & 1
            dc = ((s >> 1) ^ (turn >> 1)) & 1
            here, there = b * seq + s, (b ^ dc) * seq + 2 * (b & 1) + j
            pairs.append((there, here) if back else (here, there))
    return pairs


def place_of(turn):
    b, s = lax.axis_index("batch"), lax.axis_index("seq")
    j = (s ^ turn) & 1
    half = (b ^ (s >> 1) ^ (turn >> 1)) & 1
    return j, half


def deal(array):
    half = array.shape[1] // 2
    parts = []
    for turn in range(4):
        j, c = place_of(turn)
        piece = lax.dynamic_slice(array, (j, c * half, 0), (1, half, array.shape[2]))[0]
        parts.append(lax.ppermute(piece, ("batch", "seq"), deal_pairs(turn)))
    return jnp.concatenate(parts, axis=0)


def undeal(array):
    half = array.shape[0] // 4
    out = jnp.zeros((2, 2 * half, array.shape[1]), array.dtype)
    for turn in range(4):
        got = lax.ppermute(array[turn * half : (turn + 1) * half], ("batch", "seq"), deal_pairs(turn, True))
        j, c = place_of(turn)
        out = lax.dynamic_update_slice(out, got[None], (j, c * half, 0))
    return out


def norm_forward(values):
    centre = values - jnp.mean(values, axis=-1, keepdims=True)
    factor = lax.rsqrt(jnp.mean(centre * centre, axis=-1, keepdims=True) + 1e-06)
    return centre * factor, factor


def norm_back(grad, normed, factor):
    return factor * (
        grad
        - jnp.mean(grad, axis=-1, keepdims=True)
        - normed * jnp.mean(grad * normed, axis=-1, keepdims=True)
    )


def gather(array, axis="batch"):
    return lax.all_gather(array, axis, axis=0, tiled=True)


def scatter_sum(array):
    part = lax.psum_scatter(array.astype(bf16), "batch", scatter_dimension=0, tiled=True)
    return lax.psum(part, "seq").astype(f32)


def body(
    inputs,
    conds,
    heights,
    widths,
    qkv_weight,
    qv_bias,
    out_weight,
    out_bias,
    up_weight,
    up_bias,
    down_weight,
    down_bias,
    mod_weight,
    mod_bias,
    cotangent,
):
    devices = lax.axis_size("batch")
    b, s = lax.axis_index("batch"), lax.axis_index("seq")
    c = b & 1
    width = inputs.shape[2]
    hidden = up_weight.shape[1]
    slot_dev = inputs.shape[1]
    half = slot_dev // 2
    rows = qkv_weight.shape[0]
    mods = mod_weight.shape[1]

    tokens16 = deal(inputs)
    counts = (heights * widths).astype(jnp.int32)
    upstream16 = deal(cotangent)

    small = jnp.concatenate([conds.reshape(-1), qv_bias, out_bias, up_bias, down_bias])
    sizes = [conds.size, qv_bias.size, out_bias.size, up_bias.size, down_bias.size]
    small = gather(small[None])
    spots = [sum(sizes[:i]) for i in range(6)]
    every = [small[:, spots[i] : spots[i + 1]] for i in range(5)]
    cond_all = every[0].reshape(2 * devices, width)
    qv_offset, out_offset, up_offset, down_offset = (e.reshape(-1).astype(f32) for e in every[1:])

    qkv_matrix = gather(qkv_weight)

    cond_single = cond_all.astype(f32)
    silu_all = jax.nn.silu(cond_single).astype(bf16)
    silu_rows = lax.dynamic_slice(silu_all, (0, b * rows), (2 * devices, rows))
    plane = lax.dynamic_index_in_dim(silu_rows.reshape(devices // 2, 4, rows), s, axis=1, keepdims=False)
    partial = dot(plane, mod_weight)
    own_bias = lax.dynamic_update_slice(jnp.zeros((mods,), f32), mod_bias.astype(f32), (b * mod_bias.shape[0],))
    partial = partial + own_bias[None]
    partial = jnp.broadcast_to(partial[:, None], (devices // 2, 2, mods)).reshape(devices, mods)
    modulation = lax.psum_scatter(partial, "batch", scatter_dimension=0, tiled=True)
    shift1, scale1, gate1, shift2, scale2, gate2 = jnp.split(modulation, 6, axis=-1)

    pair_counts = pair_swap(jnp.broadcast_to(counts[:, None], (2, 128)))[:, 0]
    group = jnp.where(c == 0, jnp.concatenate([counts, pair_counts]), jnp.concatenate([pair_counts, counts]))
    count = lax.dynamic_index_in_dim(group, s, keepdims=False)
    limits = []
    for part in range(2):
        core = c ^ part
        base = (s & 1) | (((s >> 1) ^ core) << 1)
        for turn in range(4):
            limits.append(count - (slot_dev * (base ^ turn) + half * core))
    limits = jnp.stack(limits).astype(jnp.int32)

    out_matrix = gather(out_weight)
    up_matrix = gather(up_weight)
    down_matrix = gather(down_weight)

    tokens = tokens16.astype(f32)
    normed, factor = norm_forward(tokens)
    moved = (normed * (1.0 + scale1) + shift1).astype(bf16)
    offsets = jnp.concatenate([qv_offset[:width], jnp.zeros((width,), f32), qv_offset[width:]])
    qkv = (dot(moved, qkv_matrix) + offsets).astype(bf16)

    def by_heads(array, parts):
        split = array.reshape(array.shape[0], parts, 2, width // 2)
        own = lax.dynamic_index_in_dim(split, c, axis=2, keepdims=False)
        other = lax.dynamic_index_in_dim(split, 1 - c, axis=2, keepdims=False)
        shape = (array.shape[0], parts * width // 2)
        return own.reshape(shape), pair_swap(other.reshape(shape))

    def by_tokens(own, other, parts):
        shape = (own.shape[0], parts, 1, width // 2)
        got = pair_swap(other).reshape(shape)
        own = own.reshape(shape)
        whole = jnp.where(c == 0, jnp.concatenate([own, got], axis=2), jnp.concatenate([got, own], axis=2))
        return whole.reshape(own.shape[0], parts * width)

    mine, theirs = by_heads(qkv, 3)
    att_mine, att_theirs, lse = attend(limits, mine, theirs)
    attended = by_tokens(att_mine, att_theirs, 1)
    projected = dot(attended, out_matrix) + out_offset
    middle = tokens + gate1 * projected
    normed2, factor2 = norm_forward(middle)
    moved2 = (normed2 * (1.0 + scale2) + shift2).astype(bf16)
    upper = dot(moved2, up_matrix) + up_offset
    gelu_value, gelu_pull = jax.vjp(lambda u: jax.nn.gelu(u, approximate=True), upper)
    act = gelu_value.astype(bf16)
    lowered = dot(act, down_matrix) + down_offset
    output = undeal((middle + gate2 * lowered).astype(bf16))

    upstream = upstream16.astype(f32)
    d_gate2 = jnp.sum(upstream * lowered, axis=0)
    d_lowered = (gate2 * upstream).astype(bf16)
    down_grad = scatter_sum(dot(act, d_lowered, TN))
    down_offset_grad = jnp.sum(d_lowered.astype(f32), axis=0)
    d_act = dot(d_lowered, down_matrix, NT)
    d_upper = gelu_pull(d_act)[0].astype(bf16)
    up_grad = scatter_sum(dot(moved2, d_upper, TN))
    up_offset_grad = jnp.sum(d_upper.astype(f32), axis=0)
    d_moved2 = dot(d_upper, up_matrix, NT)
    d_shift2 = jnp.sum(d_moved2, axis=0)
    d_scale2 = jnp.sum(d_moved2 * normed2, axis=0)
    d_middle = upstream + norm_back(d_moved2 * (1.0 + scale2), normed2, factor2)
    d_gate1 = jnp.sum(d_middle * projected, axis=0)
    d_projected = (gate1 * d_middle).astype(bf16)
    out_grad = scatter_sum(dot(attended, d_projected, TN))
    out_offset_grad = jnp.sum(d_projected.astype(f32), axis=0)
    d_attended = dot(d_projected, out_matrix, NT).astype(bf16)
    d_att_mine, d_att_theirs = by_heads(d_attended, 1)
    d_mine, d_theirs = attend_back(limits, mine, theirs, d_att_mine, d_att_theirs, lse)
    d_qkv = by_tokens(d_mine, d_theirs, 3)
    qkv_grad = scatter_sum(dot(moved, d_qkv, TN))
    column_sums = jnp.sum(d_qkv.astype(f32), axis=0)
    qv_offset_grad = jnp.concatenate([column_sums[:width], column_sums[2 * width :]])
    d_moved = dot(d_qkv, qkv_matrix, NT)
    d_shift1 = jnp.sum(d_moved, axis=0)
    d_scale1 = jnp.sum(d_moved * normed, axis=0)
    input_grad = undeal((d_middle + norm_back(d_moved * (1.0 + scale1), normed, factor)).astype(bf16)).astype(f32)

    partial_mod = jnp.concatenate([d_shift1, d_scale1, d_gate1, d_shift2, d_scale2, d_gate2])
    d_mod = (partial_mod + pair_swap(partial_mod)).astype(bf16)
    share = lax.dynamic_slice(d_mod, (c * (mods // 2),), (mods // 2,))
    all_mod = gather(gather(share[None], "seq"), "batch")
    d_mod_all = (
        all_mod.reshape(devices // 2, 2, 4, mods // 2).transpose(0, 2, 1, 3).reshape(2 * devices, mods)
    )
    mod_grad = dot(silu_rows, d_mod_all, TN)
    mod_offset_grad = jnp.sum(
        lax.dynamic_slice(d_mod_all, (0, b * mod_bias.shape[0]), (2 * devices, mod_bias.shape[0])).astype(f32), axis=0
    )
    d_silu_rows = dot(d_mod_all, mod_weight, NT)
    d_silu = lax.all_to_all(d_silu_rows.reshape(devices, 2, rows), "batch", 0, 0, tiled=True)
    d_silu = d_silu.transpose(1, 0, 2).reshape(2, width)
    cond_grad = jax.vjp(jax.nn.silu, conds.astype(f32))[1](d_silu)[0]

    own_shapes = (qv_bias.shape[0], out_bias.shape[0], up_bias.shape[0], down_bias.shape[0])
    bias = jnp.concatenate(
        [
            g.reshape(devices, -1)
            for g in (qv_offset_grad, out_offset_grad, up_offset_grad, down_offset_grad)
        ],
        axis=1,
    )
    bias = lax.psum(lax.psum_scatter(bias, "batch", scatter_dimension=0, tiled=True), "seq")[0]
    cuts = [sum(own_shapes[:i]) for i in range(5)]
    qv_g, out_g, up_g, down_g = (bias[cuts[i] : cuts[i + 1]] for i in range(4))
    return (
        output,
        input_grad,
        cond_grad,
        qkv_grad,
        qv_g,
        out_grad,
        out_g,
        up_grad,
        up_g,
        down_grad,
        down_g,
        mod_grad,
        mod_offset_grad,
    )


def solution(mesh):
    in_specs = (
        P("batch", "seq", None),
        P("batch", None),
        P("batch"),
        P("batch"),
        P("batch", None),
        P("batch"),
        P("batch", None),
        P("batch"),
        P("batch", None),
        P("batch"),
        P("batch", None),
        P("batch"),
        P("batch", None),
        P("batch"),
        P("batch", "seq", None),
    )
    out_specs = (
        P("batch", "seq", None),
        P("batch", "seq", None),
        P("batch", None),
        P("batch", None),
        P("batch"),
        P("batch", None),
        P("batch"),
        P("batch", None),
        P("batch"),
        P("batch", None),
        P("batch"),
        P("batch", None),
        P("batch"),
    )
    return jax.shard_map(body, mesh=mesh, in_specs=in_specs, out_specs=out_specs, check_vma=False)
```

time: 2020 us -> 868 us (0.43)
  waiting for transfers between devices: 1510 us -> 359 us
  matrix products: 246 us -> 130 us
  Pallas kernels: 0 us -> 79 us
  starting transfers between devices: 1.02 us -> 44.3 us
  other arithmetic: 66.3 us -> 24.6 us
  blocking collectives: 93.9 us -> 120 us
    reduce_scatter x7 -> x4, waiting for transfers between devices: 803 us -> 123 us  [scatter_sum(): lax.psum_scatter(array.astype(bf16), 'batch', scatter_dimension=0, tiled=...]
    psum x1, waiting for transfers between devices: 345 us -> 76.7 us  [scatter_sum(): return lax.psum(part, 'seq').astype(f32)]
    all_gather x7 -> x4, waiting for transfers between devices: 357 us -> 104 us  [gather(): return lax.all_gather(array, axis, axis=0, tiled=True)]
    dot_general x21 -> x15, matrix products: 246 us -> 130 us  [dot(): return lax.dot_general(a, b, dims, preferred_element_type=f32)]
    all_gather x0 -> x3, blocking collectives: none -> 82.6 us  [gather(): return lax.all_gather(array, axis, axis=0, tiled=True)]
    pallas_call x0 -> x2, Pallas kernels: none -> 79 us  [the longest x1 46.8 us: attend_back(): pl.pallas_call(functools.partial(back_kernel, heads), out_shape=(jax.Shap...]
    ppermute x0 -> x22, starting transfers between devices: none -> 40.4 us  [the longest x8 20.1 us: undeal(): lax.ppermute(array[turn * half:(turn + 1) * half], ('batch', 'seq'), deal...]
    unnamed x15 -> x11, waiting for transfers between devices: 3.8 us -> 43.6 us
  transfers between devices with their start and end apart: 15 -> 33, of which waited for: 13 -> 11; matrix products, arithmetic and copies ran while one was open for 13% -> 19% of each run, Pallas kernels for 0% -> 9%
where the time goes in v1:
time: 868 us; the launch traced here: 863 us
  waiting for transfers between devices  359 us (41%)
  matrix products  130 us (15%)
  blocking collectives  120 us (14%)
  local copies, waits for them, and re-layouts  85.5 us (10%)
  Pallas kernels  79 us (9%)
  starting transfers between devices  44.3 us (5%)
  other arithmetic  24.6 us (3%)
  between operations  20.5 us (2%)
    dot_general x15, matrix products, dot(): return lax.dot_general(a, b, dims, preferred_element_type=f32)  130 us
    reduce_scatter x4, waiting for transfers between devices, scatter_sum(): lax.psum_scatter(array.astype(bf16), 'batch', scatter_dimension=0, tiled=...  123 us
    all_gather x4, waiting for transfers between devices, gather(): return lax.all_gather(array, axis, axis=0, tiled=True)  104 us
    all_gather x3, blocking collectives, gather(): return lax.all_gather(array, axis, axis=0, tiled=True)  82.6 us
    psum x1, waiting for transfers between devices, scatter_sum(): return lax.psum(part, 'seq').astype(f32)  76.7 us
    pallas_call x1, Pallas kernels, attend_back(): pl.pallas_call(functools.partial(back_kernel, heads), out_shape=(jax.Shap...  46.8 us
    unnamed x11, waiting for transfers between devices  43.6 us
    pallas_call x1, Pallas kernels, attend(): pl.pallas_call(functools.partial(attend_kernel, heads), out_shape=(jax.Sh...  32.1 us
  transfers between devices with their start and end apart: 33, of which 11 were waited for; matrix products, arithmetic and copies ran while one was open for 19% of the time, Pallas kernels for 9%

profile of v1, /device:TPU:0, one launch (start us, length us, event | category | flops | bytes accessed | tf_op | source)
XLA Modules:
  0.0 862.7 jit_solution(11465135278944677627)
XLA Ops:
  8.1 2.8 concatenate.49
  10.9 10.7 %all-gather.2 = bf16[8,1,3456]{2,1,0:T(2,128)(2,1)S(1)} all-gather(bf16[1,1,3456]{2,1,0:T(2,128)(2,1)S(1)} %reshape.229), channel_id=2, replica_groups=mesh['batch'=8,'seq'=4] {'batch'}, dimensions={0}, use_global_device_ids=true | all-gather | bytes 62208 | tf_op jit(solution)/shard_map/all_gather | solution.py:225
  29.2 4.1 collective-permute-start.2
  35.4 41.1 %all-reduce.6.cloned.1.call-done = f32[8,6912]{1,0:T(8,128)} async-done(((f32[8,6912]{1,0:T(8,128)}), f32[8,6912]{1,0:T(8,128)}) %all-reduce.6.cloned.1.call-update) | async-done | bytes 221200
  76.5 2.3 dynamic-slice_reduce_fusion.1
  79.6 52.4 %all-gather.10.cloned.1.call-done = bf16[1152,3456]{1,0:T(8,128)(2,1)} async-done(((bf16[144,3456]{1,0:T(8,128)(2,1)}), bf16[1152,3456]{1,0:T(8,128)(2,1)}) %all-gather.10.cloned.1.call-update) | async-done | bytes 7962640 | tf_op jit(solution)/shard_map/all_gather | solution.py:225
  132.0 11.2 %add_convert_fusion = bf16[512,3456]{1,0:T(8,128)(2,1)} fusion(bf16[1152,3456]{1,0:T(8,128)(2,1)} %all-gather.10.cloned.1.call-done, f32[3456]{0:T(1024)S(1)} %copy-done.35, f32[1152]{0:T(1024)S(1)} %copy-done.41, f32[1152]{0:T(1024)S(1)} %get-tuple-element.36, f32[512]{0:T(512)S(1)} %add_rsqrt_fusion.1, f32[512]{0:T(512)S(1)} %broadcast_multiply_fusion.5, ...), kind=kOutput, calls=%fused_computation.17 | convolution fusion | flops 4088070144 | bytes 12708352 | tf_op jit(solution)/shard_map/dot_general | solution.py:20
  143.2 5.8 copy.75
  149.0 4.3 constant_dynamic-slice_fusion.1
  153.8 3.2 collective-permute-done.4
  163.0 3.8 copy.76.mine
  166.7 3.7 copy.77.theirs
  172.0 1.7 copy-done.3
  173.7 32.1 %shard_map.246 = (bf16[512,576]{1,0:T(8,128)(2,1)S(1)}, bf16[512,576]{1,0:T(8,128)(2,1)S(1)}, f32[8,1024]{1,0:T(8,128)S(1)}) custom-call(s32[8]{0:T(128)S(1)} %stack.35.limits, bf16[512,1728]{1,0:T(8,128)(2,1)S(1)} %copy-done.1, bf16[512,1728]{1,0:T(8,128)(2,1)S(1)} %copy-done.3), custom_call_target="tpu_custom_call" | custom-call | flops 4294967296 | bytes 4718592 | tf_op jit(solution)/shard_map/pallas_call | solution.py:63
  207.3 2.4 dynamic-slice_bitcast_fusion.4
  209.7 2.8 collective-permute-start.13
  213.3 3.7 collective-permute-start.11
  218.6 2.9 maximum_select_fusion.1
  221.4 2.6 copy.80
  224.1 5.7 fusion.45
  231.6 12.2 %fusion.44 = f32[512,4608]{1,0:T(8,128)} fusion(bf16[1152,4608]{1,0:T(8,128)(2,1)} %all-gather.14.cloned.1.call-done, f32[512,1152]{1,0:T(8,128)} %copy-done.24, f32[1152]{0:T(1024)S(1)} %copy-done.39, f32[1152]{0:T(1024)S(1)} %copy-done.37, f32[512]{0:T(512)S(1)} %add_rsqrt_fusion, f32[512]{0:T(512)S(1)} %broadcast_multiply_fusion.4), kind=kOutput, calls=%fused_computation.139 | convolution fusion | flops 5438767104 | bytes 22426624 | tf_op jit(solution)/shard_map/dot_general | solution.py:20
  243.9 52.0 %all-gather.16.cloned.1.call-done = bf16[4608,1152]{1,0:T(8,128)(2,1)} async-done(((bf16[576,1152]{1,0:T(8,128)(2,1)}), bf16[4608,1152]{1,0:T(8,128)(2,1)}) %all-gather.16.cloned.1.call-update) | async-done | bytes 10616848 | tf_op jit(solution)/shard_map/all_gather | solution.py:225
  295.9 16.2 %convert_reduce_fusion = (f32[4608]{0:T(1024)S(1)}, bf16[512,4608]{1,0:T(8,128)(2,1)S(1)}) fusion(f32[512,4608]{1,0:T(8,128)} %fusion.44, f32[4608]{0:T(1024)S(1)} %reshape.225, bf16[4608,1152]{1,0:T(8,128)(2,1)} %all-gather.16.cloned.1.call-done, f32[1152]{0:T(1024)S(1)} %copy-done.36, bf16[128,1152]{1,0:T(8,128)(2,1)} %collective-permute-done.14, ...), kind=kOutput, calls=%fused_computation.12 | convolution fusion | flops 5495975424 | bytes 25993728 | tf_op jit(solution)/shard_map/dot_general | solution.py:20
  312.1 13.1 %multiply_reduce_fusion = (f32[1152]{0:T(1024)}, f32[512]{0:T(512)S(1)}, f32[512]{0:T(512)S(1)}, f32[1152]{0:T(1024)}, f32[512,1152]{1,0:T(8,128)S(1)}) fusion(f32[512,1152]{1,0:T(8,128)S(1)} %copy-done.25, f32[512]{0:T(512)S(1)} %add_rsqrt_fusion, f32[512]{0:T(512)S(1)} %broadcast_multiply_fusion.4, f32[1152]{0:T(1024)S(1)} %copy-done.37, ...), kind=kOutput, calls=%fused_computation.47 | convolution fusion | flops 5441123328 | bytes 20076032 | tf_op jit(solution)/shard_map/dot_general | solution.py:20
  325.2 16.4 %convert_reduce_fusion.3 = (f32[1152]{0:T(1024)}, f32[1152]{0:T(1024)}, bf16[512,1152]{1,0:T(8,128)(2,1)}, f32[1152]{0:T(1024)}, bf16[512,1152]{1,0:T(8,128)(2,1)S(1)}, /*index=5*/f32[512,1152]{1,0:T(8,128)}) fusion(f32[1152]{0:T(1024)S(1)} %copy-done.36, bf16[128,1152]{1,0:T(8,128)(2,1)} %collective-permute-done.14, ...), kind=kOutput, calls=%fused_computation.45 | convolution fusion | flops 5477102592 | bytes 30729728 | tf_op jit(solution)/shard_map/dot_general | solution.py:20
  342.7 2.9 convolution_convert_fusion.4
  349.9 4.8 convolution_convert_fusion.3
  359.4 46.8 %shard_map.247 = (bf16[512,1728]{1,0:T(8,128)(2,1)S(1)}, bf16[512,1728]{1,0:T(8,128)(2,1)S(1)}) custom-call(s32[8]{0:T(128)S(1)} %stack.35.limits, bf16[512,1728]{1,0:T(8,128)(2,1)S(1)} %copy-done.2, bf16[512,1728]{1,0:T(8,128)(2,1)S(1)} %copy-done.4, bf16[512,576]{1,0:T(8,128)(2,1)S(1)} %bitcast.97, bf16[512,576]{1,0:T(8,128)(2,1)S(1)} %copy.85.d_theirs, ...), custom_call_target="tpu_custom_call" | custom-call | flops 10737418240 | bytes 9437184 | tf_op jit(solution)/shard_map/pallas_call | solution.py:140
  408.7 3.8 copy.87
  412.7 3.8 copy.86
  416.5 3.9 convert_reduce_fusion.1
  421.0 1.8 copy-done.7
  422.8 7.6 convolution_convert_fusion.2
  431.1 11.8 %convolution_convert_fusion.1 = bf16[1152,4608]{1,0:T(8,128)(2,1)} fusion(bf16[512,4608]{1,0:T(8,128)(2,1)} %copy-done.58, f32[512,1152]{1,0:T(8,128)} %copy-done.24, f32[1152]{0:T(1024)S(1)} %copy-done.40, f32[1152]{0:T(1024)S(1)} %copy-done.38, f32[512]{0:T(512)S(1)} %copy-done.52, f32[512]{0:T(512)S(1)} %broadcast_multiply_fusion.4), kind=kOutput, calls=%fused_computation.1 | convolution fusion | flops 5444075520 | bytes 17708032 | tf_op jit(solution)/shard_map/dot_general | solution.py:20
  443.0 14.5 %convolution_convert_fusion = bf16[4608,1152]{1,0:T(8,128)(2,1)} fusion(f32[1152]{0:T(1024)S(1)} %copy-done.36, bf16[128,1152]{1,0:T(8,128)(2,1)} %collective-permute-done.14, bf16[128,1152]{1,0:T(8,128)(2,1)} %collective-permute-done.13, bf16[128,1152]{1,0:T(8,128)(2,1)} %collective-permute-done.12, bf16[128,1152]{1,0:T(8,128)(2,1)} %collective-permute-done.11, ...), kind=kOutput, calls=%fused_computation | convolution fusion | flops 5470617600 | bytes 21256704 | tf_op jit(solution)/shard_map/dot_general | solution.py:20
  457.6 2.2 fusion.47
  459.7 3.7 collective-permute-start.7
  463.5 1.6 collective-permute-start.8
  465.1 2.6 collective-permute-start.9
  467.7 2.2 collective-permute-start.10
  472.0 2.1 bitcast_dynamic-update-slice_fusion.7
  474.1 2.1 collective-permute-done.8
  476.2 1.7 bitcast_dynamic-update-slice_fusion.6
  479.2 1.7 bitcast_dynamic-update-slice_fusion.5
  480.9 3.0 collective-permute-done.10
  483.9 1.7 bitcast_dynamic-update-slice_fusion.4
  485.6 9.8 %fusion.20 = (f32[1152]{0:T(1024)S(1)}, f32[512]{0:T(512)S(1)}, f32[512]{0:T(512)S(1)}, f32[1152]{0:T(1024)S(1)}, f32[512,1152]{1,0:T(8,128)S(1)}) fusion(f32[512]{0:T(512)} %copy-done.48, f32[512]{0:T(512)S(1)} %broadcast_multiply_fusion.5, bf16[128,1152]{1,0:T(8,128)(2,1)S(1)} %copy-done.11, bf16[128,1152]{1,0:T(8,128)(2,1)S(1)} %copy-done.14, ...), kind=kOutput, calls=%fused_computation.41 | convolution fusion | flops 4086887424 | bytes 15062528 | tf_op jit(solution)/shard_map/dot_general | solution.py:20
  498.1 1.9 multiply_reduce_fusion.1
  505.2 5.2 collective-permute-start.21
  510.8 23.7 %all-reduce.1 = f32[8,1152]{1,0:T(8,128)S(1)} all-reduce(f32[8,1152]{1,0:T(8,128)S(1)} %concatenate.62), channel_id=6, replica_groups=mesh['batch'=8,'seq'=4] {'batch'}, use_global_device_ids=true, to_apply=%region_21.22.clone | all-reduce | flops 9216 | bytes 73728
  535.1 13.7 %psum.36 = f32[1,1152]{1,0:T(1,128)S(1)} all-reduce(f32[1,1152]{1,0:T(1,128)S(1)} %constant_dynamic-slice_fusion.4), channel_id=1, replica_groups=mesh['batch'=8,'seq'=4] {'seq'}, use_global_device_ids=true, to_apply=%region_22.23 | all-reduce | flops 1152 | bytes 9216 | tf_op jit(solution)/shard_map/psum | solution.py:386
  549.5 37.2 %reduce-scatter.9.cloned.1.call-done = bf16[144,4608]{1,0:T(8,128)(2,1)} async-done(((bf16[1152,4608]{1,0:T(8,128)(2,1)}), bf16[144,4608]{1,0:T(8,128)(2,1)}) %reduce-scatter.9.cloned.1.call-update) | async-done | bytes 1327120 | tf_op jit(solution)/shard_map/reduce_scatter | solution.py:229
  586.7 86.1 %reduce-scatter.11.cloned.1.call-done = bf16[576,1152]{1,0:T(8,128)(2,1)} async-done(((bf16[4608,1152]{1,0:T(8,128)(2,1)}), bf16[576,1152]{1,0:T(8,128)(2,1)}) %reduce-scatter.11.cloned.1.call-update) | async-done | bytes 1327120 | tf_op jit(solution)/shard_map/reduce_scatter | solution.py:229
  675.1 3.7 collective-permute-start.17
  680.3 2.2 collective-permute-start.19
  682.5 2.5 collective-permute-start.20
  685.8 63.5 %all-gather.3 = bf16[4,1,3456]{2,1,0:T(2,128)(2,1)S(1)} all-gather(bf16[1,1,3456]{2,1,0:T(2,128)(2,1)S(1)} %reshape.231), channel_id=3, replica_groups=mesh['batch'=8,'seq'=4] {'seq'}, dimensions={0}, use_global_device_ids=true | all-gather | bytes 34560 | tf_op jit(solution)/shard_map/all_gather | solution.py:225
  749.3 8.4 all-gather.4
  759.3 3.3 all-to-all-start
  762.7 2.6 fusion.51
  771.9 76.7 %all-reduce.8.cloned.1.call-done = (bf16[144,3456]{1,0:T(8,128)(2,1)}, bf16[144,1152]{1,0:T(8,128)(2,1)}, bf16[144,4608]{1,0:T(8,128)(2,1)}, bf16[576,1152]{1,0:T(8,128)(2,1)}) async-done(((bf16[144,3456]{1,0:T(8,128)(2,1)}, bf16[144,1152]{1,0:T(8,128)(2,1)}, bf16[144,4608]{1,0:T(8,128)(2,1)}, bf16[576,1152]{1,0:T(8,128)(2,1)}), (bf16[144,3456]{1,0:T(8,128)(2,1)}, bf16[144,1152]{1,0:T(8,128)(2,1)}, ...) | async-done | bytes 3981328 | tf_op jit(solution)/shard_map/psum | solution.py:230
  848.6 2.7 convert_element_type.158
  852.2 1.8 convert_element_type.166
  854.0 1.7 convert_element_type.168
  (260 shorter events, 59.8 us)
Async XLA Ops:
  7.2 15.4 %copy-start = (bf16[144,6912]{1,0:T(8,128)(2,1)S(1)}, bf16[144,6912]{1,0:T(8,128)(2,1)}, u32[]{:S(2)}) copy-start(bf16[144,6912]{1,0:T(8,128)(2,1)} %param.27) | copy-start | bytes 5971972
  7.2 69.3 %all-reduce.6.cloned.1.call-start = ((), (), s32[]{:S(2)}) async-start(), calls=%async_computation.13 | async-start | bytes 442368
  23.9 108.0 %all-gather.10.cloned.1.call-start = ((), (), s32[]{:S(2)}) async-start(), calls=%async_computation.5 | async-start | bytes 8957952 | tf_op jit(solution)/shard_map/all_gather | solution.py:225
  24.7 199.3 %all-gather.12.cloned.1.call-start = ((), (), s32[]{:S(2)}) async-start(), calls=%async_computation.6 | async-start | bytes 2985984 | tf_op jit(solution)/shard_map/all_gather | solution.py:225
  25.4 8.8 %copy-start.56 = (u32[32]{0:T(128)S(1)}, u32[32]{0:T(128)}, u32[]{:S(2)}) copy-start(u32[32]{0:T(128)} %constant.97) | copy-start | bytes 388
  25.4 206.1 %all-gather.14.cloned.1.call-start = ((), (), s32[]{:S(2)}) async-start(), calls=%async_computation.7 | async-start | bytes 11943936 | tf_op jit(solution)/shard_map/all_gather | solution.py:225
  26.0 269.9 %all-gather.16.cloned.1.call-start = ((), (), s32[]{:S(2)}) async-start(), calls=%async_computation.8 | async-start | bytes 11943936 | tf_op jit(solution)/shard_map/all_gather | solution.py:225
  26.6 522.9 %reduce-scatter.7.cloned.1.call-start = ((), (), s32[]{:S(2)}) async-start(), calls=%async_computation.10 | async-start | bytes 2985984 | tf_op jit(solution)/shard_map/reduce_scatter | solution.py:229
  27.6 51.2 %collective-permute-start.3 = (bf16[128,1152]{1,0:T(8,128)(2,1)}, bf16[128,1152]{1,0:T(8,128)(2,1)S(1)}, u32[]{:S(2)}, u32[]{:S(2)}) collective-permute-start(bf16[128,1152]{1,0:T(8,128)(2,1)} %get-tuple-element.76), channel_id=1, source_target_pairs={{0,5},{1,4},{2,1},{3,0},{4,3},{5,2},{6,7},{7,6},{8,13},{9,12},{10,... | collective-permute-start | bytes 884744 | tf_op jit(solution)/shard_map/ppermute | solution.py:196
  29.2 49.6 %collective-permute-start.2 = (bf16[128,1152]{1,0:T(8,128)(2,1)}, bf16[128,1152]{1,0:T(8,128)(2,1)S(1)}, u32[]{:S(2)}, u32[]{:S(2)}) collective-permute-start(bf16[128,1152]{1,0:T(8,128)(2,1)} %get-tuple-element.77), channel_id=1, source_target_pairs={{0,4},{1,5},{2,0},{3,1},{4,2},{5,3},{6,6},{7,7},{8,12},{9,13},{10,... | collective-permute-start | bytes 884744 | tf_op jit(solution)/shard_map/ppermute | solution.py:196
  33.3 45.6 %collective-permute-start.1 = (bf16[128,1152]{1,0:T(8,128)(2,1)}, bf16[128,1152]{1,0:T(8,128)(2,1)S(1)}, u32[]{:S(2)}, u32[]{:S(2)}) collective-permute-start(bf16[128,1152]{1,0:T(8,128)(2,1)} %get-tuple-element.75), channel_id=1, source_target_pairs={{0,1},{1,0},{2,5},{3,4},{4,7},{5,6},{6,3},{7,2},{8,9},{9,8},{10,13... | collective-permute-start | bytes 884744 | tf_op jit(solution)/shard_map/ppermute | solution.py:196
  33.3 45.5 %collective-permute-start = (bf16[128,1152]{1,0:T(8,128)(2,1)S(1)}, bf16[128,1152]{1,0:T(8,128)(2,1)S(1)}, u32[]{:S(2)}, u32[]{:S(2)}) collective-permute-start(bf16[128,1152]{1,0:T(8,128)(2,1)S(1)} %get-tuple-element.74), channel_id=1, source_target_pairs={{0,0},{1,1},{2,4},{3,5},{4,6},{5,7},{6,2},{7,3},{8,8},{9,9},{10,12... | collective-permute-start | bytes 884744 | tf_op jit(solution)/shard_map/ppermute | solution.py:196
  35.4 96.6 %copy-start.35 = (f32[3456]{0:T(1024)S(1)}, f32[3456]{0:T(1024)}, u32[]{:S(2)}) copy-start(f32[3456]{0:T(1024)} %pad_maximum_fusion.2) | copy-start | bytes 41476
  78.8 64.4 %copy-start.9 = (bf16[128,1152]{1,0:T(8,128)(2,1)}, bf16[128,1152]{1,0:T(8,128)(2,1)S(1)}, u32[]{:S(2)}) copy-start(bf16[128,1152]{1,0:T(8,128)(2,1)S(1)} %collective-permute-done.3) | copy-start | bytes 884740
  78.8 64.4 %copy-start.12 = (bf16[128,1152]{1,0:T(8,128)(2,1)}, bf16[128,1152]{1,0:T(8,128)(2,1)S(1)}, u32[]{:S(2)}) copy-start(bf16[128,1152]{1,0:T(8,128)(2,1)S(1)} %collective-permute-done.2) | copy-start | bytes 884740
  78.8 64.3 %copy-start.16 = (bf16[128,1152]{1,0:T(8,128)(2,1)}, bf16[128,1152]{1,0:T(8,128)(2,1)S(1)}, u32[]{:S(2)}) copy-start(bf16[128,1152]{1,0:T(8,128)(2,1)S(1)} %collective-permute-done.1) | copy-start | bytes 884740
  78.8 64.3 %copy-start.20 = (bf16[128,1152]{1,0:T(8,128)(2,1)}, bf16[128,1152]{1,0:T(8,128)(2,1)S(1)}, u32[]{:S(2)}) copy-start(bf16[128,1152]{1,0:T(8,128)(2,1)S(1)} %collective-permute-done) | copy-start | bytes 884740
  78.8 53.1 %copy-start.41 = (f32[1152]{0:T(1024)S(1)}, f32[1152]{0:T(1024)}, u32[]{:S(2)}) copy-start(f32[1152]{0:T(1024)} %get-tuple-element.35) | copy-start | bytes 13828
  79.6 63.6 %copy-start.48 = (f32[512]{0:T(512)}, f32[512]{0:T(512)S(1)}, u32[]{:S(2)}) copy-start(f32[512]{0:T(512)S(1)} %add_rsqrt_fusion.1) | copy-start | bytes 6148
  149.0 4.5 copy-start.54
  149.0 4.5 copy-start.55
  153.2 13.5 %collective-permute-start.5 = (bf16[512,1728]{0,1:T(8,128)(2,1)}, bf16[512,1728]{0,1:T(8,128)(2,1)}, u32[]{:S(2)}, u32[]{:S(2)}) collective-permute-start(bf16[512,1728]{0,1:T(8,128)(2,1)} %bitcast.16), channel_id=1, source_target_pairs={{0,4},{4,0},{8,12},{12,8},{16,20},{20,16},{24,28},{28,24},{1,5},{5... | collective-permute-start | bytes 5308424 | tf_op jit(solution)/shard_map/ppermute | solution.py:168
  153.5 3.5 collective-permute-start.4
  206.9 10.5 %collective-permute-start.6 = (bf16[512,576]{0,1:T(8,128)(2,1)}, bf16[512,576]{0,1:T(8,128)(2,1)S(1)}, u32[]{:S(2)}, u32[]{:S(2)}) collective-permute-start(bf16[512,576]{0,1:T(8,128)(2,1)} %copy.78), channel_id=1, source_target_pairs={{0,4},{4,0},{8,12},{12,8},{16,20},{20,16},{24,28},{28,24},{1,5},{5... | collective-permute-start | bytes 1769480 | tf_op jit(solution)/shard_map/ppermute | solution.py:168
  209.7 34.1 %collective-permute-start.14 = (bf16[128,1152]{1,0:T(8,128)(2,1)}, bf16[128,1152]{1,0:T(8,128)(2,1)}, u32[]{:S(2)}, u32[]{:S(2)}) collective-permute-start(bf16[128,1152]{1,0:T(8,128)(2,1)} %get-tuple-element.68), channel_id=1, source_target_pairs={{0,5},{1,4},{2,1},{3,0},{4,3},{5,2},{6,7},{7,6},{8,13},{9,12},{10,... | collective-permute-start | bytes 884744 | tf_op jit(solution)/shard_map/ppermute | solution.py:196
  209.7 34.1 %collective-permute-start.13 = (bf16[128,1152]{1,0:T(8,128)(2,1)}, bf16[128,1152]{1,0:T(8,128)(2,1)}, u32[]{:S(2)}, u32[]{:S(2)}) collective-permute-start(bf16[128,1152]{1,0:T(8,128)(2,1)} %get-tuple-element.69), channel_id=1, source_target_pairs={{0,4},{1,5},{2,0},{3,1},{4,2},{5,3},{6,6},{7,7},{8,12},{9,13},{10,... | collective-permute-start | bytes 884744 | tf_op jit(solution)/shard_map/ppermute | solution.py:196
  212.5 31.3 %collective-permute-start.12 = (bf16[128,1152]{1,0:T(8,128)(2,1)}, bf16[128,1152]{1,0:T(8,128)(2,1)}, u32[]{:S(2)}, u32[]{:S(2)}) collective-permute-start(bf16[128,1152]{1,0:T(8,128)(2,1)} %get-tuple-element.67), channel_id=1, source_target_pairs={{0,1},{1,0},{2,5},{3,4},{4,7},{5,6},{6,3},{7,2},{8,9},{9,8},{10,13... | collective-permute-start | bytes 884744 | tf_op jit(solution)/shard_map/ppermute | solution.py:196
  213.3 30.5 %collective-permute-start.11 = (bf16[128,1152]{1,0:T(8,128)(2,1)}, bf16[128,1152]{1,0:T(8,128)(2,1)}, u32[]{:S(2)}, u32[]{:S(2)}) collective-permute-start(bf16[128,1152]{1,0:T(8,128)(2,1)} %get-tuple-element.66), channel_id=1, source_target_pairs={{0,0},{1,1},{2,4},{3,5},{4,6},{5,7},{6,2},{7,3},{8,8},{9,9},{10,12... | collective-permute-start | bytes 884744 | tf_op jit(solution)/shard_map/ppermute | solution.py:196
  218.6 5.5 copy-start.10
  218.6 5.5 copy-start.13
  218.6 5.5 copy-start.43
  231.5 93.7 %copy-start.51 = (f32[512]{0:T(512)}, f32[512]{0:T(512)S(1)}, u32[]{:S(2)}) copy-start(f32[512]{0:T(512)S(1)} %add_rsqrt_fusion) | copy-start | bytes 6148
  231.6 64.3 %copy-start.36 = (f32[1152]{0:T(1024)S(1)}, f32[1152]{0:T(1024)}, u32[]{:S(2)}) copy-start(f32[1152]{0:T(1024)} %get-tuple-element.33) | copy-start | bytes 13828
  295.9 16.2 %copy-start.25 = (f32[512,1152]{1,0:T(8,128)S(1)}, f32[512,1152]{1,0:T(8,128)}, u32[]{:S(2)}) copy-start(f32[512,1152]{1,0:T(8,128)} %copy-done.24) | copy-start | bytes 7077892
  312.1 13.1 %copy-start.58 = (bf16[512,4608]{1,0:T(8,128)(2,1)}, bf16[512,4608]{1,0:T(8,128)(2,1)S(1)}, u32[]{:S(2)}) copy-start(bf16[512,4608]{1,0:T(8,128)(2,1)S(1)} %get-tuple-element.90) | copy-start | bytes 14155780
  325.2 17.5 %copy-start.53 = (bf16[1152,1152]{1,0:T(8,128)(2,1)S(1)}, bf16[1152,1152]{1,0:T(8,128)(2,1)}, u32[]{:S(2)}) copy-start(bf16[1152,1152]{1,0:T(8,128)(2,1)} %all-gather.12.cloned.1.call-done) | copy-start | bytes 7962628
  348.3 6.7 collective-permute-start.15
  354.7 194.8 %reduce-scatter.5.cloned.1.call-start = ((), (), s32[]{:S(2)}) async-start(), calls=%async_computation.9 | async-start | bytes 8957952 | tf_op jit(solution)/shard_map/reduce_scatter | solution.py:229
  412.5 4.1 collective-permute-start.16
  430.4 156.3 %reduce-scatter.9.cloned.1.call-start = ((), (), s32[]{:S(2)}) async-start(), calls=%async_computation.11 | async-start | bytes 11943936 | tf_op jit(solution)/shard_map/reduce_scatter | solution.py:229
  443.0 229.9 %reduce-scatter.11.cloned.1.call-start = ((), (), s32[]{:S(2)}) async-start(), calls=%async_computation.12 | async-start | bytes 11943936 | tf_op jit(solution)/shard_map/reduce_scatter | solution.py:229
  457.5 12.4 %copy-start.47 = (f32[1152]{0:T(1024)S(1)}, f32[1152]{0:T(1024)}, u32[]{:S(2)}) copy-start(f32[1152]{0:T(1024)} %get-tuple-element.55) | copy-start | bytes 13828
  457.5 391.1 %all-reduce.8.cloned.1.call-start = ((), (), s32[]{:S(2)}) async-start(), calls=%async_computation.14 | async-start | bytes 7962624 | tf_op jit(solution)/shard_map/psum | solution.py:230
  459.7 11.1 %collective-permute-start.7 = (bf16[128,1152]{1,0:T(8,128)(2,1)}, bf16[128,1152]{1,0:T(8,128)(2,1)}, u32[]{:S(2)}, u32[]{:S(2)}) collective-permute-start(bf16[128,1152]{1,0:T(8,128)(2,1)} %get-tuple-element.73), channel_id=1, source_target_pairs={{0,0},{1,1},{4,2},{5,3},{6,4},{7,5},{2,6},{3,7},{8,8},{9,9},{12,10... | collective-permute-start | bytes 884744 | tf_op jit(solution)/shard_map/ppermute | solution.py:204
  463.5 12.7 %collective-permute-start.8 = (bf16[128,1152]{1,0:T(8,128)(2,1)}, bf16[128,1152]{1,0:T(8,128)(2,1)}, u32[]{:S(2)}, u32[]{:S(2)}) collective-permute-start(bf16[128,1152]{1,0:T(8,128)(2,1)} %get-tuple-element.72), channel_id=1, source_target_pairs={{1,0},{0,1},{5,2},{4,3},{7,4},{6,5},{3,6},{2,7},{9,8},{8,9},{13,10... | collective-permute-start | bytes 884744 | tf_op jit(solution)/shard_map/ppermute | solution.py:204
  465.1 14.1 %collective-permute-start.9 = (bf16[128,1152]{1,0:T(8,128)(2,1)}, bf16[128,1152]{1,0:T(8,128)(2,1)}, u32[]{:S(2)}, u32[]{:S(2)}) collective-permute-start(bf16[128,1152]{1,0:T(8,128)(2,1)} %get-tuple-element.71), channel_id=1, source_target_pairs={{4,0},{5,1},{0,2},{1,3},{2,4},{3,5},{6,6},{7,7},{12,8},{13,9},{8,1... | collective-permute-start | bytes 884744 | tf_op jit(solution)/shard_map/ppermute | solution.py:204
  467.7 16.2 %collective-permute-start.10 = (bf16[128,1152]{1,0:T(8,128)(2,1)S(1)}, bf16[128,1152]{1,0:T(8,128)(2,1)}, u32[]{:S(2)}, u32[]{:S(2)}) collective-permute-start(bf16[128,1152]{1,0:T(8,128)(2,1)S(1)} %get-tuple-element.70), channel_id=1, source_target_pairs={{5,0},{4,1},{1,2},{0,3},{3,4},{2,5},{7,6},{6,7},{13,8},{12,9},{9,1... | collective-permute-start | bytes 884744 | tf_op jit(solution)/shard_map/ppermute | solution.py:204
  470.9 14.7 %copy-start.8 = (bf16[512,3,2,576]{0,3,2,1:T(8,128)(2,1)S(1)}, bf16[512,3,2,576]{0,3,2,1:T(8,128)(2,1)}, u32[]{:S(2)}) copy-start(bf16[512,3,2,576]{0,3,2,1:T(8,128)(2,1)} %copy-done.7) | copy-start | bytes 10616836
  485.6 12.5 %copy-start.15 = (bf16[128,1152]{1,0:T(8,128)(2,1)S(1)}, bf16[128,1152]{1,0:T(8,128)(2,1)}, u32[]{:S(2)}) copy-start(bf16[128,1152]{1,0:T(8,128)(2,1)} %copy-done.12) | copy-start | bytes 884740
  485.6 12.5 %copy-start.19 = (bf16[128,1152]{1,0:T(8,128)(2,1)S(1)}, bf16[128,1152]{1,0:T(8,128)(2,1)}, u32[]{:S(2)}) copy-start(bf16[128,1152]{1,0:T(8,128)(2,1)} %copy-done.16) | copy-start | bytes 884740
  485.6 12.5 %copy-start.23 = (bf16[128,1152]{1,0:T(8,128)(2,1)S(1)}, bf16[128,1152]{1,0:T(8,128)(2,1)}, u32[]{:S(2)}) copy-start(bf16[128,1152]{1,0:T(8,128)(2,1)} %copy-done.20) | copy-start | bytes 884740
  485.6 12.5 %copy-start.26 = (f32[512,1152]{1,0:T(8,128)S(1)}, f32[512,1152]{1,0:T(8,128)}, u32[]{:S(2)}) copy-start(f32[512,1152]{1,0:T(8,128)} %get-tuple-element.86) | copy-start | bytes 7077892
  485.6 12.5 %copy-start.27 = (f32[512,1152]{1,0:T(8,128)S(1)}, f32[512,1152]{1,0:T(8,128)}, u32[]{:S(2)}) copy-start(f32[512,1152]{1,0:T(8,128)} %get-tuple-element.57) | copy-start | bytes 7077892
  485.6 12.5 %copy-start.50 = (f32[512]{0:T(512)S(1)}, f32[512]{0:T(512)}, u32[]{:S(2)}) copy-start(f32[512]{0:T(512)} %copy-done.48) | copy-start | bytes 6148
  498.1 4.5 copy-start.44
  498.1 5.8 copy-start.46
  505.2 179.7 %collective-permute-start.21 = (f32[6912]{0:T(1024)}, f32[6912]{0:T(1024)S(1)}, u32[]{:S(2)}, u32[]{:S(2)}) collective-permute-start(f32[6912]{0:T(1024)} %constant_dynamic-update-slice_fusion.1), channel_id=1, source_target_pairs={{0,4},{4,0},{8,12},{12,8},{16,20},{20,16},{24,28},{28,24},{1,5},{5... | collective-permute-start | bytes 82952 | tf_op jit(solution)/shard_map/ppermute | solution.py:168
  674.5 88.3 %copy-start.33 = (bf16[16,144]{1,0:T(8,128)(2,1)S(1)}, bf16[16,144]{1,0:T(8,128)(2,1)}, u32[]{:S(2)}) copy-start(bf16[16,144]{1,0:T(8,128)(2,1)} %copy-done.32) | copy-start | bytes 13828
  675.1 93.0 %collective-permute-start.17 = (bf16[128,1152]{1,0:T(8,128)(2,1)}, bf16[128,1152]{1,0:T(8,128)(2,1)}, u32[]{:S(2)}, u32[]{:S(2)}) collective-permute-start(bf16[128,1152]{1,0:T(8,128)(2,1)} %get-tuple-element.63), channel_id=1, source_target_pairs={{0,0},{1,1},{4,2},{5,3},{6,4},{7,5},{2,6},{3,7},{8,8},{9,9},{12,10... | collective-permute-start | bytes 884744 | tf_op jit(solution)/shard_map/ppermute | solution.py:204
  678.8 90.4 %collective-permute-start.18 = (bf16[128,1152]{1,0:T(8,128)(2,1)}, bf16[128,1152]{1,0:T(8,128)(2,1)}, u32[]{:S(2)}, u32[]{:S(2)}) collective-permute-start(bf16[128,1152]{1,0:T(8,128)(2,1)} %get-tuple-element.62), channel_id=1, source_target_pairs={{1,0},{0,1},{5,2},{4,3},{7,4},{6,5},{3,6},{2,7},{9,8},{8,9},{13,10... | collective-permute-start | bytes 884744 | tf_op jit(solution)/shard_map/ppermute | solution.py:204
  680.3 89.9 %collective-permute-start.19 = (bf16[128,1152]{1,0:T(8,128)(2,1)}, bf16[128,1152]{1,0:T(8,128)(2,1)S(1)}, u32[]{:S(2)}, u32[]{:S(2)}) collective-permute-start(bf16[128,1152]{1,0:T(8,128)(2,1)} %get-tuple-element.61), channel_id=1, source_target_pairs={{4,0},{5,1},{0,2},{1,3},{2,4},{3,5},{6,6},{7,7},{12,8},{13,9},{8,1... | collective-permute-start | bytes 884744 | tf_op jit(solution)/shard_map/ppermute | solution.py:204
  682.5 87.8 %collective-permute-start.20 = (bf16[128,1152]{1,0:T(8,128)(2,1)S(1)}, bf16[128,1152]{1,0:T(8,128)(2,1)S(1)}, u32[]{:S(2)}, u32[]{:S(2)}) collective-permute-start(bf16[128,1152]{1,0:T(8,128)(2,1)S(1)} %get-tuple-element.60), channel_id=1, source_target_pairs={{5,0},{4,1},{1,2},{0,3},{3,4},{2,5},{7,6},{6,7},{13,8},{12,9},{9,1... | collective-permute-start | bytes 884744 | tf_op jit(solution)/shard_map/ppermute | solution.py:204
  759.3 8.0 all-to-all-start
  762.7 4.8 copy-start.34
  (28 other events, 54.8 us)
Sparse Core Ops, SparseCore 0:
  24.1 52.4 all-reduce.5
  78.6 53.3 all-gather.9
  134.0 30.2 all-gather.11
  166.2 63.9 all-gather.13
  232.1 63.7 all-gather.15
  354.9 43.7 reduce-scatter.6
  430.5 70.0 reduce-scatter.4
  504.5 82.1 reduce-scatter.8
  590.7 82.1 reduce-scatter.10
  675.5 173.0 all-reduce.7

commit v2 on v1

v2 whole, which is shorter than its diff:
```python
import functools

import jax
import jax.numpy as jnp
from jax import lax
from jax.experimental import pallas as pl
from jax.experimental.pallas import tpu as pltpu
from jax.sharding import PartitionSpec as P

HEADS = 16
HEAD = 72
SCALE = HEAD ** (-0.5)
LOG2E = 1.4426950408889634
f32 = jnp.float32
bf16 = jnp.bfloat16
NT = (((1,), (1,)), ((), ()))
TN = (((0,), (0,)), ((), ()))


def dot(a, b, dims=(((1,), (0,)), ((), ()))):
    return lax.dot_general(a, b, dims, preferred_element_type=f32)


WHOLE = pl.BlockSpec()
SMEM = pl.BlockSpec(memory_space=pltpu.SMEM)
HBM = pl.BlockSpec(memory_space=pltpu.HBM)
BLOCK = 512
PAD = 128
ROOT = 0.7978845608028654
VMEM_ATT = 48
LIGHT = pl.CostEstimate(flops=0, bytes_accessed=0, transcendentals=0)


def shaped(shape, kind):
    return pltpu.HBM(shape, kind)


def in_hbm(*arrays):
    return tuple(pltpu.with_memory_space_constraint(array, pltpu.HBM) for array in arrays)


def lanes(wide):
    return -(-wide // 128) * 128


def params(mib):
    return pltpu.CompilerParams(vmem_limit_bytes=mib * 2**20)


def on_core(core, work):
    for c in range(2):
        pl.when(core[0] == c)(functools.partial(work, c))


def split_kernel(core, source, mine, away):
    wide = source.shape[1] // 2

    def work(c):
        for ref, d in ((mine, c), (away, 1 - c)):
            ref[:, :wide] = source[:, d * wide : (d + 1) * wide]

    on_core(core, work)


def split_heads(core, array):
    rows, wide = array.shape[0], array.shape[1] // 2
    return pl.pallas_call(
        split_kernel,
        out_shape=(shaped((rows, wide), bf16), shaped((rows, lanes(wide)), bf16)),
        in_specs=[SMEM, WHOLE],
        out_specs=(WHOLE,) * 2,
        compiler_params=params(48),
        cost_estimate=LIGHT,
    )(core, *in_hbm(array))


def join_kernel(steps, core, *refs):
    own, got, whole = refs[:steps], refs[steps : 2 * steps], refs[2 * steps]
    narrow = own[0].shape[1] // 3
    wide = 2 * narrow * steps

    def work(c):
        for kind in range(3):
            for d, arrays in ((c, own), (1 - c, got)):
                for i, ref in enumerate(arrays):
                    at = kind * wide + (d * steps + i) * narrow
                    whole[:, at : at + narrow] = ref[:, kind * narrow : (kind + 1) * narrow]

    on_core(core, work)


def join_heads(core, own, got):
    steps, (rows, wide) = len(own), own[0].shape
    return pl.pallas_call(
        functools.partial(join_kernel, steps),
        out_shape=shaped((rows, 2 * steps * wide), own[0].dtype),
        in_specs=[SMEM] + [WHOLE] * (2 * steps),
        out_specs=WHOLE,
        compiler_params=params(48),
        cost_estimate=LIGHT,
    )(core, *in_hbm(*own, *got))


def assemble(spots, pieces, matrix, sems):
    copies = []
    for i, piece in enumerate(pieces):
        rows = pl.ds(pl.multiple_of(spots[i], 16), piece.shape[0])
        copies.append(pltpu.make_async_copy(piece, matrix.at[rows], sems.at[i]))
    for copy in copies:
        copy.start()
    for copy in copies:
        copy.wait()


def norm_rows(value):
    centre = value - jnp.mean(value, axis=1, keepdims=True)
    scale = lax.rsqrt(jnp.mean(centre * centre, axis=1, keepdims=True) + 1e-06)
    return centre * scale, scale


def back_rows(grad, normed, scale):
    return scale * (
        grad - jnp.mean(grad, axis=1, keepdims=True) - normed * jnp.mean(grad * normed, axis=1, keepdims=True)
    )


def row_chunks(rows, step=128):
    return [slice(i, i + step) for i in range(0, rows, step)]


def project_kernel(number, core, spots, tokens, mods, offset, *refs):
    pieces = refs[:number]
    mine, away, moved, whole, matrix, made, sems, out_sem = refs[number:]
    width = made.shape[1]
    half = width // 2
    for at in row_chunks(tokens.shape[0]):
        normed, _ = norm_rows(tokens[at, :].astype(f32))
        moved[at, :] = (normed * (1.0 + mods[:, width : 2 * width]) + mods[:, :width]).astype(bf16)
    assemble(spots, pieces, matrix, sems)
    out = pltpu.make_async_copy(matrix, whole, out_sem)
    out.start()
    for kind in range(3):
        at = slice(kind * width, (kind + 1) * width)
        made[...] = (dot(moved[...], matrix[:, at]) + offset[:, at]).astype(bf16)

        def work(c):
            for ref, d in ((mine, c), (away, 1 - c)):
                ref[:, kind * half : (kind + 1) * half] = made[:, d * half : (d + 1) * half]

        on_core(core, work)
    out.wait()


def project(core, gathered, tokens, mods, offset):
    spots, pieces = gathered
    rows, width = tokens.shape
    wide = pieces[0].shape[1]
    return pl.pallas_call(
        functools.partial(project_kernel, len(pieces)),
        out_shape=(
            shaped((rows, wide // 2), bf16),
            shaped((rows, lanes(wide // 2)), bf16),
            shaped((rows, width), bf16),
            shaped((width, wide), bf16),
        ),
        in_specs=[SMEM, SMEM, WHOLE, WHOLE, WHOLE] + [HBM] * len(pieces),
        out_specs=(WHOLE, WHOLE, WHOLE, HBM),
        scratch_shapes=[
            pltpu.VMEM((width, wide), bf16),
            pltpu.VMEM((rows, width), bf16),
            pltpu.SemaphoreType.DMA((len(pieces),)),
            pltpu.SemaphoreType.DMA,
        ],
        compiler_params=params(48),
        cost_estimate=LIGHT,
    )(core, spots, *in_hbm(tokens, mods, offset, *pieces))


def middle_kernel(number, core, spots, own, got, tokens, mods, offset, *refs):
    pieces = refs[:number]
    attended, projected, normed, factor, moved, whole, matrix, sems, out_sem = refs[number:]
    assemble(spots, pieces, matrix, sems)
    out = pltpu.make_async_copy(matrix, whole, out_sem)
    out.start()
    width = matrix.shape[1]
    half = width // 2

    def work(c):
        attended[:, c * half : (c + 1) * half] = own[...]
        attended[:, (1 - c) * half : (2 - c) * half] = got[:, :half]

    on_core(core, work)
    gate1, shift2, scale2 = (mods[:, i * width : (i + 1) * width] for i in (2, 3, 4))
    projected[...] = dot(attended[...], matrix[...]) + offset[...]
    for at in row_chunks(own.shape[0]):
        made = projected[at, :]
        value = tokens[at, :].astype(f32) + gate1 * made
        value, scale = norm_rows(value)
        normed[at, :] = value
        factor[at, :] = scale
        moved[at, :] = (value * (1.0 + scale2) + shift2).astype(bf16)
    out.wait()


def middle_part(core, gathered, own, got, tokens, mods, offset):
    spots, pieces = gathered
    rows, width = tokens.shape
    return pl.pallas_call(
        functools.partial(middle_kernel, len(pieces)),
        out_shape=(
            shaped((rows, width), bf16),
            shaped((rows, width), f32),
            shaped((rows, width), f32),
            shaped((rows, 1), f32),
            shaped((rows, width), bf16),
            shaped((width, width), bf16),
        ),
        in_specs=[SMEM, SMEM] + [WHOLE] * 5 + [HBM] * len(pieces),
        out_specs=(WHOLE,) * 5 + (HBM,),
        scratch_shapes=[
            pltpu.VMEM((width, width), bf16),
            pltpu.SemaphoreType.DMA((len(pieces),)),
            pltpu.SemaphoreType.DMA,
        ],
        compiler_params=params(48),
        cost_estimate=LIGHT,
    )(core, spots, *in_hbm(own, got, tokens, mods, offset, *pieces))


def pair_grad_kernel(add_got, where, left, right, *refs):
    made = refs[-1]
    half = left.shape[1] // 2
    side = where[1]
    for d in range(2):

        @pl.when(side == d)
        def _():
            value = dot(left[:, d * half : (d + 1) * half], right[...], TN)
            if add_got:
                value = value + refs[0][0].astype(f32)
            made[0] = value.astype(bf16)


def pair_grad(left, right, b, side, got=None):
    rows, wide = left.shape
    step = wide // 4
    where = jnp.stack([b >> 1, side]).astype(jnp.int32)
    shape = (4, step // 2, right.shape[1])
    block = pl.BlockSpec((1,) + shape[1:], lambda m, where: (m, 0, 0))
    specs = [
        pl.BlockSpec((rows, step), lambda m, where: (0, where[0] ^ m)),
        pl.BlockSpec(right.shape, lambda m, where: (0, 0)),
    ]
    return pl.pallas_call(
        functools.partial(pair_grad_kernel, got is not None),
        out_shape=shaped(shape, bf16),
        grid_spec=pltpu.PrefetchScalarGridSpec(
            num_scalar_prefetch=1,
            grid=(4,),
            in_specs=specs + ([block] if got is not None else []),
            out_specs=block,
        ),
        compiler_params=params(48),
        cost_estimate=LIGHT,
    )(where, *in_hbm(left, right, *([got] if got is not None else [])))


def up_kernel(moved, matrix, offset, act, slope):
    for at in row_chunks(moved.shape[0], 256):
        u = dot(moved[at, :], matrix[...]) + offset[...]
        square = u * u
        t = jnp.tanh(ROOT * (u + 0.044715 * (square * u)))
        act[at, :] = (0.5 * u * (1.0 + t)).astype(bf16)
        slope[at, :] = 0.5 * (1.0 + t) + (0.5 * ROOT) * u * (1.0 - t * t) * (1.0 + (3 * 0.044715) * square)


def up_part(moved, matrix, offset):
    (rows, width), hidden = moved.shape, matrix.shape[1]
    step = hidden // 4
    return pl.pallas_call(
        up_kernel,
        out_shape=(shaped((rows, hidden), bf16), shaped((rows, hidden), f32)),
        grid=(4,),
        in_specs=[WHOLE, pl.BlockSpec((width, step), lambda i: (0, i)), pl.BlockSpec((1, step), lambda i: (0, i))],
        out_specs=(pl.BlockSpec((rows, step), lambda i: (0, i)), pl.BlockSpec((rows, step), lambda i: (0, i))),
        compiler_params=params(48),
        cost_estimate=LIGHT,
    )(*in_hbm(moved, matrix, offset))


def slope_kernel(grad, matrix, slope, d_upper, sums):
    total = jnp.zeros(sums.shape, f32)
    for at in row_chunks(grad.shape[0], 256):
        value = (dot(grad[at, :], matrix[...], NT) * slope[at, :]).astype(bf16)
        d_upper[at, :] = value
        total = total + jnp.sum(value.astype(f32), axis=0, keepdims=True)
    sums[...] = total


def slope_part(grad, matrix, slope):
    (rows, width), hidden = grad.shape, matrix.shape[0]
    step = hidden // 4
    across = pl.BlockSpec((rows, step), lambda i: (0, i))
    return pl.pallas_call(
        slope_kernel,
        out_shape=(shaped((rows, hidden), bf16), shaped((1, hidden), f32)),
        grid=(4,),
        in_specs=[WHOLE, pl.BlockSpec((step, width), lambda i: (i, 0)), across],
        out_specs=(across, pl.BlockSpec((1, step), lambda i: (0, i))),
        compiler_params=params(48),
        cost_estimate=LIGHT,
    )(*in_hbm(grad, matrix, slope))


def down_kernel(act, matrix, offset, tokens, projected, mods, grad, output, d_gate, total):
    step = pl.program_id(0)
    width = matrix.shape[1]

    @pl.when(step == 0)
    def _():
        total[...] = dot(act[...], matrix[...])

    @pl.when(step > 0)
    def _():
        total[...] += dot(act[...], matrix[...])

    @pl.when(step == pl.num_programs(0) - 1)
    def _():
        gate1, gate2 = mods[:, 2 * width : 3 * width], mods[:, 5 * width :]
        summed = jnp.zeros(d_gate.shape, f32)
        for at in row_chunks(act.shape[0]):
            lowered = total[at, :] + offset[...]
            middle = tokens[at, :].astype(f32) + gate1 * projected[at, :]
            output[at, :] = (middle + gate2 * lowered).astype(bf16)
            summed = summed + jnp.sum(grad[at, :].astype(f32) * lowered, axis=0, keepdims=True)
        d_gate[...] = summed


def down_part(act, matrix, offset, tokens, projected, mods, grad):
    rows, hidden = act.shape
    step, width = hidden // 4, matrix.shape[1]
    return pl.pallas_call(
        down_kernel,
        out_shape=(shaped((rows, width), bf16), shaped((1, width), f32)),
        grid=(4,),
        in_specs=[pl.BlockSpec((rows, step), lambda i: (0, i)), pl.BlockSpec((step, width), lambda i: (i, 0))]
        + [WHOLE] * 5,
        out_specs=(WHOLE, WHOLE),
        scratch_shapes=[pltpu.VMEM((rows, width), f32)],
        compiler_params=params(48),
        cost_estimate=LIGHT,
    )(*in_hbm(act, matrix, offset, tokens, projected, mods, grad))


def middle_back_kernel(core, d_upper, matrix, normed, factor, projected, grad, mods, out_matrix, d_middle, d_projected, mine, away, sums, total):
    step = pl.program_id(0)
    width = matrix.shape[0]
    half = width // 2

    @pl.when(step == 0)
    def _():
        total[...] = dot(d_upper[...], matrix[...], NT)

    @pl.when(step > 0)
    def _():
        total[...] += dot(d_upper[...], matrix[...], NT)

    @pl.when(step == pl.num_programs(0) - 1)
    def _():
        gate1, scale2 = mods[:, 2 * width : 3 * width], mods[:, 4 * width : 5 * width]
        summed = [jnp.zeros((1, width), f32) for _ in range(4)]
        for at in row_chunks(grad.shape[0]):
            d_moved, n = total[at, :], normed[at, :]
            value = grad[at, :].astype(f32) + back_rows(d_moved * (1.0 + scale2), n, factor[at, :])
            d_middle[at, :] = value
            d_proj = (gate1 * value).astype(bf16)
            d_projected[at, :] = d_proj
            terms = d_moved, d_moved * n, value * projected[at, :], d_proj.astype(f32)
            summed = [u + jnp.sum(v, axis=0, keepdims=True) for u, v in zip(summed, terms)]
        total[...] = dot(d_projected[...], out_matrix[...], NT)

        def work(c):
            mine[...] = total[:, c * half : (c + 1) * half].astype(bf16)
            away[:, :half] = total[:, (1 - c) * half : (2 - c) * half].astype(bf16)

        on_core(core, work)
        for i, value in enumerate(summed):
            sums[i : i + 1, :] = value


def middle_back(core, d_upper, matrix, normed, factor, projected, grad, mods, out_matrix):
    rows, hidden = d_upper.shape
    step, width = hidden // 4, matrix.shape[0]
    return pl.pallas_call(
        middle_back_kernel,
        out_shape=(
            shaped((rows, width), f32),
            shaped((rows, width), bf16),
            shaped((rows, width // 2), bf16),
            shaped((rows, lanes(width // 2)), bf16),
            shaped((4, width), f32),
        ),
        grid=(4,),
        in_specs=[SMEM, pl.BlockSpec((rows, step), lambda i: (0, i)), pl.BlockSpec((width, step), lambda i: (0, i))]
        + [WHOLE] * 6,
        out_specs=(WHOLE,) * 5,
        scratch_shapes=[pltpu.VMEM((rows, width), f32)],
        compiler_params=params(48),
        cost_estimate=LIGHT,
    )(core, *in_hbm(d_upper, matrix, normed, factor, projected, grad, mods, out_matrix))


def input_back_kernel(d_qkv, matrix, tokens, mods, d_middle, input_grad, sums, columns, total):
    step = pl.program_id(0)
    width = matrix.shape[0]
    columns[...] = jnp.sum(d_qkv[...].astype(f32), axis=0, keepdims=True)

    @pl.when(step == 0)
    def _():
        total[...] = dot(d_qkv[...], matrix[...], NT)

    @pl.when(step > 0)
    def _():
        total[...] += dot(d_qkv[...], matrix[...], NT)

    @pl.when(step == pl.num_programs(0) - 1)
    def _():
        scale1 = mods[:, width : 2 * width]
        summed = [jnp.zeros((1, width), f32) for _ in range(2)]
        for at in row_chunks(tokens.shape[0]):
            normed, factor = norm_rows(tokens[at, :].astype(f32))
            d_moved = total[at, :]
            input_grad[at, :] = (d_middle[at, :] + back_rows(d_moved * (1.0 + scale1), normed, factor)).astype(bf16)
            summed = [u + jnp.sum(v, axis=0, keepdims=True) for u, v in zip(summed, (d_moved, d_moved * normed))]
        for i, value in enumerate(summed):
            sums[i : i + 1, :] = value


def input_back(d_qkv, matrix, tokens, mods, d_middle):
    rows, wide = d_qkv.shape
    width = matrix.shape[0]
    return pl.pallas_call(
        input_back_kernel,
        out_shape=(shaped((rows, width), bf16), shaped((2, width), f32), shaped((1, wide), f32)),
        grid=(wide // width,),
        in_specs=[pl.BlockSpec((rows, width), lambda i: (0, i)), pl.BlockSpec((width, width), lambda i: (0, i))]
        + [WHOLE] * 3,
        out_specs=(WHOLE, WHOLE, pl.BlockSpec((1, width), lambda i: (0, i))),
        scratch_shapes=[pltpu.VMEM((rows, width), f32)],
        compiler_params=params(48),
        cost_estimate=LIGHT,
    )(*in_hbm(d_qkv, matrix, tokens, mods, d_middle))


def block_grad_kernel(add_got, spots, left, right, *refs):
    made, chosen, turned = refs[-3:]
    rows = made.shape[1]

    @pl.when(pl.program_id(0) == 0)
    def _():
        turned[...] = jnp.transpose(left[...])
        for e in range(4):
            at = pl.ds(pl.multiple_of(spots[e], 16), rows)
            chosen[e * rows : (e + 1) * rows, :] = turned[at, :]

    value = dot(chosen[...], right[...])
    for e in range(4):
        part = value[e * rows : (e + 1) * rows, :]
        if add_got:
            part = part + refs[0][e].astype(f32)
        made[e] = part.astype(bf16)


def block_grad(left, right, b, side, got=None):
    (slots, wide), columns = left.shape, right.shape[1]
    rows = wide // 8
    spots = jnp.stack([((b >> 1) ^ m) * 2 * rows + side * rows for m in range(4)]).astype(jnp.int32)
    step = 1152 if columns % 1152 == 0 else columns
    block = pl.BlockSpec((4, rows, step), lambda i: (0, 0, i))
    return pl.pallas_call(
        functools.partial(block_grad_kernel, got is not None),
        out_shape=shaped((4, rows, columns), bf16),
        grid=(columns // step,),
        in_specs=[SMEM, WHOLE, pl.BlockSpec((slots, step), lambda i: (0, i))] + ([block] if got is not None else []),
        out_specs=block,
        scratch_shapes=[pltpu.VMEM((4 * rows, slots), bf16), pltpu.VMEM((wide, slots), bf16)],
        compiler_params=params(48),
        cost_estimate=LIGHT,
    )(spots, *in_hbm(left, right, *([got] if got is not None else [])))


def fill(h, heads, mine, theirs, qs, ks, vs):
    half, wide, lo = mine.shape[0], heads * HEAD, h * HEAD
    for part, ref in ((0, mine), (1, theirs)):
        rows = slice(part * half, (part + 1) * half)
        qs[rows, :HEAD] = ref[:, lo : lo + HEAD]
        ks[rows, :HEAD] = ref[:, wide + lo : wide + lo + HEAD]
        vs[rows, :] = ref[:, 2 * wide + lo : 2 * wide + lo + HEAD]


def mark_valid(limits, qs, ks):
    total = qs.shape[0]
    chunks = limits.shape[0]
    sub = lax.broadcasted_iota(jnp.int32, (total // chunks, 1), 0)
    bias = jnp.concatenate([jnp.where(sub < limits[i], 0.0, -1e30) for i in range(chunks)], axis=0)
    qs[...] = jnp.zeros_like(qs)
    ks[...] = jnp.zeros_like(ks)
    qs[:, HEAD : HEAD + 1] = jnp.ones((total, 1), bf16)
    ks[:, HEAD : HEAD + 1] = bias.astype(bf16)


def attend_kernel(heads, limits, mine, theirs, out_mine, out_theirs, lse, qs, ks, vs, os, ls):
    half = mine.shape[0]
    total = 2 * half
    mark_valid(limits, qs, ks)
    for h in range(heads):
        fill(h, heads, mine, theirs, qs, ks, vs)
        for i in range(total // BLOCK):
            at = slice(i * BLOCK, (i + 1) * BLOCK)
            scores = dot(qs[at, :], ks[...], NT) * (SCALE * LOG2E)
            peak = jnp.max(scores, axis=1, keepdims=True)
            expo = jnp.exp2(scores - peak)
            summed = jnp.sum(expo, axis=1, keepdims=True)
            probs = (expo * (1.0 / summed)).astype(bf16)
            os[at, :] = dot(probs, vs[...]).astype(bf16)
            ls[at, :] = peak + jnp.log2(summed)
        lo = h * HEAD
        out_mine[:, lo : lo + HEAD] = os[:half, :]
        out_theirs[:, lo : lo + HEAD] = os[half:, :]
        lse[h : h + 1, :] = jnp.transpose(ls[...])


def attend(limits, mine, theirs):
    half, wide3 = mine.shape
    wide = wide3 // 3
    heads = wide // HEAD
    total = 2 * half
    return pl.pallas_call(
        functools.partial(attend_kernel, heads),
        out_shape=(shaped((half, wide), bf16), shaped((half, lanes(wide)), bf16), shaped((heads, total), f32)),
        in_specs=[SMEM, WHOLE, WHOLE],
        out_specs=(WHOLE,) * 3,
        scratch_shapes=[
            pltpu.VMEM((total, PAD), bf16),
            pltpu.VMEM((total, PAD), bf16),
            pltpu.VMEM((total, HEAD), bf16),
            pltpu.VMEM((total, HEAD), bf16),
            pltpu.VMEM((total, 1), f32),
        ],
        compiler_params=params(VMEM_ATT),
        cost_estimate=LIGHT,
    )(limits, *in_hbm(mine, theirs))


def back_kernel(heads, first, number, limits, mine, theirs, d_mine, d_theirs, lse, out_mine, out_theirs, qs, ks, vs, ds, dq, dk, dv):
    half = mine.shape[0]
    total = 2 * half
    narrow = number * HEAD
    mark_valid(limits, qs, ks)
    for h in range(first, first + number):
        fill(h, heads, mine, theirs, qs, ks, vs)
        lo = h * HEAD
        ds[:half, :] = d_mine[:, lo : lo + HEAD]
        ds[half:, :] = d_theirs[:, lo : lo + HEAD]
        for i in range(total // BLOCK):
            at = slice(i * BLOCK, (i + 1) * BLOCK)
            query, d_out = qs[at, :], ds[at, :]
            exact = jnp.exp2(dot(ks[...], query, NT) * (SCALE * LOG2E) - lse[h : h + 1, at])
            d_probs = dot(vs[...], d_out, NT)
            more = dot(exact.astype(bf16), d_out)
            dv[...] = more if i == 0 else dv[...] + more
            product = exact * d_probs
            centred = jnp.sum(product, axis=0, keepdims=True)
            d_scores = (product - exact * centred).astype(bf16)
            more = dot(d_scores, query)
            dk[...] = more if i == 0 else dk[...] + more
            dq[at, :] = (dot(d_scores, ks[...], TN) * SCALE).astype(bf16)
        lo = (h - first) * HEAD
        for part, ref in ((0, out_mine), (1, out_theirs)):
            rows = slice(part * half, (part + 1) * half)
            ref[:, lo : lo + HEAD] = dq[rows, :HEAD]
            ref[:, narrow + lo : narrow + lo + HEAD] = (dk[rows, :HEAD] * SCALE).astype(bf16)
            ref[:, 2 * narrow + lo : 2 * narrow + lo + HEAD] = dv[rows, :].astype(bf16)


def attend_back(limits, mine, theirs, d_mine, d_theirs, lse, first, number):
    half, wide3 = mine.shape
    wide = wide3 // 3
    heads = wide // HEAD
    total = 2 * half
    return pl.pallas_call(
        functools.partial(back_kernel, heads, first, number),
        out_shape=(shaped((half, 3 * number * HEAD), bf16), shaped((half, lanes(3 * number * HEAD)), bf16)),
        in_specs=[SMEM] + [WHOLE] * 5,
        out_specs=(WHOLE,) * 2,
        scratch_shapes=[
            pltpu.VMEM((total, PAD), bf16),
            pltpu.VMEM((total, PAD), bf16),
            pltpu.VMEM((total, HEAD), bf16),
            pltpu.VMEM((total, HEAD), bf16),
            pltpu.VMEM((total, PAD), bf16),
            pltpu.VMEM((total, PAD), f32),
            pltpu.VMEM((total, HEAD), f32),
        ],
        compiler_params=params(VMEM_ATT),
        cost_estimate=LIGHT,
    )(limits, *in_hbm(mine, theirs, d_mine, d_theirs, lse))


def pair_swap(array):
    size = lax.axis_size("batch")
    return lax.ppermute(array, "batch", [(i, i ^ 1) for i in range(size)])


def deal_pairs(turn, back=False):
    pairs = []
    seq = lax.axis_size("seq")
    for b in range(lax.axis_size("batch")):
        for s in range(seq):
            j = (s ^ turn) & 1
            dc = ((s >> 1) ^ (turn >> 1)) & 1
            here, there = b * seq + s, (b ^ dc) * seq + 2 * (b & 1) + j
            pairs.append((there, here) if back else (here, there))
    return pairs


def place_of(turn):
    b, s = lax.axis_index("batch"), lax.axis_index("seq")
    j = (s ^ turn) & 1
    half = (b ^ (s >> 1) ^ (turn >> 1)) & 1
    return j, half


def deal(array):
    half = array.shape[1] // 2
    parts = []
    for turn in range(4):
        j, c = place_of(turn)
        piece = lax.dynamic_slice(array, (j, c * half, 0), (1, half, array.shape[2]))[0]
        parts.append(lax.ppermute(piece, ("batch", "seq"), deal_pairs(turn)))
    return jnp.concatenate(parts, axis=0)


def undeal(array):
    half = array.shape[0] // 4
    out = jnp.zeros((2, 2 * half, array.shape[1]), array.dtype)
    for turn in range(4):
        got = lax.ppermute(array[turn * half : (turn + 1) * half], ("batch", "seq"), deal_pairs(turn, True))
        j, c = place_of(turn)
        out = lax.dynamic_update_slice(out, got[None], (j, c * half, 0))
    return out


def norm_forward(values):
    centre = values - jnp.mean(values, axis=-1, keepdims=True)
    factor = lax.rsqrt(jnp.mean(centre * centre, axis=-1, keepdims=True) + 1e-06)
    return centre * factor, factor


def norm_back(grad, normed, factor):
    return factor * (
        grad
        - jnp.mean(grad, axis=-1, keepdims=True)
        - normed * jnp.mean(grad * normed, axis=-1, keepdims=True)
    )


def gather(array):
    return lax.all_gather(array, "batch", axis=0, tiled=True)


def hop(array, bits):
    size = lax.axis_size("batch")
    return lax.ppermute(array, "batch", [(i, i ^ bits) for i in range(size)])


class Hops:
    def __init__(self, array):
        self.array = array
        self.plain = lax.axis_size("batch") != 8
        if self.plain:
            self.whole = gather(array)
            self.moving = (self.whole,)
        else:
            self.moving = self.along_x, self.along_y = hop(array, 2), hop(array, 4)

    def pieces(self, *done):
        if self.plain:
            return jnp.zeros((1,), jnp.int32), [self.whole]
        rows = self.array.shape[0]
        cut = rows // 2 // 16 * 16
        b = lax.axis_index("batch")
        along_x, along_y = after((self.along_x, self.along_y), *done)
        corner = hop(along_x[:cut], 4), hop(along_y[cut:], 2)
        self.moving = along_x, along_y, *corner
        pieces = [(0, 0, self.array), (2, 0, along_x), (4, 0, along_y), (6, 0, corner[0]), (6, cut, corner[1])]
        pieces += [(bits ^ 1, at, hop(piece, 1)) for bits, at, piece in pieces]
        spots = jnp.stack([(b ^ bits) * rows + at for bits, at, _ in pieces]).astype(jnp.int32)
        return spots, [piece for _, _, piece in pieces]


def after(value, *done):
    return lax.optimization_barrier((value, done))[0]


def add(u, v):
    return (u.astype(f32) + v.astype(f32)).astype(bf16)


class Grad:
    def __init__(self, left, right, paired=False):
        self.left, self.right, self.paired = left, right, paired
        self.rows = left.shape[1] // lax.axis_size("batch")
        self.plain = lax.axis_size("batch") != 8 or lax.axis_size("seq") != 4

    def away(self, *done):
        if self.plain:
            made = self.made = dot(after(self.left, *done), self.right, TN).astype(bf16)
            return made
        self.left = after(self.left, *done)
        b = lax.axis_index("batch")
        made = (pair_grad if self.paired else block_grad)(self.left, self.right, b, 1 - (b & 1))
        self.got = hop(made, 1)
        return made

    def stay(self, *done):
        if self.plain:
            part = lax.psum_scatter(self.made, "batch", scatter_dimension=0, tiled=True)
            self.part = lax.psum(part, "seq")
            return self.part
        self.left = after(self.left, *done)
        b = lax.axis_index("batch")
        made = (pair_grad if self.paired else block_grad)(self.left, self.right, b, b & 1, self.got)
        both = made.reshape(4 * self.rows, -1)
        rows, cut = self.rows, self.rows // 2 // 8 * 8
        self.own, self.to_x, self.to_y, corner = (both[i * rows : (i + 1) * rows] for i in range(4))
        self.cut = cut
        self.got_x, self.got_y = hop(corner[:cut], 2), hop(corner[cut:], 4)
        return made

    def mix(self, *done):
        if self.plain:
            return self.part
        cut = self.cut
        to_x, to_y = after((self.to_x, self.to_y), *done)
        to_y = jnp.concatenate([add(to_y[:cut], self.got_x), to_y[cut:]], axis=0)
        to_x = jnp.concatenate([to_x[:cut], add(to_x[cut:], self.got_y)], axis=0)
        self.got_x, self.got_y = hop(to_x, 2), hop(to_y, 4)
        return to_x, to_y

    def finish(self, *done, extra=None):
        if self.plain:
            return (self.land(extra=extra),) * 2
        own = after(self.own, *done)
        part = (own.astype(f32) + self.got_x.astype(f32) + self.got_y.astype(f32)).astype(bf16)
        if extra is not None:
            part = jnp.concatenate([part, extra.astype(bf16)], axis=0)
        total = lax.psum(part, "seq")
        self.part, self.plain = total[: self.rows], True
        if extra is not None:
            self.extra = total[self.rows :].astype(f32)
        return part, total

    def land(self, *done, extra=None, chunks=1):
        if self.plain:
            if extra is not None:
                self.extra = lax.psum(extra, "seq")
            return self.part
        own = after(self.own, *done)
        part = (own.astype(f32) + self.got_x.astype(f32) + self.got_y.astype(f32)).astype(bf16)
        if extra is not None:
            part = jnp.concatenate([part, extra.astype(bf16)], axis=0)
        step = -(-part.shape[0] // chunks // 8) * 8
        self.parts = [part[i * step : (i + 1) * step] for i in range(chunks)]
        self.gots = [lax.ppermute(part, "seq", [(0, 1), (3, 2)]) for part in self.parts]
        return part

    def pass_on(self, pairs, done):
        if self.plain:
            return self.part
        parts = after(tuple(self.parts), *done)
        self.parts, gots = [], self.gots
        self.gots = []
        for part, got in zip(parts, gots):
            part = add(part, got)
            self.parts.append(part)
            self.gots.append(lax.ppermute(part, "seq", pairs))
        return tuple(self.parts)

    def across(self, *done):
        return self.pass_on([(1, 2), (2, 1)], done)

    def outward(self, *done):
        return self.pass_on([(1, 0), (2, 3)], done)

    def result(self, *done):
        if self.plain:
            part = after(self.part, *done).astype(f32)
            return part if not hasattr(self, "extra") else (part, self.extra)
        s = lax.axis_index("seq")
        ends = (s == 0) | (s == 3)
        parts = after(tuple(self.parts), *done)
        total = [jnp.where(ends, got, part).astype(f32) for part, got in zip(parts, self.gots)]
        total = total[0] if len(total) == 1 else jnp.concatenate(total, axis=0)
        if total.shape[0] > self.rows:
            return total[: self.rows], total[self.rows :]
        return total


def all_samples(row):
    rows = row[None]
    for bit in (1, 2):
        rows = jnp.concatenate([rows, lax.ppermute(rows, "seq", [(i, i ^ bit) for i in range(4)])], axis=0)
    bits = 2
    while bits < lax.axis_size("batch"):
        rows = jnp.concatenate([rows, hop(rows, bits)], axis=0)
        bits *= 2
    return rows


def xor_order(array, index):
    size, bit = array.shape[0], 1
    while bit < size:
        split = array.reshape((size // (2 * bit), 2, bit) + array.shape[1:])
        array = jnp.where((index & bit) != 0, split[:, ::-1], split).reshape(array.shape)
        bit *= 2
    return array


def body(
    inputs,
    conds,
    heights,
    widths,
    qkv_weight,
    qv_bias,
    out_weight,
    out_bias,
    up_weight,
    up_bias,
    down_weight,
    down_bias,
    mod_weight,
    mod_bias,
    cotangent,
):
    devices = lax.axis_size("batch")
    b, s = lax.axis_index("batch"), lax.axis_index("seq")
    c = b & 1
    width = inputs.shape[2]
    hidden = up_weight.shape[1]
    slot_dev = inputs.shape[1]
    half = slot_dev // 2
    rows = qkv_weight.shape[0]
    mods = mod_weight.shape[1]

    tokens16 = deal(inputs)
    upstream16 = deal(cotangent)

    core = jnp.reshape(c, (1,)).astype(jnp.int32)
    qkv_hops = Hops(qkv_weight)

    small = [conds.reshape(-1), qv_bias, out_bias, up_bias, down_bias, heights.astype(bf16), widths.astype(bf16)]
    spots = [sum(e.size for e in small[:i]) for i in range(len(small) + 1)]
    small.append(jnp.zeros((-spots[-1] % 128,), bf16))
    small = gather(jnp.concatenate(small)[None])
    every = [small[:, spots[i] : spots[i + 1]] for i in range(7)]
    cond_all = every[0].reshape(2 * devices, width)
    qv_offset, out_offset, up_offset, down_offset = (e.reshape(-1).astype(f32) for e in every[1:5])
    counts = (every[5].astype(jnp.int32) * every[6].astype(jnp.int32)).reshape(2 * devices)
    sample = 4 * (b // 2) + s
    count = lax.dynamic_index_in_dim(counts, sample, keepdims=False)

    silu_all = jax.nn.silu(cond_all.astype(f32)).astype(bf16)
    silu_rows = lax.dynamic_slice(silu_all, (0, b * rows), (2 * devices, rows))
    plane = lax.dynamic_index_in_dim(silu_rows.reshape(devices // 2, 4, rows), s, axis=1, keepdims=False)
    partial = dot(plane, mod_weight)
    qkv_pieces = qkv_hops.pieces(partial, tokens16)
    out_pieces = Hops(after(out_weight, qkv_hops.moving)).pieces()
    up_matrix = gather(after(up_weight, qkv_hops.moving))
    own_bias = lax.dynamic_update_slice(jnp.zeros((mods,), f32), mod_bias.astype(f32), (b * mod_bias.shape[0],))
    partial = partial + own_bias[None]
    partial = jnp.broadcast_to(partial[:, None], (devices // 2, 2, mods)).reshape(devices, mods)
    modulation = jnp.sum(lax.all_to_all(partial, "batch", 0, 0, tiled=True), axis=0, keepdims=True)
    shift1, scale1, gate1, shift2, scale2, gate2 = jnp.split(modulation, 6, axis=-1)

    limits = []
    for part in range(2):
        side = c ^ part
        base = (s & 1) | (((s >> 1) ^ side) << 1)
        for turn in range(4):
            limits.append(count - (slot_dev * (base ^ turn) + half * side))
    limits = jnp.stack(limits).astype(jnp.int32)

    offsets = jnp.concatenate([qv_offset[:width], jnp.zeros((width,), f32), qv_offset[width:]])
    mine, away, moved, qkv_matrix = project(core, qkv_pieces, tokens16, modulation, offsets[None])
    theirs = pair_swap(away)
    down_matrix = gather(after(down_weight, mine))
    att_mine, att_away, lse = attend(limits, mine, theirs)
    att_mine = after(att_mine, upstream16)
    attended, projected, normed2, factor2, moved2, out_matrix = middle_part(
        core, out_pieces, att_mine, pair_swap(att_away), tokens16, modulation, out_offset[None]
    )
    act, slope = up_part(moved2, up_matrix, up_offset[None])

    d_lowered = (gate2 * upstream16.astype(f32)).astype(bf16)
    down_offset_grad = jnp.sum(d_lowered.astype(f32), axis=0)
    down_g = Grad(act, d_lowered, True)
    mark = down_g.away(act)
    d_upper, up_sums = slope_part(after(d_lowered, mark), down_matrix, slope)
    mark = down_g.stay(d_upper)
    up_g = Grad(moved2, d_upper)
    mark = up_g.away(mark)
    mark = down_g.mix(mark)
    d_middle, d_projected, d_att_mine, d_att_away, sums2 = middle_back(
        core, after(d_upper, mark), up_matrix, normed2, factor2, projected, upstream16, modulation, out_matrix
    )
    d_shift2, d_scale2, d_gate1, out_offset_grad = sums2
    d_att_theirs = pair_swap(d_att_away)
    mark = up_g.stay(d_att_mine)
    out_g = Grad(attended, d_projected)
    mark = out_g.away(mark)
    mark = out_g.stay(mark)
    mark, down_total = down_g.finish(mark)
    mark = up_g.mix(mark)
    heads = HEADS // 2
    steps = 2
    own, got = [], []
    for i in range(steps):
        made = attend_back(
            limits, after(mine, mark), theirs, d_att_mine, d_att_theirs, lse, i * heads // steps, heads // steps
        )
        own.append(made[0])
        got.append(pair_swap(made[1]))
        mark = made
    mark = out_g.mix(mark)
    up_part_sum, up_total = up_g.finish(mark, down_total)
    mark = up_part_sum
    d_qkv = join_heads(core, own, got)
    qkv_g = Grad(moved, d_qkv)
    mark = qkv_g.away(mark)
    mark, out_total = out_g.finish(mark, down_total)
    input_grad, sums1, column_sums = input_back(after(d_qkv, mark), qkv_matrix, tokens16, modulation, d_middle)
    d_shift1, d_scale1 = sums1
    mark = qkv_g.stay(input_grad)
    input_grad = undeal(after(input_grad, mark)).astype(f32)
    column_sums = after(column_sums[0], mark)
    qv_offset_grad = jnp.concatenate([column_sums[:width], column_sums[2 * width :]])
    own_shapes = (qv_bias.shape[0], out_bias.shape[0], up_bias.shape[0], down_bias.shape[0])
    bias = jnp.concatenate(
        [
            g.reshape(devices, -1)
            for g in (qv_offset_grad, out_offset_grad, up_sums, down_offset_grad)
        ],
        axis=1,
    )
    length = bias.shape[1]
    bias = jnp.sum(lax.all_to_all(bias, "batch", 0, 0, tiled=True), axis=0, keepdims=True)
    bias = jnp.pad(bias, ((0, 7), (0, 3 * width - length)))
    output, d_gate2 = down_part(
        after(act, mark), down_matrix, down_offset[None], tokens16, projected, modulation, upstream16
    )
    mark = qkv_g.mix(output)
    output = undeal(after(output, mark))
    mark, qkv_total = qkv_g.finish(mark, up_total, out_total, extra=bias)

    partial_mod = jnp.concatenate([d_shift1, d_scale1, d_gate1, d_shift2, d_scale2, d_gate2[0]])
    partial_mod = after(partial_mod, mark)
    d_mod = (partial_mod + pair_swap(partial_mod)).astype(bf16)
    d_mod_all = all_samples(d_mod)
    mod_grad = dot(xor_order(silu_rows, sample), d_mod_all, TN)
    mod_offset_grad = jnp.sum(
        lax.dynamic_slice(d_mod_all, (0, b * mod_bias.shape[0]), (2 * devices, mod_bias.shape[0])).astype(f32), axis=0
    )
    d_silu_rows = xor_order(dot(d_mod_all, mod_weight, NT), sample)
    d_silu = lax.all_to_all(d_silu_rows.reshape(devices, 2 * rows), "batch", 0, 0, tiled=True)
    d_silu = d_silu.reshape(devices, 2, rows).transpose(1, 0, 2).reshape(2, width)
    cond_grad = jax.vjp(jax.nn.silu, conds.astype(f32))[1](d_silu)[0]

    down_grad, up_grad, out_grad = (grad.result(d_mod_all) for grad in (down_g, up_g, out_g))
    qkv_grad, bias = qkv_g.result()
    bias = bias[0, :length]
    cuts = [sum(own_shapes[:i]) for i in range(5)]
    qv_b, out_b, up_b, down_b = (bias[cuts[i] : cuts[i + 1]] for i in range(4))
    return (
        output,
        input_grad,
        cond_grad,
        qkv_grad,
        qv_b,
        out_grad,
        out_b,
        up_grad,
        up_b,
        down_grad,
        down_b,
        mod_grad,
        mod_offset_grad,
    )


def solution(mesh):
    in_specs = (
        P("batch", "seq", None),
        P("batch", None),
        P("batch"),
        P("batch"),
        P("batch", None),
        P("batch"),
        P("batch", None),
        P("batch"),
        P("batch", None),
        P("batch"),
        P("batch", None),
        P("batch"),
        P("batch", None),
        P("batch"),
        P("batch", "seq", None),
    )
    out_specs = (
        P("batch", "seq", None),
        P("batch", "seq", None),
        P("batch", None),
        P("batch", None),
        P("batch"),
        P("batch", None),
        P("batch"),
        P("batch", None),
        P("batch"),
        P("batch", None),
        P("batch"),
        P("batch", None),
        P("batch"),
    )
    return jax.shard_map(body, mesh=mesh, in_specs=in_specs, out_specs=out_specs, check_vma=False)
```

time: 868 us -> 614 us (0.71)
  waiting for transfers between devices: 359 us -> 137 us
  Pallas kernels: 79 us -> 224 us
  matrix products: 130 us -> 3.6 us
  blocking collectives: 120 us -> 16.5 us
  starting transfers between devices: 44.3 us -> 105 us
  local copies, waits for them, and re-layouts: 85.5 us -> 60.8 us
  other arithmetic: 24.6 us -> 36.3 us
    pallas_call x2 -> x19, Pallas kernels: 79 us -> 224 us  [the longest x6 40.4 us: block_grad(): pl.pallas_call(functools.partial(block_grad_kernel, got is not None), out...]
    dot_general x15 -> x3, matrix products: 130 us -> 3.6 us  [dot(): return lax.dot_general(a, b, dims, preferred_element_type=f32)]
    reduce_scatter x4 -> x0, waiting for transfers between devices: 123 us -> none  [scatter_sum(): lax.psum_scatter(array.astype(bf16), 'batch', scatter_dimension=0, tiled=...]
    all_gather x4 -> x2, waiting for transfers between devices: 104 us -> 9.46 us  [gather(): return lax.all_gather(array, 'batch', axis=0, tiled=True)]
    ppermute x0 -> x42, waiting for transfers between devices: none -> 80.9 us  [the longest x40 64.7 us: hop(): return lax.ppermute(array, 'batch', [(i, i ^ bits) for i in range(size)])]
    all_gather x3 -> x1, blocking collectives: 82.6 us -> 16.5 us  [gather(): return lax.all_gather(array, 'batch', axis=0, tiled=True)]
    psum x1 -> x3, waiting for transfers between devices: 76.7 us -> 33.1 us  [finish(): total = lax.psum(part, 'seq')]
    unnamed x11 -> x5, waiting for transfers between devices: 43.6 us -> 0.08 us
  transfers between devices with their start and end apart: 33 -> 72, of which waited for: 11 -> 21; matrix products, arithmetic and copies ran while one was open for 19% -> 14% of each run, Pallas kernels for 9% -> 33%
where the time goes in v2:
time: 614 us; the launch traced here: 603 us
  Pallas kernels  224 us (36%)
  waiting for transfers between devices  137 us (22%)
  starting transfers between devices  105 us (17%)
  local copies, waits for them, and re-layouts  60.8 us (10%)
  other arithmetic  36.3 us (6%)
  between operations  20.6 us (3%)
  blocking collectives  16.5 us (3%)
    ppermute x40, waiting for transfers between devices, hop(): return lax.ppermute(array, 'batch', [(i, i ^ bits) for i in range(size)])  64.7 us
    pallas_call x6, Pallas kernels, block_grad(): pl.pallas_call(functools.partial(block_grad_kernel, got is not None), out...  40.4 us
    ppermute x40, starting transfers between devices, hop(): return lax.ppermute(array, 'batch', [(i, i ^ bits) for i in range(size)])  36.4 us
    ppermute x8, starting transfers between devices, undeal(): lax.ppermute(array[turn * half:(turn + 1) * half], ('batch', 'seq'), deal...  36.2 us
    pallas_call x2, Pallas kernels, attend_back(): pl.pallas_call(functools.partial(back_kernel, heads, first, number), out_...  34 us
    psum x3, waiting for transfers between devices, finish(): total = lax.psum(part, 'seq')  33.1 us
    pallas_call x1, Pallas kernels, attend(): pl.pallas_call(functools.partial(attend_kernel, heads), out_shape=(shaped...  27.2 us
    pallas_call x1, Pallas kernels, middle_back(): pl.pallas_call(middle_back_kernel, out_shape=(shaped((rows, width), f32),...  19.1 us
  transfers between devices with their start and end apart: 72, of which 21 were waited for; matrix products, arithmetic and copies ran while one was open for 14% of the time, Pallas kernels for 33%

profile of v2, /device:TPU:0, one launch (start us, length us, event | category | flops | bytes accessed | tf_op | source)
XLA Modules:
  0.0 603.3 jit_solution(13477243063745400516)
XLA Ops:
  7.3 3.0 collective-permute-start.4
  11.8 2.2 dynamic-slice_bitcast_fusion.4
  16.3 5.4 collective-permute-start.2
  21.9 16.5 %all-gather.1 = bf16[8,1,3584]{2,1,0:T(2,128)(2,1)S(1)} all-gather(bf16[1,1,3584]{2,1,0:T(2,128)(2,1)S(1)} %reshape.186), channel_id=2, replica_groups=mesh['batch'=8,'seq'=4] {'batch'}, dimensions={0}, use_global_device_ids=true | all-gather | bytes 64512 | tf_op jit(solution)/shard_map/all_gather | solution.py:669
  44.5 7.0 %collective-permute-done.3 = bf16[128,1152]{1,0:T(8,128)(2,1)S(1)} collective-permute-done((bf16[128,1152]{1,0:T(8,128)(2,1)}, bf16[128,1152]{1,0:T(8,128)(2,1)S(1)}, u32[]{:S(2)}, u32[]{:S(2)}) %collective-permute-start.3) | collective-permute-done | bytes 294944 | tf_op jit(solution)/shard_map/ppermute | solution.py:640
  56.2 8.2 %collective-permute-done.6.refs_3_ = bf16[64,3456]{1,0:T(8,128)(2,1)S(1)} collective-permute-done((bf16[64,3456]{1,0:T(8,128)(2,1)S(1)}, bf16[64,3456]{1,0:T(8,128)(2,1)S(1)}, u32[]{:S(2)}, u32[]{:S(2)}) %collective-permute-start.6) | collective-permute-done | bytes 442400 | tf_op jit(solution)/shard_map/ppermute | solution.py:674
  67.3 3.4 all-to-all-start
  72.2 6.6 %all-to-all-done = f32[8,1,6912]{2,1,0:T(1,128)S(1)} async-done(((f32[8,1,6912]{2,1,0:T(1,128)}), f32[8,1,6912]{2,1,0:T(1,128)S(1)}, u32[]{:S(2)}, u32[]{:S(2)}) %all-to-all-start) | async-done | bytes 221216 | tf_op jit(solution)/shard_map/all_to_all | solution.py:884
  80.6 13.7 %shard_map.246 = (bf16[512,1728]{1,0:T(8,128)(2,1)}, bf16[512,1792]{1,0:T(8,128)(2,1)}, bf16[512,1152]{1,0:T(8,128)(2,1)}, bf16[1152,3456]{1,0:T(8,128)(2,1)}) custom-call(s32[1]{0:T(128)} %bitcast.core, s32[10]{0:T(128)S(1)} %stack.145.spots, bf16[512,1152]{1,0:T(8,128)(2,1)} %copy-done.1, f32[1,6912]{1,0:T(1,128)} %broadcast_in_dim.60.mods, ...), custom_call_target="tpu_custom_call" | custom-call | tf_op jit(solution)/shard_map/pallas_call | solution.py:158
  96.7 3.7 collective-permute-start.14
  100.4 1.9 collective-permute-start.16
  102.3 2.3 collective-permute-start.17
  117.2 1.9 collective-permute-start.23
  120.1 27.2 %shard_map.247 = (bf16[512,576]{1,0:T(8,128)(2,1)}, bf16[512,640]{1,0:T(8,128)(2,1)}, f32[8,1024]{1,0:T(8,128)}) custom-call(s32[8]{0:T(128)S(1)} %stack.154.limits, bf16[512,1728]{1,0:T(8,128)(2,1)} %get-tuple-element.127.mine, bf16[512,1792]{1,0:T(8,128)(2,1)} %collective-permute-done.13.theirs), custom_call_target="tpu_custom_call" | custom-call | tf_op jit(solution)/shard_map/pallas_call | solution.py:538
  153.1 7.0 %collective-permute-done.21.refs_3_ = bf16[64,1152]{1,0:T(8,128)(2,1)S(1)} collective-permute-done((bf16[64,1152]{1,0:T(8,128)(2,1)S(1)}, bf16[64,1152]{1,0:T(8,128)(2,1)S(1)}, u32[]{:S(2)}, u32[]{:S(2)}) %collective-permute-start.21) | collective-permute-done | bytes 147488 | tf_op jit(solution)/shard_map/ppermute | solution.py:674
  163.8 10.6 %shard_map.248 = (bf16[512,1152]{1,0:T(8,128)(2,1)}, f32[512,1152]{1,0:T(8,128)}, f32[512,1152]{1,0:T(8,128)}, f32[512,1]{1,0:T(8,128)}, bf16[512,1152]{1,0:T(8,128)(2,1)}, /*index=5*/bf16[1152,1152]{1,0:T(8,128)(2,1)}) custom-call(s32[1]{0:T(128)} %bitcast.core, s32[10]{0:T(128)S(1)} %stack.145.spots, bf16[512,576]{1,0:T(8,128)(2,1)} %get-tuple-element.90.own, ...), custom_call_target="tpu_custom_call" | custom-call | tf_op jit(solution)/shard_map/pallas_call | solution.py:208
  174.4 16.1 %shard_map.249 = (bf16[512,4608]{1,0:T(8,128)(2,1)}, f32[512,4608]{1,0:T(8,128)}) custom-call(bf16[512,1152]{1,0:T(8,128)(2,1)} %get-tuple-element.114.moved.left, bf16[1152,4608]{1,0:T(8,128)(2,1)} %all-gather.5.cloned.1.call-done.matrix, f32[1,4608]{1,0:T(1,128)} %reshape.183.offset), custom_call_target="tpu_custom_call" | custom-call | tf_op jit(solution)/shard_map/pallas_call | solution.py:280
  190.5 8.8 %shard_map.250 = bf16[4,576,1152]{2,1,0:T(8,128)(2,1)} custom-call(s32[2]{0:T(128)S(1)} %pad_add_fusion.2.where, bf16[512,4608]{1,0:T(8,128)(2,1)} %get-tuple-element.140.left.act, bf16[512,1152]{1,0:T(8,128)(2,1)} %get-tuple-element.100.right.grad), custom_call_target="tpu_custom_call" | custom-call | tf_op jit(solution)/shard_map/pallas_call | solution.py:254
  199.5 9.4 %all-gather.7.cloned.1.call-done.matrix = bf16[4608,1152]{1,0:T(8,128)(2,1)} async-done(((bf16[576,1152]{1,0:T(8,128)(2,1)}), bf16[4608,1152]{1,0:T(8,128)(2,1)}) %all-gather.7.cloned.1.call-update) | async-done | bytes 10616848 | tf_op jit(solution)/shard_map/all_gather | solution.py:669
  208.9 13.5 %shard_map.251 = (bf16[512,4608]{1,0:T(8,128)(2,1)}, f32[1,4608]{1,0:T(1,128)}) custom-call(bf16[512,1152]{1,0:T(8,128)(2,1)} %get-tuple-element.100.right.grad, bf16[4608,1152]{1,0:T(8,128)(2,1)} %all-gather.7.cloned.1.call-done.matrix, f32[512,4608]{1,0:T(8,128)} %get-tuple-element.102.slope), custom_call_target="tpu_custom_call" | custom-call | tf_op jit(solution)/shard_map/pallas_call | solution.py:304
  222.4 9.3 %shard_map.252 = bf16[4,576,1152]{2,1,0:T(8,128)(2,1)} custom-call(s32[2]{0:T(128)S(1)} %pad_add_fusion.1.where, bf16[512,4608]{1,0:T(8,128)(2,1)} %get-tuple-element.140.left.act, bf16[512,1152]{1,0:T(8,128)(2,1)} %get-tuple-element.100.right.grad, bf16[4,576,1152]{2,1,0:T(8,128)(2,1)} %collective-permute-done.28.refs_0_), custom_call_target="tpu_custom_call" | custom-call | tf_op jit(solution)/shard_map/pallas_call | solution.py:254
  231.7 7.9 %shard_map.253 = bf16[4,144,4608]{2,1,0:T(8,128)(2,1)} custom-call(s32[4]{0:T(128)S(1)} %pad_add_fusion.3.spots, bf16[512,1152]{1,0:T(8,128)(2,1)} %get-tuple-element.114.moved.left, bf16[512,4608]{1,0:T(8,128)(2,1)} %get-tuple-element.108.right.d_upper), custom_call_target="tpu_custom_call" | custom-call | tf_op jit(solution)/shard_map/pallas_call | solution.py:480
  242.7 2.4 slice_bitcast_fusion
  246.8 11.7 %collective-permute-done.30 = bf16[288,1152]{1,0:T(8,128)(2,1)S(1)} collective-permute-done((bf16[288,1152]{1,0:T(8,128)(2,1)S(1)}, bf16[288,1152]{1,0:T(8,128)(2,1)S(1)}, u32[]{:S(2)}, u32[]{:S(2)}) %collective-permute-start.30) | collective-permute-done | bytes 663584 | tf_op jit(solution)/shard_map/ppermute | solution.py:674
  260.2 2.6 collective-permute-done.29
  264.3 19.1 %shard_map.254 = (f32[512,1152]{1,0:T(8,128)}, bf16[512,1152]{1,0:T(8,128)(2,1)}, bf16[512,576]{1,0:T(8,128)(2,1)}, bf16[512,640]{1,0:T(8,128)(2,1)}, f32[4,1152]{1,0:T(4,128)}) custom-call(s32[1]{0:T(128)} %bitcast.core, bf16[512,4608]{1,0:T(8,128)(2,1)} %get-tuple-element.108.right.d_upper, bf16[1152,4608]{1,0:T(8,128)(2,1)} %all-gather.5.cloned.1.call-done.matrix, ...), custom_call_target="tpu_custom_call" | custom-call | tf_op jit(solution)/shard_map/pallas_call | solution.py:394
  283.4 9.1 %shard_map.255 = bf16[4,144,4608]{2,1,0:T(8,128)(2,1)} custom-call(s32[4]{0:T(128)S(1)} %pad_add_fusion.spots, bf16[512,1152]{1,0:T(8,128)(2,1)} %get-tuple-element.114.moved.left, bf16[512,4608]{1,0:T(8,128)(2,1)} %get-tuple-element.108.right.d_upper, bf16[4,144,4608]{2,1,0:T(8,128)(2,1)} %collective-permute-done.31.refs_0_), custom_call_target="tpu_custom_call" | custom-call | tf_op jit(solution)/shard_map/pallas_call | solution.py:480
  292.6 4.1 shard_map.256
  297.2 2.4 slice_bitcast_fusion.10
  300.7 2.0 slice_bitcast_fusion.3
  304.3 4.4 shard_map.257
  313.1 3.6 collective-permute-done.35
  325.2 16.8 %shard_map.258 = (bf16[512,864]{1,0:T(8,128)(2,1)}, bf16[512,896]{1,0:T(8,128)(2,1)}) custom-call(s32[8]{0:T(128)S(1)} %stack.154.limits, bf16[512,1728]{1,0:T(8,128)(2,1)} %get-tuple-element.127.mine, bf16[512,1792]{1,0:T(8,128)(2,1)} %collective-permute-done.13.theirs, bf16[512,576]{1,0:T(8,128)(2,1)} %get-tuple-element.113.d_mine, ...), custom_call_target="tpu_custom_call" | custom-call | tf_op jit(solution)/shard_map/pallas_call | solution.py:591
  341.9 17.2 %shard_map.259 = (bf16[512,864]{1,0:T(8,128)(2,1)}, bf16[512,896]{1,0:T(8,128)(2,1)}) custom-call(s32[8]{0:T(128)S(1)} %stack.154.limits, bf16[512,1728]{1,0:T(8,128)(2,1)} %get-tuple-element.127.mine, bf16[512,1792]{1,0:T(8,128)(2,1)} %collective-permute-done.13.theirs, bf16[512,576]{1,0:T(8,128)(2,1)} %get-tuple-element.113.d_mine, ...), custom_call_target="tpu_custom_call" | custom-call | tf_op jit(solution)/shard_map/pallas_call | solution.py:591
  360.8 5.1 collective-permute-done.38
  368.6 5.2 shard_map.260.right.d_qkv
  373.8 3.3 add_convert_fusion
  377.1 6.8 %shard_map.261 = bf16[4,144,3456]{2,1,0:T(8,128)(2,1)} custom-call(s32[4]{0:T(128)S(1)} %pad_add_fusion.3.spots, bf16[512,1152]{1,0:T(8,128)(2,1)} %get-tuple-element.139.left, bf16[512,3456]{1,0:T(8,128)(2,1)} %shard_map.260.right.d_qkv), custom_call_target="tpu_custom_call" | custom-call | tf_op jit(solution)/shard_map/pallas_call | solution.py:480
  387.0 8.1 %collective-permute-done.45 = bf16[144,1152]{1,0:T(8,128)(2,1)S(1)} collective-permute-done((bf16[144,1152]{1,0:T(8,128)(2,1)S(1)}, bf16[144,1152]{1,0:T(8,128)(2,1)S(1)}, u32[]{:S(2)}, u32[]{:S(2)}) %collective-permute-start.45) | collective-permute-done | bytes 331808 | tf_op jit(solution)/shard_map/ppermute | solution.py:674
  395.3 1.8 add_convert_fusion.9
  397.2 12.5 %shard_map.262 = (bf16[512,1152]{1,0:T(8,128)(2,1)}, f32[2,1152]{1,0:T(2,128)}, f32[1,3456]{1,0:T(1,128)}) custom-call(bf16[512,3456]{1,0:T(8,128)(2,1)} %shard_map.260.right.d_qkv, bf16[1152,3456]{1,0:T(8,128)(2,1)} %get-tuple-element.136.matrix, bf16[512,1152]{1,0:T(8,128)(2,1)} %copy-done.1, f32[1,6912]{1,0:T(1,128)} %broadcast_in_dim.60.mods, ...), custom_call_target="tpu_custom_call" | custom-call | tf_op jit(solution)/shard_map/pallas_call | solution.py:442
  411.4 8.1 %shard_map.263 = bf16[4,144,3456]{2,1,0:T(8,128)(2,1)} custom-call(s32[4]{0:T(128)S(1)} %pad_add_fusion.spots, bf16[512,1152]{1,0:T(8,128)(2,1)} %get-tuple-element.139.left, bf16[512,3456]{1,0:T(8,128)(2,1)} %shard_map.260.right.d_qkv, bf16[4,144,3456]{2,1,0:T(8,128)(2,1)} %collective-permute-done.46.refs_0_), custom_call_target="tpu_custom_call" | custom-call | tf_op jit(solution)/shard_map/pallas_call | solution.py:480
  419.5 3.0 slice_bitcast_fusion.6
  422.4 3.0 slice_bitcast_fusion.13
  425.4 13.3 %shard_map.264 = (bf16[512,1152]{1,0:T(8,128)(2,1)}, f32[1,1152]{1,0:T(1,128)}) custom-call(bf16[512,4608]{1,0:T(8,128)(2,1)} %get-tuple-element.140.left.act, bf16[4608,1152]{1,0:T(8,128)(2,1)} %all-gather.7.cloned.1.call-done.matrix, f32[1,1152]{1,0:T(1,128)} %reshape.184.offset, bf16[512,1152]{1,0:T(8,128)(2,1)} %copy-done.1, ...), custom_call_target="tpu_custom_call" | custom-call | tf_op jit(solution)/shard_map/pallas_call | solution.py:342
  442.6 3.7 collective-permute-start.53
  447.3 3.3 all-to-all-start.1
  450.9 2.7 collective-permute-start.55
  455.8 23.8 %collective-permute-start.56 = (bf16[128,1152]{1,0:T(8,128)(2,1)S(1)}, bf16[128,1152]{1,0:T(8,128)(2,1)}, u32[]{:S(2)}, u32[]{:S(2)}) collective-permute-start(bf16[128,1152]{1,0:T(8,128)(2,1)S(1)} %get-tuple-element.187), channel_id=1, source_target_pairs={{5,0},{4,1},{1,2},{0,3},{3,4},{2,5},{7,6},{6,7},{13,8},{12,9},{9,1... | collective-permute-start | bytes 884744 | tf_op jit(solution)/shard_map/ppermute | solution.py:648
  490.4 2.3 fusion.12
  492.7 3.8 collective-permute-start.49
  496.5 7.8 %collective-permute-done.58 = bf16[144,3456]{1,0:T(8,128)(2,1)} collective-permute-done((bf16[144,3456]{1,0:T(8,128)(2,1)}, bf16[144,3456]{1,0:T(8,128)(2,1)}, u32[]{:S(2)}, u32[]{:S(2)}) %collective-permute-start.58) | collective-permute-done | bytes 995360 | tf_op jit(solution)/shard_map/ppermute | solution.py:674
  504.3 2.9 collective-permute-done.57
  507.1 1.9 add_convert_fusion.2
  512.7 1.9 collective-permute-start.51
  514.7 3.6 collective-permute-start.60
  519.4 11.5 %collective-permute-done.60 = bf16[1,6912]{1,0:T(2,128)(2,1)S(1)} collective-permute-done((bf16[1,6912]{1,0:T(2,128)(2,1)S(1)}, bf16[1,6912]{1,0:T(2,128)(2,1)S(1)}, u32[]{:S(2)}, u32[]{:S(2)}) %collective-permute-start.60) | collective-permute-done | bytes 13856 | tf_op jit(solution)/shard_map/ppermute | solution.py:813
  531.2 4.8 collective-permute-done.61
  537.2 3.1 collective-permute-done.62
  541.6 3.7 collective-permute-done.63
  548.0 3.3 all-to-all-start.2
  551.3 2.6 fusion.17
  555.7 1.8 convert_element_type.290
  559.9 32.4 %all-reduce.8.cloned.1.call-done = bf16[152,3456]{1,0:T(8,128)(2,1)} async-done(((bf16[152,3456]{1,0:T(8,128)(2,1)}), bf16[152,3456]{1,0:T(8,128)(2,1)}) %all-reduce.8.cloned.1.call-update) | async-done | bytes 1050640 | tf_op jit(solution)/shard_map/psum | solution.py:758
  (389 shorter events, 110.6 us)
Async XLA Ops:
  7.3 167.2 %all-gather.5.cloned.1.call-start = ((), (), s32[]{:S(2)}) async-start(), calls=%async_computation.3 | async-start | bytes 11943936 | tf_op jit(solution)/shard_map/all_gather | solution.py:669
  7.3 44.2 %collective-permute-start.4 = (bf16[144,3456]{1,0:T(8,128)(2,1)}, bf16[144,3456]{1,0:T(8,128)(2,1)}, u32[]{:S(2)}, u32[]{:S(2)}) collective-permute-start(bf16[144,3456]{1,0:T(8,128)(2,1)} %refs_0_.1), channel_id=1, source_target_pairs={{0,8},{4,12},{8,0},{12,4},{16,24},{20,28},{24,16},{28,20},{1,9},{5... | collective-permute-start | bytes 2985992 | tf_op jit(solution)/shard_map/ppermute | solution.py:674
  10.3 41.2 %collective-permute-start.5 = (bf16[144,3456]{1,0:T(8,128)(2,1)}, bf16[144,3456]{1,0:T(8,128)(2,1)}, u32[]{:S(2)}, u32[]{:S(2)}) collective-permute-start(bf16[144,3456]{1,0:T(8,128)(2,1)} %refs_0_.1), channel_id=1, source_target_pairs={{0,16},{4,20},{8,24},{12,28},{16,0},{20,4},{24,8},{28,12},{1,17},{... | collective-permute-start | bytes 2985992 | tf_op jit(solution)/shard_map/ppermute | solution.py:674
  14.0 25.2 %collective-permute-start = (bf16[128,1152]{1,0:T(8,128)(2,1)S(1)}, bf16[128,1152]{1,0:T(8,128)(2,1)S(1)}, u32[]{:S(2)}, u32[]{:S(2)}) collective-permute-start(bf16[128,1152]{1,0:T(8,128)(2,1)S(1)} %get-tuple-element.201), channel_id=1, source_target_pairs={{0,0},{1,1},{2,4},{3,5},{4,6},{5,7},{6,2},{7,3},{8,8},{9,9},{10,12... | collective-permute-start | bytes 884744 | tf_op jit(solution)/shard_map/ppermute | solution.py:640
  14.7 27.8 %collective-permute-start.1 = (bf16[128,1152]{1,0:T(8,128)(2,1)}, bf16[128,1152]{1,0:T(8,128)(2,1)}, u32[]{:S(2)}, u32[]{:S(2)}) collective-permute-start(bf16[128,1152]{1,0:T(8,128)(2,1)} %get-tuple-element.200), channel_id=1, source_target_pairs={{0,1},{1,0},{2,5},{3,4},{4,7},{5,6},{6,3},{7,2},{8,9},{9,8},{10,13... | collective-permute-start | bytes 884744 | tf_op jit(solution)/shard_map/ppermute | solution.py:640
  16.3 27.1 %collective-permute-start.2 = (bf16[128,1152]{1,0:T(8,128)(2,1)}, bf16[128,1152]{1,0:T(8,128)(2,1)}, u32[]{:S(2)}, u32[]{:S(2)}) collective-permute-start(bf16[128,1152]{1,0:T(8,128)(2,1)} %get-tuple-element.202), channel_id=1, source_target_pairs={{0,4},{1,5},{2,0},{3,1},{4,2},{5,3},{6,6},{7,7},{8,12},{9,13},{10,... | collective-permute-start | bytes 884744 | tf_op jit(solution)/shard_map/ppermute | solution.py:640
  39.9 11.5 %collective-permute-start.3 = (bf16[128,1152]{1,0:T(8,128)(2,1)}, bf16[128,1152]{1,0:T(8,128)(2,1)S(1)}, u32[]{:S(2)}, u32[]{:S(2)}) collective-permute-start(bf16[128,1152]{1,0:T(8,128)(2,1)} %get-tuple-element.199), channel_id=1, source_target_pairs={{0,5},{1,4},{2,1},{3,0},{4,3},{5,2},{6,7},{7,6},{8,13},{9,12},{10,... | collective-permute-start | bytes 884744 | tf_op jit(solution)/shard_map/ppermute | solution.py:640
  53.0 12.5 %collective-permute-start.7 = (bf16[80,3456]{1,0:T(8,128)(2,1)S(1)}, bf16[80,3456]{1,0:T(8,128)(2,1)}, u32[]{:S(2)}, u32[]{:S(2)}) collective-permute-start(bf16[80,3456]{1,0:T(8,128)(2,1)S(1)} %slice.317), channel_id=1, source_target_pairs={{0,8},{4,12},{8,0},{12,4},{16,24},{20,28},{24,16},{28,20},{1,9},{5... | collective-permute-start | bytes 1658888 | tf_op jit(solution)/shard_map/ppermute | solution.py:674
  54.6 9.7 %collective-permute-start.6 = (bf16[64,3456]{1,0:T(8,128)(2,1)S(1)}, bf16[64,3456]{1,0:T(8,128)(2,1)S(1)}, u32[]{:S(2)}, u32[]{:S(2)}) collective-permute-start(bf16[64,3456]{1,0:T(8,128)(2,1)S(1)} %slice.316), channel_id=1, source_target_pairs={{0,16},{4,20},{8,24},{12,28},{16,0},{20,4},{24,8},{28,12},{1,17},{... | collective-permute-start | bytes 1327112 | tf_op jit(solution)/shard_map/ppermute | solution.py:674
  65.5 14.1 %collective-permute-start.8 = (bf16[144,3456]{1,0:T(8,128)(2,1)}, bf16[144,3456]{1,0:T(8,128)(2,1)}, u32[]{:S(2)}, u32[]{:S(2)}) collective-permute-start(bf16[144,3456]{1,0:T(8,128)(2,1)} %refs_0_.1), channel_id=1, source_target_pairs={{0,4},{4,0},{8,12},{12,8},{16,20},{20,16},{24,28},{28,24},{1,5},{5... | collective-permute-start | bytes 2985992 | tf_op jit(solution)/shard_map/ppermute | solution.py:674
  65.6 14.0 %collective-permute-start.10 = (bf16[144,3456]{1,0:T(8,128)(2,1)}, bf16[144,3456]{1,0:T(8,128)(2,1)S(1)}, u32[]{:S(2)}, u32[]{:S(2)}) collective-permute-start(bf16[144,3456]{1,0:T(8,128)(2,1)} %collective-permute-done.5.refs_2_), channel_id=1, source_target_pairs={{0,4},{4,0},{8,12},{12,8},{16,20},{20,16},{24,28},{28,24},{1,5},{5... | collective-permute-start | bytes 2985992 | tf_op jit(solution)/shard_map/ppermute | solution.py:674
  66.1 13.6 %collective-permute-start.9 = (bf16[144,3456]{1,0:T(8,128)(2,1)}, bf16[144,3456]{1,0:T(8,128)(2,1)}, u32[]{:S(2)}, u32[]{:S(2)}) collective-permute-start(bf16[144,3456]{1,0:T(8,128)(2,1)} %collective-permute-done.4.refs_1_), channel_id=1, source_target_pairs={{0,4},{4,0},{8,12},{12,8},{16,20},{20,16},{24,28},{28,24},{1,5},{5... | collective-permute-start | bytes 2985992 | tf_op jit(solution)/shard_map/ppermute | solution.py:674
  67.3 11.6 %all-to-all-start = ((f32[8,1,6912]{2,1,0:T(1,128)}), f32[8,1,6912]{2,1,0:T(1,128)S(1)}, u32[]{:S(2)}, u32[]{:S(2)}) async-start(f32[8,1,6912]{2,1,0:T(1,128)} %all_to_all.18), calls=%async_computation | async-start | bytes 442368 | tf_op jit(solution)/shard_map/all_to_all | solution.py:884
  70.7 138.3 %all-gather.7.cloned.1.call-start = ((), (), s32[]{:S(2)}) async-start(), calls=%async_computation.4 | async-start | bytes 11943936 | tf_op jit(solution)/shard_map/all_gather | solution.py:669
  70.7 8.9 %collective-permute-start.11 = (bf16[64,3456]{1,0:T(8,128)(2,1)}, bf16[64,3456]{1,0:T(8,128)(2,1)}, u32[]{:S(2)}, u32[]{:S(2)}) collective-permute-start(bf16[64,3456]{1,0:T(8,128)(2,1)} %copy-done.27), channel_id=1, source_target_pairs={{0,4},{4,0},{8,12},{12,8},{16,20},{20,16},{24,28},{28,24},{1,5},{5... | collective-permute-start | bytes 1327112 | tf_op jit(solution)/shard_map/ppermute | solution.py:674
  71.2 8.5 %collective-permute-start.12 = (bf16[80,3456]{1,0:T(8,128)(2,1)}, bf16[80,3456]{1,0:T(8,128)(2,1)}, u32[]{:S(2)}, u32[]{:S(2)}) collective-permute-start(bf16[80,3456]{1,0:T(8,128)(2,1)} %collective-permute-done.7.refs_4_), channel_id=1, source_target_pairs={{0,4},{4,0},{8,12},{12,8},{16,20},{20,16},{24,28},{28,24},{1,5},{5... | collective-permute-start | bytes 1658888 | tf_op jit(solution)/shard_map/ppermute | solution.py:674
  94.3 279.5 %all-reduce.6.cloned.1.call-start = ((), (), s32[]{:S(2)}) async-start(), calls=%async_computation.5 | async-start | bytes 2654208 | tf_op jit(solution)/shard_map/psum | solution.py:758
  94.4 22.8 %collective-permute-start.13 = (bf16[512,1792]{1,0:T(8,128)(2,1)}, bf16[512,1792]{1,0:T(8,128)(2,1)}, u32[]{:S(2)}, u32[]{:S(2)}) collective-permute-start(bf16[512,1792]{1,0:T(8,128)(2,1)} %get-tuple-element.88), channel_id=1, source_target_pairs={{0,4},{4,0},{8,12},{12,8},{16,20},{20,16},{24,28},{28,24},{1,5},{5... | collective-permute-start | bytes 5505032 | tf_op jit(solution)/shard_map/ppermute | solution.py:612
  96.7 18.4 %collective-permute-start.14 = (bf16[128,1152]{1,0:T(8,128)(2,1)}, bf16[128,1152]{1,0:T(8,128)(2,1)}, u32[]{:S(2)}, u32[]{:S(2)}) collective-permute-start(bf16[128,1152]{1,0:T(8,128)(2,1)} %get-tuple-element.197), channel_id=1, source_target_pairs={{0,0},{1,1},{2,4},{3,5},{4,6},{5,7},{6,2},{7,3},{8,8},{9,9},{10,12... | collective-permute-start | bytes 884744 | tf_op jit(solution)/shard_map/ppermute | solution.py:640
  100.4 15.7 %collective-permute-start.15 = (bf16[128,1152]{1,0:T(8,128)(2,1)}, bf16[128,1152]{1,0:T(8,128)(2,1)}, u32[]{:S(2)}, u32[]{:S(2)}) collective-permute-start(bf16[128,1152]{1,0:T(8,128)(2,1)} %get-tuple-element.196), channel_id=1, source_target_pairs={{0,1},{1,0},{2,5},{3,4},{4,7},{5,6},{6,3},{7,2},{8,9},{9,8},{10,13... | collective-permute-start | bytes 884744 | tf_op jit(solution)/shard_map/ppermute | solution.py:640
  100.4 46.9 %collective-permute-start.16 = (bf16[128,1152]{1,0:T(8,128)(2,1)}, bf16[128,1152]{1,0:T(8,128)(2,1)}, u32[]{:S(2)}, u32[]{:S(2)}) collective-permute-start(bf16[128,1152]{1,0:T(8,128)(2,1)} %get-tuple-element.198), channel_id=1, source_target_pairs={{0,4},{1,5},{2,0},{3,1},{4,2},{5,3},{6,6},{7,7},{8,12},{9,13},{10,... | collective-permute-start | bytes 884744 | tf_op jit(solution)/shard_map/ppermute | solution.py:640
  102.3 46.8 %collective-permute-start.17 = (bf16[128,1152]{1,0:T(8,128)(2,1)}, bf16[128,1152]{1,0:T(8,128)(2,1)}, u32[]{:S(2)}, u32[]{:S(2)}) collective-permute-start(bf16[128,1152]{1,0:T(8,128)(2,1)} %get-tuple-element.195), channel_id=1, source_target_pairs={{0,5},{1,4},{2,1},{3,0},{4,3},{5,2},{6,7},{7,6},{8,13},{9,12},{10,... | collective-permute-start | bytes 884744 | tf_op jit(solution)/shard_map/ppermute | solution.py:640
  116.0 32.3 %collective-permute-start.19 = (bf16[144,1152]{1,0:T(8,128)(2,1)S(1)}, bf16[144,1152]{1,0:T(8,128)(2,1)S(1)}, u32[]{:S(2)}, u32[]{:S(2)}) collective-permute-start(bf16[144,1152]{1,0:T(8,128)(2,1)S(1)} %copy-done.31), channel_id=1, source_target_pairs={{0,8},{4,12},{8,0},{12,4},{16,24},{20,28},{24,16},{28,20},{1,9},{5... | collective-permute-start | bytes 995336 | tf_op jit(solution)/shard_map/ppermute | solution.py:674
  116.1 32.3 %collective-permute-start.20 = (bf16[144,1152]{1,0:T(8,128)(2,1)S(1)}, bf16[144,1152]{1,0:T(8,128)(2,1)S(1)}, u32[]{:S(2)}, u32[]{:S(2)}) collective-permute-start(bf16[144,1152]{1,0:T(8,128)(2,1)S(1)} %copy-done.31), channel_id=1, source_target_pairs={{0,16},{4,20},{8,24},{12,28},{16,0},{20,4},{24,8},{28,12},{1,17},{... | collective-permute-start | bytes 995336 | tf_op jit(solution)/shard_map/ppermute | solution.py:674
  117.2 33.3 %collective-permute-start.23 = (bf16[144,1152]{1,0:T(8,128)(2,1)S(1)}, bf16[144,1152]{1,0:T(8,128)(2,1)S(1)}, u32[]{:S(2)}, u32[]{:S(2)}) collective-permute-start(bf16[144,1152]{1,0:T(8,128)(2,1)S(1)} %copy-done.31), channel_id=1, source_target_pairs={{0,4},{4,0},{8,12},{12,8},{16,20},{20,16},{24,28},{28,24},{1,5},{5... | collective-permute-start | bytes 995336 | tf_op jit(solution)/shard_map/ppermute | solution.py:674
  147.3 14.7 %collective-permute-start.18 = (bf16[512,640]{1,0:T(8,128)(2,1)}, bf16[512,640]{1,0:T(8,128)(2,1)S(1)}, u32[]{:S(2)}, u32[]{:S(2)}) collective-permute-start(bf16[512,640]{1,0:T(8,128)(2,1)} %get-tuple-element.91), channel_id=1, source_target_pairs={{0,4},{4,0},{8,12},{12,8},{16,20},{20,16},{24,28},{28,24},{1,5},{5... | collective-permute-start | bytes 1966088 | tf_op jit(solution)/shard_map/ppermute | solution.py:612
  148.4 13.5 %collective-permute-start.24 = (bf16[144,1152]{1,0:T(8,128)(2,1)S(1)}, bf16[144,1152]{1,0:T(8,128)(2,1)S(1)}, u32[]{:S(2)}, u32[]{:S(2)}) collective-permute-start(bf16[144,1152]{1,0:T(8,128)(2,1)S(1)} %collective-permute-done.19.refs_1_), channel_id=1, source_target_pairs={{0,4},{4,0},{8,12},{12,8},{16,20},{20,16},{24,28},{28,24},{1,5},{5... | collective-permute-start | bytes 995336 | tf_op jit(solution)/shard_map/ppermute | solution.py:674
  148.9 13.0 %collective-permute-start.25 = (bf16[144,1152]{1,0:T(8,128)(2,1)S(1)}, bf16[144,1152]{1,0:T(8,128)(2,1)S(1)}, u32[]{:S(2)}, u32[]{:S(2)}) collective-permute-start(bf16[144,1152]{1,0:T(8,128)(2,1)S(1)} %collective-permute-done.20.refs_2_), channel_id=1, source_target_pairs={{0,4},{4,0},{8,12},{12,8},{16,20},{20,16},{24,28},{28,24},{1,5},{5... | collective-permute-start | bytes 995336 | tf_op jit(solution)/shard_map/ppermute | solution.py:674
  149.1 11.2 %collective-permute-start.22 = (bf16[80,1152]{1,0:T(8,128)(2,1)S(1)}, bf16[80,1152]{1,0:T(8,128)(2,1)S(1)}, u32[]{:S(2)}, u32[]{:S(2)}) collective-permute-start(bf16[80,1152]{1,0:T(8,128)(2,1)S(1)} %slice.320), channel_id=1, source_target_pairs={{0,8},{4,12},{8,0},{12,4},{16,24},{20,28},{24,16},{28,20},{1,9},{5... | collective-permute-start | bytes 552968 | tf_op jit(solution)/shard_map/ppermute | solution.py:674
  150.5 9.6 %collective-permute-start.21 = (bf16[64,1152]{1,0:T(8,128)(2,1)S(1)}, bf16[64,1152]{1,0:T(8,128)(2,1)S(1)}, u32[]{:S(2)}, u32[]{:S(2)}) collective-permute-start(bf16[64,1152]{1,0:T(8,128)(2,1)S(1)} %slice.319), channel_id=1, source_target_pairs={{0,16},{4,20},{8,24},{12,28},{16,0},{20,4},{24,8},{28,12},{1,17},{... | collective-permute-start | bytes 442376 | tf_op jit(solution)/shard_map/ppermute | solution.py:674
  199.3 23.1 %collective-permute-start.28 = (bf16[4,576,1152]{2,1,0:T(8,128)(2,1)}, bf16[4,576,1152]{2,1,0:T(8,128)(2,1)}, u32[]{:S(2)}, u32[]{:S(2)}) collective-permute-start(bf16[4,576,1152]{2,1,0:T(8,128)(2,1)} %shard_map.250), channel_id=1, source_target_pairs={{0,4},{4,0},{8,12},{12,8},{16,20},{20,16},{24,28},{28,24},{1,5},{5... | collective-permute-start | bytes 15925256 | tf_op jit(solution)/shard_map/ppermute | solution.py:674
  239.6 43.9 %collective-permute-start.31 = (bf16[4,144,4608]{2,1,0:T(8,128)(2,1)}, bf16[4,144,4608]{2,1,0:T(8,128)(2,1)}, u32[]{:S(2)}, u32[]{:S(2)}) collective-permute-start(bf16[4,144,4608]{2,1,0:T(8,128)(2,1)} %shard_map.253), channel_id=1, source_target_pairs={{0,4},{4,0},{8,12},{12,8},{16,20},{20,16},{24,28},{28,24},{1,5},{5... | collective-permute-start | bytes 15925256 | tf_op jit(solution)/shard_map/ppermute | solution.py:674
  241.6 16.9 %collective-permute-start.30 = (bf16[288,1152]{1,0:T(8,128)(2,1)S(1)}, bf16[288,1152]{1,0:T(8,128)(2,1)S(1)}, u32[]{:S(2)}, u32[]{:S(2)}) collective-permute-start(bf16[288,1152]{1,0:T(8,128)(2,1)S(1)} %get-tuple-element.175), channel_id=1, source_target_pairs={{0,8},{4,12},{8,0},{12,4},{16,24},{20,28},{24,16},{28,20},{1,9},{5... | collective-permute-start | bytes 1990664 | tf_op jit(solution)/shard_map/ppermute | solution.py:674
  245.2 17.7 %collective-permute-start.29 = (bf16[288,1152]{1,0:T(8,128)(2,1)S(1)}, bf16[288,1152]{1,0:T(8,128)(2,1)S(1)}, u32[]{:S(2)}, u32[]{:S(2)}) collective-permute-start(bf16[288,1152]{1,0:T(8,128)(2,1)S(1)} %get-tuple-element.176), channel_id=1, source_target_pairs={{0,16},{4,20},{8,24},{12,28},{16,0},{20,4},{24,8},{28,12},{1,17},{... | collective-permute-start | bytes 1990664 | tf_op jit(solution)/shard_map/ppermute | solution.py:674
  258.8 49.8 %collective-permute-start.34 = (bf16[576,1152]{1,0:T(8,128)(2,1)S(1)}, bf16[576,1152]{1,0:T(8,128)(2,1)S(1)}, u32[]{:S(2)}, u32[]{:S(2)}) collective-permute-start(bf16[576,1152]{1,0:T(8,128)(2,1)S(1)} %pad_maximum_fusion.1), channel_id=1, source_target_pairs={{0,16},{4,20},{8,24},{12,28},{16,0},{20,4},{24,8},{28,12},{1,17},{... | collective-permute-start | bytes 3981320 | tf_op jit(solution)/shard_map/ppermute | solution.py:674
  263.2 45.5 %collective-permute-start.33 = (bf16[576,1152]{1,0:T(8,128)(2,1)S(1)}, bf16[576,1152]{1,0:T(8,128)(2,1)S(1)}, u32[]{:S(2)}, u32[]{:S(2)}) collective-permute-start(bf16[576,1152]{1,0:T(8,128)(2,1)S(1)} %pad_maximum_fusion), channel_id=1, source_target_pairs={{0,8},{4,12},{8,0},{12,4},{16,24},{20,28},{24,16},{28,20},{1,9},{5... | collective-permute-start | bytes 3981320 | tf_op jit(solution)/shard_map/ppermute | solution.py:674
  283.4 41.7 %collective-permute-start.37 = (bf16[512,640]{1,0:T(8,128)(2,1)}, bf16[512,640]{1,0:T(8,128)(2,1)}, u32[]{:S(2)}, u32[]{:S(2)}) collective-permute-start(bf16[512,640]{1,0:T(8,128)(2,1)} %get-tuple-element.123), channel_id=1, source_target_pairs={{0,4},{4,0},{8,12},{12,8},{16,20},{20,16},{24,28},{28,24},{1,5},{5... | collective-permute-start | bytes 1966088 | tf_op jit(solution)/shard_map/ppermute | solution.py:612
  299.6 17.2 %collective-permute-start.35 = (bf16[72,4608]{1,0:T(8,128)(2,1)}, bf16[72,4608]{1,0:T(8,128)(2,1)}, u32[]{:S(2)}, u32[]{:S(2)}) collective-permute-start(bf16[72,4608]{1,0:T(8,128)(2,1)} %get-tuple-element.170), channel_id=1, source_target_pairs={{0,16},{4,20},{8,24},{12,28},{16,0},{20,4},{24,8},{28,12},{1,17},{... | collective-permute-start | bytes 1990664 | tf_op jit(solution)/shard_map/ppermute | solution.py:674
  302.8 18.2 %collective-permute-start.36 = (bf16[72,4608]{1,0:T(8,128)(2,1)}, bf16[72,4608]{1,0:T(8,128)(2,1)}, u32[]{:S(2)}, u32[]{:S(2)}) collective-permute-start(bf16[72,4608]{1,0:T(8,128)(2,1)} %get-tuple-element.171), channel_id=1, source_target_pairs={{0,8},{4,12},{8,0},{12,4},{16,24},{20,28},{24,16},{28,20},{1,9},{5... | collective-permute-start | bytes 1990664 | tf_op jit(solution)/shard_map/ppermute | solution.py:674
  310.3 180.1 %all-reduce.10.cloned.1.call-start = ((), (), s32[]{:S(2)}) async-start(), calls=%async_computation.7 | async-start | bytes 3317760 | tf_op jit(solution)/shard_map/psum | solution.py:758
  312.0 47.7 %collective-permute-start.39 = (bf16[72,1152]{1,0:T(8,128)(2,1)S(1)}, bf16[72,1152]{1,0:T(8,128)(2,1)S(1)}, u32[]{:S(2)}, u32[]{:S(2)}) collective-permute-start(bf16[72,1152]{1,0:T(8,128)(2,1)S(1)} %get-tuple-element.185), channel_id=1, source_target_pairs={{0,8},{4,12},{8,0},{12,4},{16,24},{20,28},{24,16},{28,20},{1,9},{5... | collective-permute-start | bytes 497672 | tf_op jit(solution)/shard_map/ppermute | solution.py:674
  319.2 54.6 %collective-permute-start.40 = (bf16[144,4608]{1,0:T(8,128)(2,1)}, bf16[144,4608]{1,0:T(8,128)(2,1)}, u32[]{:S(2)}, u32[]{:S(2)}) collective-permute-start(bf16[144,4608]{1,0:T(8,128)(2,1)} %pad_maximum_fusion.2), channel_id=1, source_target_pairs={{0,8},{4,12},{8,0},{12,4},{16,24},{20,28},{24,16},{28,20},{1,9},{5... | collective-permute-start | bytes 3981320 | tf_op jit(solution)/shard_map/ppermute | solution.py:674
  323.4 50.4 %collective-permute-start.41 = (bf16[144,4608]{1,0:T(8,128)(2,1)}, bf16[144,4608]{1,0:T(8,128)(2,1)}, u32[]{:S(2)}, u32[]{:S(2)}) collective-permute-start(bf16[144,4608]{1,0:T(8,128)(2,1)} %pad_maximum_fusion.3), channel_id=1, source_target_pairs={{0,16},{4,20},{8,24},{12,28},{16,0},{20,4},{24,8},{28,12},{1,17},{... | collective-permute-start | bytes 3981320 | tf_op jit(solution)/shard_map/ppermute | solution.py:674
  341.9 24.8 %collective-permute-start.42 = (bf16[512,896]{1,0:T(8,128)(2,1)}, bf16[512,896]{1,0:T(8,128)(2,1)S(1)}, u32[]{:S(2)}, u32[]{:S(2)}) collective-permute-start(bf16[512,896]{1,0:T(8,128)(2,1)} %get-tuple-element.126), channel_id=1, source_target_pairs={{0,4},{4,0},{8,12},{12,8},{16,20},{20,16},{24,28},{28,24},{1,5},{5... | collective-permute-start | bytes 2752520 | tf_op jit(solution)/shard_map/ppermute | solution.py:612
  359.1 7.6 %collective-permute-start.43 = (bf16[512,896]{1,0:T(8,128)(2,1)}, bf16[512,896]{1,0:T(8,128)(2,1)S(1)}, u32[]{:S(2)}, u32[]{:S(2)}) collective-permute-start(bf16[512,896]{1,0:T(8,128)(2,1)} %get-tuple-element.129), channel_id=1, source_target_pairs={{0,4},{4,0},{8,12},{12,8},{16,20},{20,16},{24,28},{28,24},{1,5},{5... | collective-permute-start | bytes 2752520 | tf_op jit(solution)/shard_map/ppermute | solution.py:612
  383.9 27.4 %collective-permute-start.46 = (bf16[4,144,3456]{2,1,0:T(8,128)(2,1)}, bf16[4,144,3456]{2,1,0:T(8,128)(2,1)}, u32[]{:S(2)}, u32[]{:S(2)}) collective-permute-start(bf16[4,144,3456]{2,1,0:T(8,128)(2,1)} %shard_map.261), channel_id=1, source_target_pairs={{0,4},{4,0},{8,12},{12,8},{16,20},{20,16},{24,28},{28,24},{1,5},{5... | collective-permute-start | bytes 11943944 | tf_op jit(solution)/shard_map/ppermute | solution.py:674
  384.9 10.3 %collective-permute-start.45 = (bf16[144,1152]{1,0:T(8,128)(2,1)S(1)}, bf16[144,1152]{1,0:T(8,128)(2,1)S(1)}, u32[]{:S(2)}, u32[]{:S(2)}) collective-permute-start(bf16[144,1152]{1,0:T(8,128)(2,1)S(1)} %copy-done.28), channel_id=1, source_target_pairs={{0,16},{4,20},{8,24},{12,28},{16,0},{20,4},{24,8},{28,12},{1,17},{... | collective-permute-start | bytes 995336 | tf_op jit(solution)/shard_map/ppermute | solution.py:674
  385.2 10.1 %collective-permute-start.44 = (bf16[144,1152]{1,0:T(8,128)(2,1)S(1)}, bf16[144,1152]{1,0:T(8,128)(2,1)}, u32[]{:S(2)}, u32[]{:S(2)}) collective-permute-start(bf16[144,1152]{1,0:T(8,128)(2,1)S(1)} %copy-done.29), channel_id=1, source_target_pairs={{0,8},{4,12},{8,0},{12,4},{16,24},{20,28},{24,16},{28,20},{1,9},{5... | collective-permute-start | bytes 995336 | tf_op jit(solution)/shard_map/ppermute | solution.py:674
  438.7 42.0 %collective-permute-start.48 = (bf16[72,3456]{1,0:T(8,128)(2,1)}, bf16[72,3456]{1,0:T(8,128)(2,1)}, u32[]{:S(2)}, u32[]{:S(2)}) collective-permute-start(bf16[72,3456]{1,0:T(8,128)(2,1)} %get-tuple-element.180), channel_id=1, source_target_pairs={{0,8},{4,12},{8,0},{12,4},{16,24},{20,28},{24,16},{28,20},{1,9},{5... | collective-permute-start | bytes 1493000 | tf_op jit(solution)/shard_map/ppermute | solution.py:674
  440.9 43.3 %collective-permute-start.47 = (bf16[72,3456]{1,0:T(8,128)(2,1)}, bf16[72,3456]{1,0:T(8,128)(2,1)}, u32[]{:S(2)}, u32[]{:S(2)}) collective-permute-start(bf16[72,3456]{1,0:T(8,128)(2,1)} %get-tuple-element.181), channel_id=1, source_target_pairs={{0,16},{4,20},{8,24},{12,28},{16,0},{20,4},{24,8},{28,12},{1,17},{... | collective-permute-start | bytes 1493000 | tf_op jit(solution)/shard_map/ppermute | solution.py:674
  442.6 13.1 %collective-permute-start.53 = (bf16[128,1152]{1,0:T(8,128)(2,1)}, bf16[128,1152]{1,0:T(8,128)(2,1)}, u32[]{:S(2)}, u32[]{:S(2)}) collective-permute-start(bf16[128,1152]{1,0:T(8,128)(2,1)} %get-tuple-element.190), channel_id=1, source_target_pairs={{0,0},{1,1},{4,2},{5,3},{6,4},{7,5},{2,6},{3,7},{8,8},{9,9},{12,10... | collective-permute-start | bytes 884744 | tf_op jit(solution)/shard_map/ppermute | solution.py:648
  447.3 8.4 %all-to-all-start.1 = ((f32[8,1,1152]{2,1,0:T(1,128)}), f32[8,1,1152]{2,1,0:T(1,128)S(1)}, u32[]{:S(2)}, u32[]{:S(2)}) async-start(f32[8,1,1152]{2,1,0:T(1,128)} %all_to_all.20), calls=%async_computation.1 | async-start | bytes 73728 | tf_op jit(solution)/shard_map/all_to_all | solution.py:958
  450.6 141.7 %all-reduce.8.cloned.1.call-start = ((), (), s32[]{:S(2)}) async-start(), calls=%async_computation.6 | async-start | bytes 2101248 | tf_op jit(solution)/shard_map/psum | solution.py:758
  450.7 37.0 %collective-permute-start.54 = (bf16[128,1152]{1,0:T(8,128)(2,1)}, bf16[128,1152]{1,0:T(8,128)(2,1)}, u32[]{:S(2)}, u32[]{:S(2)}) collective-permute-start(bf16[128,1152]{1,0:T(8,128)(2,1)} %get-tuple-element.189), channel_id=1, source_target_pairs={{1,0},{0,1},{5,2},{4,3},{7,4},{6,5},{3,6},{2,7},{9,8},{8,9},{13,10... | collective-permute-start | bytes 884744 | tf_op jit(solution)/shard_map/ppermute | solution.py:648
  450.9 37.8 %collective-permute-start.55 = (bf16[128,1152]{1,0:T(8,128)(2,1)}, bf16[128,1152]{1,0:T(8,128)(2,1)}, u32[]{:S(2)}, u32[]{:S(2)}) collective-permute-start(bf16[128,1152]{1,0:T(8,128)(2,1)} %get-tuple-element.188), channel_id=1, source_target_pairs={{4,0},{5,1},{0,2},{1,3},{2,4},{3,5},{6,6},{7,7},{12,8},{13,9},{8,1... | collective-permute-start | bytes 884744 | tf_op jit(solution)/shard_map/ppermute | solution.py:648
  455.8 54.3 %collective-permute-start.56 = (bf16[128,1152]{1,0:T(8,128)(2,1)S(1)}, bf16[128,1152]{1,0:T(8,128)(2,1)}, u32[]{:S(2)}, u32[]{:S(2)}) collective-permute-start(bf16[128,1152]{1,0:T(8,128)(2,1)S(1)} %get-tuple-element.187), channel_id=1, source_target_pairs={{5,0},{4,1},{1,2},{0,3},{3,4},{2,5},{7,6},{6,7},{13,8},{12,9},{9,1... | collective-permute-start | bytes 884744 | tf_op jit(solution)/shard_map/ppermute | solution.py:648
  483.1 21.2 %collective-permute-start.58 = (bf16[144,3456]{1,0:T(8,128)(2,1)}, bf16[144,3456]{1,0:T(8,128)(2,1)}, u32[]{:S(2)}, u32[]{:S(2)}) collective-permute-start(bf16[144,3456]{1,0:T(8,128)(2,1)} %pad_maximum_fusion.5), channel_id=1, source_target_pairs={{0,16},{4,20},{8,24},{12,28},{16,0},{20,4},{24,8},{28,12},{1,17},{... | collective-permute-start | bytes 2985992 | tf_op jit(solution)/shard_map/ppermute | solution.py:674
  486.4 20.7 %collective-permute-start.57 = (bf16[144,3456]{1,0:T(8,128)(2,1)}, bf16[144,3456]{1,0:T(8,128)(2,1)}, u32[]{:S(2)}, u32[]{:S(2)}) collective-permute-start(bf16[144,3456]{1,0:T(8,128)(2,1)} %pad_maximum_fusion.4), channel_id=1, source_target_pairs={{0,8},{4,12},{8,0},{12,4},{16,24},{20,28},{24,16},{28,20},{1,9},{5... | collective-permute-start | bytes 2985992 | tf_op jit(solution)/shard_map/ppermute | solution.py:674
  492.7 25.6 %collective-permute-start.49 = (bf16[128,1152]{1,0:T(8,128)(2,1)}, bf16[128,1152]{1,0:T(8,128)(2,1)}, u32[]{:S(2)}, u32[]{:S(2)}) collective-permute-start(bf16[128,1152]{1,0:T(8,128)(2,1)} %get-tuple-element.194), channel_id=1, source_target_pairs={{0,0},{1,1},{4,2},{5,3},{6,4},{7,5},{2,6},{3,7},{8,8},{9,9},{12,10... | collective-permute-start | bytes 884744 | tf_op jit(solution)/shard_map/ppermute | solution.py:648
  512.7 18.4 %collective-permute-start.50 = (bf16[128,1152]{1,0:T(8,128)(2,1)S(1)}, bf16[128,1152]{1,0:T(8,128)(2,1)S(1)}, u32[]{:S(2)}, u32[]{:S(2)}) collective-permute-start(bf16[128,1152]{1,0:T(8,128)(2,1)S(1)} %copy-done.37), channel_id=1, source_target_pairs={{1,0},{0,1},{5,2},{4,3},{7,4},{6,5},{3,6},{2,7},{9,8},{8,9},{13,10... | collective-permute-start | bytes 884744 | tf_op jit(solution)/shard_map/ppermute | solution.py:648
  512.7 24.5 %collective-permute-start.51 = (bf16[128,1152]{1,0:T(8,128)(2,1)S(1)}, bf16[128,1152]{1,0:T(8,128)(2,1)S(1)}, u32[]{:S(2)}, u32[]{:S(2)}) collective-permute-start(bf16[128,1152]{1,0:T(8,128)(2,1)S(1)} %copy-done.36), channel_id=1, source_target_pairs={{4,0},{5,1},{0,2},{1,3},{2,4},{3,5},{6,6},{7,7},{12,8},{13,9},{8,1... | collective-permute-start | bytes 884744 | tf_op jit(solution)/shard_map/ppermute | solution.py:648
  514.6 26.9 %collective-permute-start.52 = (bf16[128,1152]{1,0:T(8,128)(2,1)S(1)}, bf16[128,1152]{1,0:T(8,128)(2,1)S(1)}, u32[]{:S(2)}, u32[]{:S(2)}) collective-permute-start(bf16[128,1152]{1,0:T(8,128)(2,1)S(1)} %copy-done.35), channel_id=1, source_target_pairs={{5,0},{4,1},{1,2},{0,3},{3,4},{2,5},{7,6},{6,7},{13,8},{12,9},{9,1... | collective-permute-start | bytes 884744 | tf_op jit(solution)/shard_map/ppermute | solution.py:648
  514.7 16.2 %collective-permute-start.60 = (bf16[1,6912]{1,0:T(2,128)(2,1)S(1)}, bf16[1,6912]{1,0:T(2,128)(2,1)S(1)}, u32[]{:S(2)}, u32[]{:S(2)}) collective-permute-start(bf16[1,6912]{1,0:T(2,128)(2,1)S(1)} %broadcast_in_dim.72), channel_id=1, source_target_pairs={{0,1},{1,0},{2,3},{3,2},{4,5},{5,4},{6,7},{7,6},{8,9},{9,8},{10,11... | collective-permute-start | bytes 41480 | tf_op jit(solution)/shard_map/ppermute | solution.py:813
  548.0 11.1 %all-to-all-start.2 = ((f32[8,1,288]{2,1,0:T(1,128)}), f32[8,1,288]{2,1,0:T(1,128)S(1)}, u32[]{:S(2)}, u32[]{:S(2)}) async-start(f32[8,1,288]{2,1,0:T(1,128)} %all_to_all.22), calls=%async_computation.2 | async-start | bytes 24576 | tf_op jit(solution)/shard_map/all_to_all | solution.py:976
  (66 other events, 547.7 us)
Sparse Core Ops, SparseCore 0:
  65.6 68.2 all-gather.4
  135.8 73.0 all-gather.6
  310.4 58.5 all-reduce.5
  397.3 93.0 all-reduce.9
  541.8 50.5 all-reduce.7

commit v3 on v2

--- a/solution.py
+++ b/solution.py
@@ -27,8 +27,14 @@
 BLOCK = 512
 PAD = 128
 ROOT = 0.7978845608028654
+EARLY = 0.6
 VMEM_ATT = 48
-LIGHT = pl.CostEstimate(flops=0, bytes_accessed=0, transcendentals=0)
+
+
+def lasts(microseconds):
+    return pl.CostEstimate(
+        flops=int(EARLY * microseconds * 1e9), bytes_accessed=int(EARLY * microseconds * 3.3e6), transcendentals=0
+    )
 
 
 def shaped(shape, kind):
@@ -70,7 +76,7 @@
         in_specs=[SMEM, WHOLE],
         out_specs=(WHOLE,) * 2,
         compiler_params=params(48),
-        cost_estimate=LIGHT,
+        cost_estimate=lasts(2),
     )(core, *in_hbm(array))
 
 
@@ -97,7 +103,7 @@
         in_specs=[SMEM] + [WHOLE] * (2 * steps),
         out_specs=WHOLE,
         compiler_params=params(48),
-        cost_estimate=LIGHT,
+        cost_estimate=lasts(2),
     )(core, *in_hbm(*own, *got))
 
 
@@ -128,52 +134,51 @@
     return [slice(i, i + step) for i in range(0, rows, step)]
 
 
-def project_kernel(number, core, spots, tokens, mods, offset, *refs):
-    pieces = refs[:number]
-    mine, away, moved, whole, matrix, made, sems, out_sem = refs[number:]
-    width = made.shape[1]
+def project_kernel(core, tokens, mods, offset, matrix, mine, away, moved, made):
+    width = tokens.shape[1]
     half = width // 2
-    for at in row_chunks(tokens.shape[0]):
-        normed, _ = norm_rows(tokens[at, :].astype(f32))
-        moved[at, :] = (normed * (1.0 + mods[:, width : 2 * width]) + mods[:, :width]).astype(bf16)
-    assemble(spots, pieces, matrix, sems)
-    out = pltpu.make_async_copy(matrix, whole, out_sem)
-    out.start()
+
+    @pl.when(pl.program_id(0) == 0)
+    def _():
+        for at in row_chunks(tokens.shape[0]):
+            normed, _ = norm_rows(tokens[at, :].astype(f32))
+            moved[at, :] = (normed * (1.0 + mods[:, width : 2 * width]) + mods[:, :width]).astype(bf16)
+
+    made[...] = (dot(moved[...], matrix[...]) + offset[...]).astype(bf16)
     for kind in range(3):
-        at = slice(kind * width, (kind + 1) * width)
-        made[...] = (dot(moved[...], matrix[:, at]) + offset[:, at]).astype(bf16)
-
-        def work(c):
-            for ref, d in ((mine, c), (away, 1 - c)):
-                ref[:, kind * half : (kind + 1) * half] = made[:, d * half : (d + 1) * half]
-
-        on_core(core, work)
-    out.wait()
-
-
-def project(core, gathered, tokens, mods, offset):
-    spots, pieces = gathered
+
+        @pl.when(pl.program_id(0) == kind)
+        def _():
+            def work(c):
+                for ref, d in ((mine, c), (away, 1 - c)):
+                    ref[:, kind * half : (kind + 1) * half] = made[:, d * half : (d + 1) * half]
+
+            on_core(core, work)
+
+
+def project(core, matrix, tokens, mods, offset):
     rows, width = tokens.shape
-    wide = pieces[0].shape[1]
-    return pl.pallas_call(
-        functools.partial(project_kernel, len(pieces)),
+    wide = matrix.shape[1]
+    return pl.pallas_call(
+        project_kernel,
         out_shape=(
             shaped((rows, wide // 2), bf16),
             shaped((rows, lanes(wide // 2)), bf16),
             shaped((rows, width), bf16),
-            shaped((width, wide), bf16),
         ),
-        in_specs=[SMEM, SMEM, WHOLE, WHOLE, WHOLE] + [HBM] * len(pieces),
-        out_specs=(WHOLE, WHOLE, WHOLE, HBM),
-        scratch_shapes=[
-            pltpu.VMEM((width, wide), bf16),
-            pltpu.VMEM((rows, width), bf16),
-            pltpu.SemaphoreType.DMA((len(pieces),)),
-            pltpu.SemaphoreType.DMA,
+        grid=(3,),
+        in_specs=[
+            SMEM,
+            WHOLE,
+            WHOLE,
+            pl.BlockSpec((1, width), lambda i: (0, i)),
+            pl.BlockSpec((width, width), lambda i: (0, i)),
         ],
-        compiler_params=params(48),
-        cost_estimate=LIGHT,
-    )(core, spots, *in_hbm(tokens, mods, offset, *pieces))
+        out_specs=(WHOLE,) * 3,
+        scratch_shapes=[pltpu.VMEM((rows, width), bf16)],
+        compiler_params=params(48),
+        cost_estimate=lasts(13),
+    )(core, *in_hbm(tokens, mods, offset, matrix))
 
 
 def middle_kernel(number, core, spots, own, got, tokens, mods, offset, *refs):
@@ -223,46 +228,8 @@
             pltpu.SemaphoreType.DMA,
         ],
         compiler_params=params(48),
-        cost_estimate=LIGHT,
+        cost_estimate=lasts(9),
     )(core, spots, *in_hbm(own, got, tokens, mods, offset, *pieces))
-
-
-def pair_grad_kernel(add_got, where, left, right, *refs):
-    made = refs[-1]
-    half = left.shape[1] // 2
-    side = where[1]
-    for d in range(2):
-
-        @pl.when(side == d)
-        def _():
-            value = dot(left[:, d * half : (d + 1) * half], right[...], TN)
-            if add_got:
-                value = value + refs[0][0].astype(f32)
-            made[0] = value.astype(bf16)
-
-
-def pair_grad(left, right, b, side, got=None):
-    rows, wide = left.shape
-    step = wide // 4
-    where = jnp.stack([b >> 1, side]).astype(jnp.int32)
-    shape = (4, step // 2, right.shape[1])
-    block = pl.BlockSpec((1,) + shape[1:], lambda m, where: (m, 0, 0))
-    specs = [
-        pl.BlockSpec((rows, step), lambda m, where: (0, where[0] ^ m)),
-        pl.BlockSpec(right.shape, lambda m, where: (0, 0)),
-    ]
-    return pl.pallas_call(
-        functools.partial(pair_grad_kernel, got is not None),
-        out_shape=shaped(shape, bf16),
-        grid_spec=pltpu.PrefetchScalarGridSpec(
-            num_scalar_prefetch=1,
-            grid=(4,),
-            in_specs=specs + ([block] if got is not None else []),
-            out_specs=block,
-        ),
-        compiler_params=params(48),
-        cost_estimate=LIGHT,
-    )(where, *in_hbm(left, right, *([got] if got is not None else [])))
 
 
 def up_kernel(moved, matrix, offset, act, slope):
@@ -284,32 +251,54 @@
         in_specs=[WHOLE, pl.BlockSpec((width, step), lambda i: (0, i)), pl.BlockSpec((1, step), lambda i: (0, i))],
         out_specs=(pl.BlockSpec((rows, step), lambda i: (0, i)), pl.BlockSpec((rows, step), lambda i: (0, i))),
         compiler_params=params(48),
-        cost_estimate=LIGHT,
+        cost_estimate=lasts(16),
     )(*in_hbm(moved, matrix, offset))
 
 
-def slope_kernel(grad, matrix, slope, d_upper, sums):
+def slope_kernel(number, spots, grad, slope, *refs):
+    pieces = refs[:number]
+    d_upper, sums, whole, matrix, sems, out_sem = refs[number:]
+    step = pl.program_id(0)
+    size = sums.shape[1]
+    out = pltpu.make_async_copy(matrix, whole, out_sem)
+
+    @pl.when(step == 0)
+    def _():
+        assemble(spots, pieces, matrix, sems)
+        out.start()
+
+    part = matrix.at[pl.ds(pl.multiple_of(step * size, size), size)]
     total = jnp.zeros(sums.shape, f32)
     for at in row_chunks(grad.shape[0], 256):
-        value = (dot(grad[at, :], matrix[...], NT) * slope[at, :]).astype(bf16)
+        value = (dot(grad[at, :], part[...], NT) * slope[at, :]).astype(bf16)
         d_upper[at, :] = value
         total = total + jnp.sum(value.astype(f32), axis=0, keepdims=True)
     sums[...] = total
 
-
-def slope_part(grad, matrix, slope):
-    (rows, width), hidden = grad.shape, matrix.shape[0]
+    @pl.when(step == pl.num_programs(0) - 1)
+    def _():
+        out.wait()
+
+
+def slope_part(grad, gathered, slope):
+    spots, pieces = gathered
+    (rows, width), hidden = grad.shape, slope.shape[1]
     step = hidden // 4
     across = pl.BlockSpec((rows, step), lambda i: (0, i))
     return pl.pallas_call(
-        slope_kernel,
-        out_shape=(shaped((rows, hidden), bf16), shaped((1, hidden), f32)),
+        functools.partial(slope_kernel, len(pieces)),
+        out_shape=(shaped((rows, hidden), bf16), shaped((1, hidden), f32), shaped((hidden, width), bf16)),
         grid=(4,),
-        in_specs=[WHOLE, pl.BlockSpec((step, width), lambda i: (i, 0)), across],
-        out_specs=(across, pl.BlockSpec((1, step), lambda i: (0, i))),
-        compiler_params=params(48),
-        cost_estimate=LIGHT,
-    )(*in_hbm(grad, matrix, slope))
+        in_specs=[SMEM, WHOLE, across] + [HBM] * len(pieces),
+        out_specs=(across, pl.BlockSpec((1, step), lambda i: (0, i)), HBM),
+        scratch_shapes=[
+            pltpu.VMEM((hidden, width), bf16),
+            pltpu.SemaphoreType.DMA((len(pieces),)),
+            pltpu.SemaphoreType.DMA,
+        ],
+        compiler_params=params(48),
+        cost_estimate=lasts(40),
+    )(spots, *in_hbm(grad, slope, *pieces))
 
 
 def down_kernel(act, matrix, offset, tokens, projected, mods, grad, output, d_gate, total):
@@ -348,7 +337,7 @@
         out_specs=(WHOLE, WHOLE),
         scratch_shapes=[pltpu.VMEM((rows, width), f32)],
         compiler_params=params(48),
-        cost_estimate=LIGHT,
+        cost_estimate=lasts(6),
     )(*in_hbm(act, matrix, offset, tokens, projected, mods, grad))
 
 
@@ -406,7 +395,7 @@
         out_specs=(WHOLE,) * 5,
         scratch_shapes=[pltpu.VMEM((rows, width), f32)],
         compiler_params=params(48),
-        cost_estimate=LIGHT,
+        cost_estimate=lasts(150),
     )(core, *in_hbm(d_upper, matrix, normed, factor, projected, grad, mods, out_matrix))
 
 
@@ -448,13 +437,70 @@
         out_specs=(WHOLE, WHOLE, pl.BlockSpec((1, width), lambda i: (0, i))),
         scratch_shapes=[pltpu.VMEM((rows, width), f32)],
         compiler_params=params(48),
-        cost_estimate=LIGHT,
+        cost_estimate=lasts(40),
     )(*in_hbm(d_qkv, matrix, tokens, mods, d_middle))
 
 
-def block_grad_kernel(add_got, spots, left, right, *refs):
-    made, chosen, turned = refs[-3:]
-    rows = made.shape[1]
+def cut_of(rows):
+    return rows // 2 // 8 * 8
+
+
+def keep(made, e, value):
+    if len(made) == 1:
+        made[0][e] = value
+    elif e == 3 and len(made) == 5:
+        cut = made[3].shape[0]
+        made[3][...], made[4][...] = value[:cut], value[cut:]
+    else:
+        made[e][...] = value
+
+
+def pair_grad_kernel(added, where, left, right, *refs):
+    gots, made = refs[:added], refs[added:]
+    half = left.shape[1] // 2
+    step = pl.program_id(0)
+    for d in range(2):
+
+        @pl.when(where[1] == d)
+        def _():
+            value = dot(left[:, d * half : (d + 1) * half], right[...], TN)
+            for e in range(4):
+
+                @pl.when(step == e)
+                def _():
+                    more = gots[0][e].astype(f32) if added else 0.0
+                    keep(made, e, (value + more).astype(bf16))
+
+
+def grad_shapes(rows, columns, added):
+    cut = cut_of(rows)
+    return [(rows, columns)] * 3 + [(cut, columns), (rows - cut, columns)] if added else [(4, rows, columns)]
+
+
+def pair_grad(left, right, b, side, gots=()):
+    slots, wide = left.shape
+    step = wide // 4
+    where = jnp.stack([b >> 1, side]).astype(jnp.int32)
+    shapes = grad_shapes(step // 2, right.shape[1], len(gots))
+    whole = lambda shape: pl.BlockSpec(shape, lambda m, where: (0,) * len(shape))
+    specs = [pl.BlockSpec((slots, step), lambda m, where: (0, where[0] ^ m)), whole(right.shape)]
+    return pl.pallas_call(
+        functools.partial(pair_grad_kernel, len(gots)),
+        out_shape=tuple(shaped(shape, bf16) for shape in shapes),
+        grid_spec=pltpu.PrefetchScalarGridSpec(
+            num_scalar_prefetch=1,
+            grid=(4,),
+            in_specs=specs + [whole(got.shape) for got in gots],
+            out_specs=tuple(whole(shape) for shape in shapes),
+        ),
+        compiler_params=params(48),
+        cost_estimate=lasts(9),
+    )(where, *in_hbm(left, right, *gots))
+
+
+def block_grad_kernel(added, spots, left, right, *refs):
+    gots, made, (chosen, turned) = refs[:added], refs[added:-2], refs[-2:]
+    rows = made[0].shape[-2]
 
     @pl.when(pl.program_id(0) == 0)
     def _():
@@ -466,27 +512,51 @@
     value = dot(chosen[...], right[...])
     for e in range(4):
         part = value[e * rows : (e + 1) * rows, :]
-        if add_got:
-            part = part + refs[0][e].astype(f32)
-        made[e] = part.astype(bf16)
-
-
-def block_grad(left, right, b, side, got=None):
+        if added:
+            part = part + gots[0][e].astype(f32)
+        keep(made, e, part.astype(bf16))
+
+
+def block_grad(left, right, b, side, gots=()):
     (slots, wide), columns = left.shape, right.shape[1]
     rows = wide // 8
     spots = jnp.stack([((b >> 1) ^ m) * 2 * rows + side * rows for m in range(4)]).astype(jnp.int32)
     step = 1152 if columns % 1152 == 0 else columns
-    block = pl.BlockSpec((4, rows, step), lambda i: (0, 0, i))
-    return pl.pallas_call(
-        functools.partial(block_grad_kernel, got is not None),
-        out_shape=shaped((4, rows, columns), bf16),
+    shapes = grad_shapes(rows, columns, len(gots))
+    block = lambda shape: pl.BlockSpec(shape[:-1] + (step,), lambda i: (0,) * (len(shape) - 1) + (i,))
+    return pl.pallas_call(
+        functools.partial(block_grad_kernel, len(gots)),
+        out_shape=tuple(shaped(shape, bf16) for shape in shapes),
         grid=(columns // step,),
-        in_specs=[SMEM, WHOLE, pl.BlockSpec((slots, step), lambda i: (0, i))] + ([block] if got is not None else []),
-        out_specs=block,
+        in_specs=[SMEM, WHOLE, pl.BlockSpec((slots, step), lambda i: (0, i))] + [block(got.shape) for got in gots],
+        out_specs=tuple(block(shape) for shape in shapes),
         scratch_shapes=[pltpu.VMEM((4 * rows, slots), bf16), pltpu.VMEM((wide, slots), bf16)],
         compiler_params=params(48),
-        cost_estimate=LIGHT,
-    )(spots, *in_hbm(left, right, *([got] if got is not None else [])))
+        cost_estimate=lasts(columns // 1152),
+    )(spots, *in_hbm(left, right, *gots))
+
+
+def mix_kernel(to_x, to_y, got_x, got_y, out_x, out_y):
+    cut = got_x.shape[0]
+    out_x[:cut, :] = to_x[:cut, :]
+    out_x[cut:, :] = add(to_x[cut:, :], got_y[...])
+    out_y[:cut, :] = add(to_y[:cut, :], got_x[...])
+    out_y[cut:, :] = to_y[cut:, :]
+
+
+def mix(to_x, to_y, got_x, got_y):
+    rows, columns = to_x.shape
+    step = 1152
+    block = lambda array: pl.BlockSpec((array.shape[0], step), lambda i: (0, i))
+    return pl.pallas_call(
+        mix_kernel,
+        out_shape=(shaped(to_x.shape, bf16),) * 2,
+        grid=(columns // step,),
+        in_specs=[block(array) for array in (to_x, to_y, got_x, got_y)],
+        out_specs=(block(to_x),) * 2,
+        compiler_params=params(48),
+        cost_estimate=lasts(1),
+    )(*in_hbm(to_x, to_y, got_x, got_y))
 
 
 def fill(h, heads, mine, theirs, qs, ks, vs):
@@ -548,7 +618,7 @@
             pltpu.VMEM((total, 1), f32),
         ],
         compiler_params=params(VMEM_ATT),
-        cost_estimate=LIGHT,
+        cost_estimate=lasts(27),
     )(limits, *in_hbm(mine, theirs))
 
 
@@ -603,7 +673,7 @@
             pltpu.VMEM((total, HEAD), f32),
         ],
         compiler_params=params(VMEM_ATT),
-        cost_estimate=LIGHT,
+        cost_estimate=lasts(17),
     )(limits, *in_hbm(mine, theirs, d_mine, d_theirs, lse))
 
 
@@ -612,57 +682,29 @@
     return lax.ppermute(array, "batch", [(i, i ^ 1) for i in range(size)])
 
 
-def deal_pairs(turn, back=False):
-    pairs = []
-    seq = lax.axis_size("seq")
-    for b in range(lax.axis_size("batch")):
-        for s in range(seq):
-            j = (s ^ turn) & 1
-            dc = ((s >> 1) ^ (turn >> 1)) & 1
-            here, there = b * seq + s, (b ^ dc) * seq + 2 * (b & 1) + j
-            pairs.append((there, here) if back else (here, there))
-    return pairs
-
-
-def place_of(turn):
-    b, s = lax.axis_index("batch"), lax.axis_index("seq")
-    j = (s ^ turn) & 1
-    half = (b ^ (s >> 1) ^ (turn >> 1)) & 1
-    return j, half
+def by_core(own, other):
+    first = (lax.axis_index("batch") & 1) == 0
+    return jnp.where(first, jnp.stack([own, other]), jnp.stack([other, own]))
 
 
 def deal(array):
-    half = array.shape[1] // 2
-    parts = []
-    for turn in range(4):
-        j, c = place_of(turn)
-        piece = lax.dynamic_slice(array, (j, c * half, 0), (1, half, array.shape[2]))[0]
-        parts.append(lax.ppermute(piece, ("batch", "seq"), deal_pairs(turn)))
-    return jnp.concatenate(parts, axis=0)
+    c = lax.axis_index("batch") & 1
+    samples, slots, width = array.shape
+    halves = array.reshape(samples, 2, slots // 2, width)
+    own = lax.dynamic_index_in_dim(halves, c, axis=1, keepdims=False)
+    other = pair_swap(lax.dynamic_index_in_dim(halves, 1 - c, axis=1, keepdims=False))
+    every = by_core(own, other).reshape(2 * samples, slots // 2, width)
+    return lax.all_to_all(every, "seq", 0, 0, tiled=True).reshape(samples * slots, width)
 
 
 def undeal(array):
-    half = array.shape[0] // 4
-    out = jnp.zeros((2, 2 * half, array.shape[1]), array.dtype)
-    for turn in range(4):
-        got = lax.ppermute(array[turn * half : (turn + 1) * half], ("batch", "seq"), deal_pairs(turn, True))
-        j, c = place_of(turn)
-        out = lax.dynamic_update_slice(out, got[None], (j, c * half, 0))
-    return out
-
-
-def norm_forward(values):
-    centre = values - jnp.mean(values, axis=-1, keepdims=True)
-    factor = lax.rsqrt(jnp.mean(centre * centre, axis=-1, keepdims=True) + 1e-06)
-    return centre * factor, factor
-
-
-def norm_back(grad, normed, factor):
-    return factor * (
-        grad
-        - jnp.mean(grad, axis=-1, keepdims=True)
-        - normed * jnp.mean(grad * normed, axis=-1, keepdims=True)
-    )
+    c = lax.axis_index("batch") & 1
+    rows, width = array.shape
+    every = lax.all_to_all(array.reshape(4, rows // 4, width), "seq", 0, 0, tiled=True)
+    every = every.reshape(2, 2, rows // 4, width)
+    own = lax.dynamic_index_in_dim(every, c, axis=0, keepdims=False)
+    other = pair_swap(lax.dynamic_index_in_dim(every, 1 - c, axis=0, keepdims=False))
+    return by_core(own, other).transpose(1, 0, 2, 3).reshape(2, rows // 2, width)
 
 
 def gather(array):
@@ -684,15 +726,21 @@
         else:
             self.moving = self.along_x, self.along_y = hop(array, 2), hop(array, 4)
 
+    def turn(self, *done):
+        if self.plain:
+            return self.moving
+        self.cut = self.array.shape[0] // 2 // 16 * 16
+        self.along_x, self.along_y = after((self.along_x, self.along_y), *done)
+        self.corner = hop(self.along_x[: self.cut], 4), hop(self.along_y[self.cut :], 2)
+        self.moving = self.along_x, self.along_y, *self.corner
+        return self.moving
+
     def pieces(self, *done):
         if self.plain:
             return jnp.zeros((1,), jnp.int32), [self.whole]
-        rows = self.array.shape[0]
-        cut = rows // 2 // 16 * 16
+        rows, cut = self.array.shape[0], self.cut
         b = lax.axis_index("batch")
-        along_x, along_y = after((self.along_x, self.along_y), *done)
-        corner = hop(along_x[:cut], 4), hop(along_y[cut:], 2)
-        self.moving = along_x, along_y, *corner
+        along_x, along_y, *corner = after(self.moving, *done)
         pieces = [(0, 0, self.array), (2, 0, along_x), (4, 0, along_y), (6, 0, corner[0]), (6, cut, corner[1])]
         pieces += [(bits ^ 1, at, hop(piece, 1)) for bits, at, piece in pieces]
         spots = jnp.stack([(b ^ bits) * rows + at for bits, at, _ in pieces]).astype(jnp.int32)
@@ -720,7 +768,7 @@
         self.left = after(self.left, *done)
         b = lax.axis_index("batch")
         made = (pair_grad if self.paired else block_grad)(self.left, self.right, b, 1 - (b & 1))
-        self.got = hop(made, 1)
+        self.gots = [hop(made[0], 1)]
         return made
 
     def stay(self, *done):
@@ -730,23 +778,18 @@
             return self.part
         self.left = after(self.left, *done)
         b = lax.axis_index("batch")
-        made = (pair_grad if self.paired else block_grad)(self.left, self.right, b, b & 1, self.got)
-        both = made.reshape(4 * self.rows, -1)
-        rows, cut = self.rows, self.rows // 2 // 8 * 8
-        self.own, self.to_x, self.to_y, corner = (both[i * rows : (i + 1) * rows] for i in range(4))
-        self.cut = cut
-        self.got_x, self.got_y = hop(corner[:cut], 2), hop(corner[cut:], 4)
+        made = (pair_grad if self.paired else block_grad)(self.left, self.right, b, b & 1, self.gots)
+        self.own, self.to_x, self.to_y, corner_x, corner_y = made
+        self.got_x, self.got_y = hop(corner_x, 2), hop(corner_y, 4)
         return made
 
     def mix(self, *done):
         if self.plain:
             return self.part
-        cut = self.cut
         to_x, to_y = after((self.to_x, self.to_y), *done)
-        to_y = jnp.concatenate([add(to_y[:cut], self.got_x), to_y[cut:]], axis=0)
-        to_x = jnp.concatenate([to_x[:cut], add(to_x[cut:], self.got_y)], axis=0)
-        self.got_x, self.got_y = hop(to_x, 2), hop(to_y, 4)
-        return to_x, to_y
+        made = mix(to_x, to_y, self.got_x, self.got_y)
+        self.got_x, self.got_y = hop(made[0], 2), hop(made[1], 4)
+        return made
 
     def finish(self, *done, extra=None):
         if self.plain:
@@ -811,6 +854,10 @@
     rows = row[None]
     for bit in (1, 2):
         rows = jnp.concatenate([rows, lax.ppermute(rows, "seq", [(i, i ^ bit) for i in range(4)])], axis=0)
+    return rows
+
+
+def all_pairs(rows):
     bits = 2
     while bits < lax.axis_size("batch"):
         rows = jnp.concatenate([rows, hop(rows, bits)], axis=0)
@@ -858,7 +905,8 @@
     upstream16 = deal(cotangent)
 
     core = jnp.reshape(c, (1,)).astype(jnp.int32)
-    qkv_hops = Hops(qkv_weight)
+    qkv_matrix = gather(qkv_weight)
+    out_hops = Hops(out_weight)
 
     small = [conds.reshape(-1), qv_bias, out_bias, up_bias, down_bias, heights.astype(bf16), widths.astype(bf16)]
     spots = [sum(e.size for e in small[:i]) for i in range(len(small) + 1)]
@@ -875,29 +923,26 @@
     silu_rows = lax.dynamic_slice(silu_all, (0, b * rows), (2 * devices, rows))
     plane = lax.dynamic_index_in_dim(silu_rows.reshape(devices // 2, 4, rows), s, axis=1, keepdims=False)
     partial = dot(plane, mod_weight)
-    qkv_pieces = qkv_hops.pieces(partial, tokens16)
-    out_pieces = Hops(after(out_weight, qkv_hops.moving)).pieces()
-    up_matrix = gather(after(up_weight, qkv_hops.moving))
     own_bias = lax.dynamic_update_slice(jnp.zeros((mods,), f32), mod_bias.astype(f32), (b * mod_bias.shape[0],))
     partial = partial + own_bias[None]
     partial = jnp.broadcast_to(partial[:, None], (devices // 2, 2, mods)).reshape(devices, mods)
     modulation = jnp.sum(lax.all_to_all(partial, "batch", 0, 0, tiled=True), axis=0, keepdims=True)
-    shift1, scale1, gate1, shift2, scale2, gate2 = jnp.split(modulation, 6, axis=-1)
-
-    limits = []
-    for part in range(2):
-        side = c ^ part
-        base = (s & 1) | (((s >> 1) ^ side) << 1)
-        for turn in range(4):
-            limits.append(count - (slot_dev * (base ^ turn) + half * side))
+    gate2 = modulation[:, 5 * width :]
+    out_hops.turn(modulation)
+    tokens16 = after(tokens16, out_hops.moving)
+    out_pieces = out_hops.pieces()
+    up_matrix = gather(after(up_weight, modulation))
+
+    limits = [count - (slot_dev * i + half * (c ^ part)) for part in range(2) for i in range(4)]
     limits = jnp.stack(limits).astype(jnp.int32)
 
     offsets = jnp.concatenate([qv_offset[:width], jnp.zeros((width,), f32), qv_offset[width:]])
-    mine, away, moved, qkv_matrix = project(core, qkv_pieces, tokens16, modulation, offsets[None])
+    mine, away, moved = project(core, qkv_matrix, tokens16, modulation, offsets[None])
     theirs = pair_swap(away)
-    down_matrix = gather(after(down_weight, mine))
-    att_mine, att_away, lse = attend(limits, mine, theirs)
-    att_mine = after(att_mine, upstream16)
+    down_hops = Hops(after(down_weight, mine))
+    att_mine, att_away, lse = attend(limits, after(mine, out_pieces[1]), theirs)
+    down_hops.turn(att_mine)
+    down_pieces = down_hops.pieces()
     attended, projected, normed2, factor2, moved2, out_matrix = middle_part(
         core, out_pieces, att_mine, pair_swap(att_away), tokens16, modulation, out_offset[None]
     )
@@ -907,22 +952,24 @@
     down_offset_grad = jnp.sum(d_lowered.astype(f32), axis=0)
     down_g = Grad(act, d_lowered, True)
     mark = down_g.away(act)
-    d_upper, up_sums = slope_part(after(d_lowered, mark), down_matrix, slope)
+    d_upper, up_sums, down_matrix = slope_part(after(d_lowered, mark), down_pieces, slope)
     mark = down_g.stay(d_upper)
+    output, d_gate2 = down_part(
+        after(act, mark), down_matrix, down_offset[None], tokens16, projected, modulation, upstream16
+    )
     up_g = Grad(moved2, d_upper)
-    mark = up_g.away(mark)
+    mark = up_g.away(output)
     mark = down_g.mix(mark)
     d_middle, d_projected, d_att_mine, d_att_away, sums2 = middle_back(
         core, after(d_upper, mark), up_matrix, normed2, factor2, projected, upstream16, modulation, out_matrix
     )
     d_shift2, d_scale2, d_gate1, out_offset_grad = sums2
     d_att_theirs = pair_swap(d_att_away)
-    mark = up_g.stay(d_att_mine)
+    output = undeal(output)
+    mark, down_total = down_g.finish(d_att_mine)
+    mark = up_g.stay(mark, output)
     out_g = Grad(attended, d_projected)
     mark = out_g.away(mark)
-    mark = out_g.stay(mark)
-    mark, down_total = down_g.finish(mark)
-    mark = up_g.mix(mark)
     heads = HEADS // 2
     steps = 2
     own, got = [], []
@@ -933,13 +980,14 @@
         own.append(made[0])
         got.append(pair_swap(made[1]))
         mark = made
-    mark = out_g.mix(mark)
-    up_part_sum, up_total = up_g.finish(mark, down_total)
-    mark = up_part_sum
+        if i == 0:
+            mark = up_g.mix(mark)
+            mark = out_g.stay(mark)
+    mark, up_total = up_g.finish(mark, down_total)
     d_qkv = join_heads(core, own, got)
     qkv_g = Grad(moved, d_qkv)
     mark = qkv_g.away(mark)
-    mark, out_total = out_g.finish(mark, down_total)
+    mark = out_g.mix(mark)
     input_grad, sums1, column_sums = input_back(after(d_qkv, mark), qkv_matrix, tokens16, modulation, d_middle)
     d_shift1, d_scale1 = sums1
     mark = qkv_g.stay(input_grad)
@@ -957,17 +1005,14 @@
     length = bias.shape[1]
     bias = jnp.sum(lax.all_to_all(bias, "batch", 0, 0, tiled=True), axis=0, keepdims=True)
     bias = jnp.pad(bias, ((0, 7), (0, 3 * width - length)))
-    output, d_gate2 = down_part(
-        after(act, mark), down_matrix, down_offset[None], tokens16, projected, modulation, upstream16
-    )
-    mark = qkv_g.mix(output)
-    output = undeal(after(output, mark))
-    mark, qkv_total = qkv_g.finish(mark, up_total, out_total, extra=bias)
-
     partial_mod = jnp.concatenate([d_shift1, d_scale1, d_gate1, d_shift2, d_scale2, d_gate2[0]])
     partial_mod = after(partial_mod, mark)
     d_mod = (partial_mod + pair_swap(partial_mod)).astype(bf16)
-    d_mod_all = all_samples(d_mod)
+    d_mod_four = all_samples(d_mod)
+    mark = qkv_g.mix(bias, d_mod_four)
+    d_mod_all = all_pairs(after(d_mod_four, mark))
+    mark, _ = out_g.finish(mark, up_total)
+    mark, _ = qkv_g.finish(mark, up_total, extra=bias)
     mod_grad = dot(xor_order(silu_rows, sample), d_mod_all, TN)
     mod_offset_grad = jnp.sum(
         lax.dynamic_slice(d_mod_all, (0, b * mod_bias.shape[0]), (2 * devices, mod_bias.shape[0])).astype(f32), axis=0

time: 614 us -> 569 us (0.927)
  starting transfers between devices: 105 us -> 62.7 us
  local copies, waits for them, and re-layouts: 60.8 us -> 30 us
  Pallas kernels: 224 us -> 240 us
  waiting for transfers between devices: 137 us -> 152 us
  other arithmetic: 36.3 us -> 29.7 us
    ppermute x16 -> x0, starting transfers between devices: 53.3 us -> none  [the longest x8 36.2 us: undeal(): lax.ppermute(array[turn * half:(turn + 1) * half], ('batch', 'seq'), deal...]
    psum x3, waiting for transfers between devices: 33.1 us -> 59.1 us  [finish(): total = lax.psum(part, 'seq')]
    slice x22 -> x5, local copies, waits for them, and re-layouts: 23.9 us -> 5.51 us  [the longest x2 2.72 us: turn(): self.along_x[:self.cut]]
    pallas_call x10 -> x14, Pallas kernels: 85.6 us -> 104 us  [the longest x6 40 us: block_grad(): pl.pallas_call(functools.partial(block_grad_kernel, len(gots)), out_shape...]
    ppermute x2, waiting for transfers between devices: 16.3 us -> 0.01 us  [all_samples(): lax.ppermute(rows, 'seq', [(i, i ^ bit) for i in range(4)])]
    all_to_all x1 -> x4, starting transfers between devices: 3.4 us -> 18.6 us  [the longest x2 9.47 us: deal(): lax.all_to_all(every, 'seq', 0, 0, tiled=True)]
    ppermute x40, waiting for transfers between devices: 64.7 us -> 78.3 us  [hop(): return lax.ppermute(array, 'batch', [(i, i ^ bits) for i in range(size)])]
    all_to_all x0 -> x1, blocking collectives: none -> 11.8 us  [body(): lax.all_to_all(partial, 'batch', 0, 0, tiled=True)]
  transfers between devices with their start and end apart: 72 -> 63, of which waited for: 21 -> 23; matrix products, arithmetic and copies ran while one was open for 14% -> 9% of each run, Pallas kernels for 33% -> 39%
where the time goes in v3:
time: 569 us; the launch traced here: 561 us
  Pallas kernels  240 us (42%)
  waiting for transfers between devices  152 us (27%)
  starting transfers between devices  62.7 us (11%)
  local copies, waits for them, and re-layouts  30 us (5%)
  other arithmetic  29.7 us (5%)
  blocking collectives  22.5 us (4%)
  between operations  20 us (4%)
    ppermute x40, waiting for transfers between devices, hop(): return lax.ppermute(array, 'batch', [(i, i ^ bits) for i in range(size)])  78.3 us
    psum x3, waiting for transfers between devices, finish(): total = lax.psum(part, 'seq')  59.1 us
    pallas_call x6, Pallas kernels, block_grad(): pl.pallas_call(functools.partial(block_grad_kernel, len(gots)), out_shape...  40 us
    pallas_call x2, Pallas kernels, attend_back(): pl.pallas_call(functools.partial(back_kernel, heads, first, number), out_...  34 us
    ppermute x40, starting transfers between devices, hop(): return lax.ppermute(array, 'batch', [(i, i ^ bits) for i in range(size)])  31 us
    pallas_call x1, Pallas kernels, attend(): pl.pallas_call(functools.partial(attend_kernel, heads), out_shape=(shaped...  27.2 us
    pallas_call x2, Pallas kernels, pair_grad(): pl.pallas_call(functools.partial(pair_grad_kernel, len(gots)), out_shape=...  20.9 us
    pallas_call x1, Pallas kernels, middle_back(): pl.pallas_call(middle_back_kernel, out_shape=(shaped((rows, width), f32),...  18.7 us
  transfers between devices with their start and end apart: 63, of which 23 were waited for; matrix products, arithmetic and copies ran while one was open for 9% of the time, Pallas kernels for 39%

profile of v3, /device:TPU:0, one launch (start us, length us, event | category | flops | bytes accessed | tf_op | source)
XLA Modules:
  0.0 561.2 jit_solution(13587723505755294735)
XLA Ops:
  10.0 2.8 concatenate.37
  12.8 10.7 %all-gather.1 = bf16[8,1,3584]{2,1,0:T(2,128)(2,1)S(1)} all-gather(bf16[1,1,3584]{2,1,0:T(2,128)(2,1)S(1)} %reshape.215), channel_id=2, replica_groups=mesh['batch'=8,'seq'=4] {'batch'}, dimensions={0}, use_global_device_ids=true | all-gather | bytes 64512 | tf_op jit(solution)/shard_map/all_gather | solution.py:711
  24.7 11.8 %all_to_all.47 = f32[8,1,6912]{2,1,0:T(1,128)S(1)} all-to-all(f32[8,1,6912]{2,1,0:T(1,128)S(1)} %all_to_all.31), channel_id=1, replica_groups=mesh['batch'=8,'seq'=4] {'batch'}, dimensions={0} | all-to-all | bytes 442368 | tf_op jit(solution)/shard_map/all_to_all | solution.py:929
  37.3 2.2 dynamic-slice_bitcast_fusion.7
  39.4 2.2 collective-permute-done
  43.0 4.9 all-to-all-start
  48.9 16.6 %collective-permute-done.1.refs_1_ = bf16[144,1152]{1,0:T(8,128)(2,1)} collective-permute-done((bf16[144,1152]{1,0:T(8,128)(2,1)}, bf16[144,1152]{1,0:T(8,128)(2,1)}, u32[]{:S(2)}, u32[]{:S(2)}) %collective-permute-start.1) | collective-permute-done | bytes 331808 | tf_op jit(solution)/shard_map/ppermute | solution.py:716
  66.5 2.0 collective-permute-start.4
  71.4 4.6 collective-permute-done.3.refs_3_
  78.2 11.7 %shard_map.246 = (bf16[512,1728]{1,0:T(8,128)(2,1)}, bf16[512,1792]{1,0:T(8,128)(2,1)}, bf16[512,1152]{1,0:T(8,128)(2,1)}) custom-call(s32[1]{0:T(128)} %bitcast.core, bf16[512,1152]{1,0:T(8,128)(2,1)} %bitcast.103, f32[1,6912]{1,0:T(1,128)} %broadcast_in_dim.35.mods, f32[1,3456]{1,0:T(1,128)} %broadcast_in_dim.37.offset, ...), custom_call_target="tpu_custom_call" | custom-call | flops 7800000000 | bytes 25740000 | tf_op jit(solution)/shard_map/pallas_call | solution.py:162
  91.5 3.9 collective-permute-done.12
  96.9 4.6 all-to-all-start.2
  109.2 27.2 %shard_map.247 = (bf16[512,576]{1,0:T(8,128)(2,1)}, bf16[512,640]{1,0:T(8,128)(2,1)}, f32[8,1024]{1,0:T(8,128)}) custom-call(s32[8]{0:T(128)S(1)} %stack.228.limits, bf16[512,1728]{1,0:T(8,128)(2,1)} %get-tuple-element.192.mine, bf16[512,1792]{1,0:T(8,128)(2,1)} %collective-permute-done.10.theirs), custom_call_target="tpu_custom_call" | custom-call | flops 16199999488 | bytes 53460000 | tf_op jit(solution)/shard_map/pallas_call | solution.py:608
  141.1 9.3 %shard_map.248 = (bf16[512,1152]{1,0:T(8,128)(2,1)}, f32[512,1152]{1,0:T(8,128)}, f32[512,1152]{1,0:T(8,128)}, f32[512,1]{1,0:T(8,128)}, bf16[512,1152]{1,0:T(8,128)(2,1)}, /*index=5*/bf16[1152,1152]{1,0:T(8,128)(2,1)}) custom-call(s32[1]{0:T(128)} %bitcast.core, s32[10]{0:T(128)S(1)} %stack.219.spots, bf16[512,576]{1,0:T(8,128)(2,1)} %get-tuple-element.131.own, ...), custom_call_target="tpu_custom_call" | custom-call | flops 5400000000 | bytes 17820000 | tf_op jit(solution)/shard_map/pallas_call | solution.py:213
  150.5 16.2 %shard_map.249 = (bf16[512,4608]{1,0:T(8,128)(2,1)}, f32[512,4608]{1,0:T(8,128)}) custom-call(bf16[512,1152]{1,0:T(8,128)(2,1)} %get-tuple-element.169.moved.left, bf16[1152,4608]{1,0:T(8,128)(2,1)} %all-gather.7.cloned.1.call-done.matrix, f32[1,4608]{1,0:T(1,128)} %reshape.211.offset), custom_call_target="tpu_custom_call" | custom-call | flops 9600000000 | bytes 31680000 | tf_op jit(solution)/shard_map/pallas_call | solution.py:247
  166.7 9.7 %shard_map.250 = bf16[4,576,1152]{2,1,0:T(8,128)(2,1)} custom-call(s32[2]{0:T(128)S(1)} %pad_add_fusion.1.where, bf16[512,4608]{1,0:T(8,128)(2,1)} %get-tuple-element.153.left.act, bf16[512,1152]{1,0:T(8,128)(2,1)} %multiply_convert_fusion.1.right.grad), custom_call_target="tpu_custom_call" | custom-call | flops 5400000000 | bytes 17820000 | tf_op jit(solution)/shard_map/pallas_call | solution.py:487
  179.2 1.8 collective-permute-start.16
  181.0 14.0 %collective-permute-done.15.refs_3_ = bf16[288,1152]{1,0:T(8,128)(2,1)S(1)} collective-permute-done((bf16[288,1152]{1,0:T(8,128)(2,1)S(1)}, bf16[288,1152]{1,0:T(8,128)(2,1)S(1)}, u32[]{:S(2)}, u32[]{:S(2)}) %collective-permute-start.15) | collective-permute-done | bytes 663584 | tf_op jit(solution)/shard_map/ppermute | solution.py:716
  198.4 3.1 collective-permute-done.20.refs_8_
  201.5 2.1 collective-permute-done.21.refs_9_
  203.7 16.8 %shard_map.251 = (bf16[512,4608]{1,0:T(8,128)(2,1)}, f32[1,4608]{1,0:T(1,128)}, bf16[4608,1152]{1,0:T(8,128)(2,1)}) custom-call(s32[10]{0:T(128)S(1)} %stack.245.spots, bf16[512,1152]{1,0:T(8,128)(2,1)} %multiply_convert_fusion.1.right.grad, f32[512,4608]{1,0:T(8,128)} %get-tuple-element.138.slope, bf16[576,1152]{1,0:T(8,128)(2,1)} %refs_0_.2, ...), custom_call_target="tpu_custom_call" | custom-call | flops 24000000000 | bytes 79200000 | tf_op jit(solution)/shard_map/pallas_call | solution.py:288
  220.5 11.2 %shard_map.252 = (bf16[576,1152]{1,0:T(8,128)(2,1)}, bf16[576,1152]{1,0:T(8,128)(2,1)}, bf16[576,1152]{1,0:T(8,128)(2,1)}, bf16[288,1152]{1,0:T(8,128)(2,1)}, bf16[288,1152]{1,0:T(8,128)(2,1)}) custom-call(s32[2]{0:T(128)S(1)} %pad_add_fusion.where, bf16[512,4608]{1,0:T(8,128)(2,1)} %get-tuple-element.153.left.act, ...), custom_call_target="tpu_custom_call" | custom-call | flops 5400000000 | bytes 17820000 | tf_op jit(solution)/shard_map/pallas_call | solution.py:487
  231.7 1.7 collective-permute-start.24
  233.4 1.7 collective-permute-start.25
  235.2 13.4 %shard_map.253 = (bf16[512,1152]{1,0:T(8,128)(2,1)}, f32[1,1152]{1,0:T(1,128)}) custom-call(bf16[512,4608]{1,0:T(8,128)(2,1)} %get-tuple-element.153.left.act, bf16[4608,1152]{1,0:T(8,128)(2,1)} %get-tuple-element.154.matrix, f32[1,1152]{1,0:T(1,128)} %reshape.212.offset, bf16[512,1152]{1,0:T(8,128)(2,1)} %bitcast.105, ...), custom_call_target="tpu_custom_call" | custom-call | flops 3600000000 | bytes 11879999 | tf_op jit(solution)/shard_map/pallas_call | solution.py:331
  248.6 7.9 %shard_map.254 = bf16[4,144,4608]{2,1,0:T(8,128)(2,1)} custom-call(s32[4]{0:T(128)S(1)} %pad_add_fusion.2.spots, bf16[512,1152]{1,0:T(8,128)(2,1)} %get-tuple-element.169.moved.left, bf16[512,4608]{1,0:T(8,128)(2,1)} %get-tuple-element.163.right.d_upper), custom_call_target="tpu_custom_call" | custom-call | flops 2400000000 | bytes 7920000 | tf_op jit(solution)/shard_map/pallas_call | solution.py:527
  256.8 5.6 %all-to-all-start.3 = ((bf16[4,128,1152]{2,1,0:T(8,128)(2,1)}), bf16[4,128,1152]{2,1,0:T(8,128)(2,1)S(1)}, u32[]{:S(2)}, u32[]{:S(2)}) async-start(bf16[4,128,1152]{2,1,0:T(8,128)(2,1)} %bitcast.116), calls=%async_computation.3 | async-start | bytes 2359296 | tf_op jit(solution)/shard_map/all_to_all | solution.py:703
  262.4 3.8 shard_map.255
  266.9 18.7 %shard_map.256 = (f32[512,1152]{1,0:T(8,128)}, bf16[512,1152]{1,0:T(8,128)(2,1)}, bf16[512,576]{1,0:T(8,128)(2,1)}, bf16[512,640]{1,0:T(8,128)(2,1)}, f32[4,1152]{1,0:T(4,128)}) custom-call(s32[1]{0:T(128)} %bitcast.core, bf16[512,4608]{1,0:T(8,128)(2,1)} %get-tuple-element.163.right.d_upper, bf16[1152,4608]{1,0:T(8,128)(2,1)} %all-gather.7.cloned.1.call-done.matrix, ...), custom_call_target="tpu_custom_call" | custom-call | flops 89999998976 | bytes 297000000 | tf_op jit(solution)/shard_map/pallas_call | solution.py:383
  285.6 5.7 %all-to-all-done.3 = bf16[4,128,1152]{2,1,0:T(8,128)(2,1)S(1)} async-done(((bf16[4,128,1152]{2,1,0:T(8,128)(2,1)}), bf16[4,128,1152]{2,1,0:T(8,128)(2,1)S(1)}, u32[]{:S(2)}, u32[]{:S(2)}) %all-to-all-start.3) | async-done | bytes 1179680 | tf_op jit(solution)/shard_map/all_to_all | solution.py:703
  292.5 5.1 collective-permute-done.26
  297.6 3.3 add_convert_fusion.1
  302.2 9.1 %shard_map.257 = (bf16[144,4608]{1,0:T(8,128)(2,1)}, bf16[144,4608]{1,0:T(8,128)(2,1)}, bf16[144,4608]{1,0:T(8,128)(2,1)}, bf16[72,4608]{1,0:T(8,128)(2,1)}, bf16[72,4608]{1,0:T(8,128)(2,1)}) custom-call(s32[4]{0:T(128)S(1)} %pad_add_fusion.3.spots, bf16[512,1152]{1,0:T(8,128)(2,1)} %get-tuple-element.169.moved.left, ...), custom_call_target="tpu_custom_call" | custom-call | flops 2400000000 | bytes 7920000 | tf_op jit(solution)/shard_map/pallas_call | solution.py:527
  311.2 1.8 collective-permute-start.30
  313.1 4.1 shard_map.258
  317.3 17.0 %shard_map.259 = (bf16[512,864]{1,0:T(8,128)(2,1)}, bf16[512,896]{1,0:T(8,128)(2,1)}) custom-call(s32[8]{0:T(128)S(1)} %copy-done.2, bf16[512,1728]{1,0:T(8,128)(2,1)} %get-tuple-element.192.mine, bf16[512,1792]{1,0:T(8,128)(2,1)} %collective-permute-done.10.theirs, bf16[512,576]{1,0:T(8,128)(2,1)} %get-tuple-element.167.d_mine, ...), custom_call_target="tpu_custom_call" | custom-call | flops 10200000512 | bytes 33660000 | tf_op jit(solution)/shard_map/pallas_call | solution.py:661
  336.0 4.3 shard_map.260
  340.7 1.8 collective-permute-start.36
  343.8 4.3 shard_map.261
  348.1 17.0 %shard_map.262 = (bf16[512,864]{1,0:T(8,128)(2,1)}, bf16[512,896]{1,0:T(8,128)(2,1)}) custom-call(s32[8]{0:T(128)S(1)} %copy-done.2, bf16[512,1728]{1,0:T(8,128)(2,1)} %get-tuple-element.192.mine, bf16[512,1792]{1,0:T(8,128)(2,1)} %collective-permute-done.10.theirs, bf16[512,576]{1,0:T(8,128)(2,1)} %get-tuple-element.167.d_mine, ...), custom_call_target="tpu_custom_call" | custom-call | flops 10200000512 | bytes 33660000 | tf_op jit(solution)/shard_map/pallas_call | solution.py:661
  365.5 6.6 %collective-permute-done.35 = bf16[144,4608]{1,0:T(8,128)(2,1)} collective-permute-done((bf16[144,4608]{1,0:T(8,128)(2,1)}, bf16[144,4608]{1,0:T(8,128)(2,1)}, u32[]{:S(2)}, u32[]{:S(2)}) %collective-permute-start.35) | collective-permute-done | bytes 1327136 | tf_op jit(solution)/shard_map/ppermute | solution.py:716
  372.2 3.3 add_convert_fusion
  375.5 5.1 shard_map.263.right.d_qkv
  380.7 6.9 %shard_map.264 = bf16[4,144,3456]{2,1,0:T(8,128)(2,1)} custom-call(s32[4]{0:T(128)S(1)} %pad_add_fusion.2.spots, bf16[512,1152]{1,0:T(8,128)(2,1)} %get-tuple-element.205.left, bf16[512,3456]{1,0:T(8,128)(2,1)} %shard_map.263.right.d_qkv), custom_call_target="tpu_custom_call" | custom-call | flops 1800000000 | bytes 5939999 | tf_op jit(solution)/shard_map/pallas_call | solution.py:527
  387.7 1.7 collective-permute-start.37
  391.9 2.8 collective-permute-done.37.got_x
  395.9 2.2 shard_map.265
  398.1 12.5 %shard_map.266 = (bf16[512,1152]{1,0:T(8,128)(2,1)}, f32[2,1152]{1,0:T(2,128)}, f32[1,3456]{1,0:T(1,128)}) custom-call(bf16[512,3456]{1,0:T(8,128)(2,1)} %shard_map.263.right.d_qkv, bf16[1152,3456]{1,0:T(8,128)(2,1)} %all-gather.5.cloned.1.call-done.matrix, bf16[512,1152]{1,0:T(8,128)(2,1)} %bitcast.106, f32[1,6912]{1,0:T(1,128)} %broadcast_in_dim.35.mods, ...), custom_call_target="tpu_custom_call" | custom-call | flops 24000000000 | bytes 79200000 | tf_op jit(solution)/shard_map/pallas_call | solution.py:431
  412.3 7.9 %shard_map.267 = (bf16[144,3456]{1,0:T(8,128)(2,1)}, bf16[144,3456]{1,0:T(8,128)(2,1)}, bf16[144,3456]{1,0:T(8,128)(2,1)}, bf16[72,3456]{1,0:T(8,128)(2,1)}, bf16[72,3456]{1,0:T(8,128)(2,1)}) custom-call(s32[4]{0:T(128)S(1)} %pad_add_fusion.3.spots, bf16[512,1152]{1,0:T(8,128)(2,1)} %get-tuple-element.205.left, bf16[512,3456]{1,0:T(8,128)(2,1)} %shard_map.263.right.d_qkv, ...), custom_call_target="tpu_custom_call" | custom-call | flops 1800000000 | bytes 5939999 | tf_op jit(solution)/shard_map/pallas_call | solution.py:527
  423.8 3.3 all-to-all-start.5
  427.3 2.5 collective-permute-start.43
  429.8 1.9 collective-permute-start.48
  433.8 3.5 all-to-all-start.4
  437.6 12.9 %collective-permute-done.44.got_x = bf16[72,3456]{1,0:T(8,128)(2,1)} collective-permute-done((bf16[72,3456]{1,0:T(8,128)(2,1)}, bf16[72,3456]{1,0:T(8,128)(2,1)}, u32[]{:S(2)}, u32[]{:S(2)}) %collective-permute-start.44) | collective-permute-done | bytes 497696 | tf_op jit(solution)/shard_map/ppermute | solution.py:716
  451.9 3.9 shard_map.268
  456.2 1.7 collective-permute-start.50
  459.4 14.2 %all-reduce.8.cloned.1.call-done = bf16[144,4608]{1,0:T(8,128)(2,1)} async-done(((bf16[144,4608]{1,0:T(8,128)(2,1)}), bf16[144,4608]{1,0:T(8,128)(2,1)}) %all-reduce.8.cloned.1.call-update) | async-done | bytes 1327120 | tf_op jit(solution)/shard_map/psum | solution.py:801
  475.1 2.0 add_convert_fusion.3
  477.1 5.4 collective-permute-done.47
  484.2 2.2 add_convert_fusion.2
  488.1 3.3 all-to-all-start.6
  493.0 2.6 fusion.9
  497.5 1.8 convert_element_type.213
  503.2 44.9 %all-reduce.10.cloned.1.call-done = (bf16[152,3456]{1,0:T(8,128)(2,1)}, bf16[144,1152]{1,0:T(8,128)(2,1)}) async-done(((bf16[152,3456]{1,0:T(8,128)(2,1)}, bf16[144,1152]{1,0:T(8,128)(2,1)}), (bf16[152,3456]{1,0:T(8,128)(2,1)}, bf16[144,1152]{1,0:T(8,128)(2,1)})) %all-reduce.10.cloned.1.call-update) | async-done | bytes 1382416 | tf_op jit(solution)/shard_map/psum | solution.py:801
  (279 shorter events, 70.0 us)
Async XLA Ops:
  7.2 71.0 %all-gather.5.cloned.1.call-start = ((), (), s32[]{:S(2)}) async-start(), calls=%async_computation.7 | async-start | bytes 8957952 | tf_op jit(solution)/shard_map/all_gather | solution.py:711
  7.9 142.5 %all-gather.7.cloned.1.call-start = ((), (), s32[]{:S(2)}) async-start(), calls=%async_computation.8 | async-start | bytes 11943936 | tf_op jit(solution)/shard_map/all_gather | solution.py:711
  39.4 2.2 collective-permute-start
  43.0 33.9 %all-to-all-start = ((bf16[4,128,1152]{2,1,0:T(8,128)(2,1)}), bf16[4,128,1152]{2,1,0:T(8,128)(2,1)S(1)}, u32[]{:S(2)}, u32[]{:S(2)}) async-start(bf16[4,128,1152]{2,1,0:T(8,128)(2,1)} %bitcast.109), calls=%async_computation | async-start | bytes 2359296 | tf_op jit(solution)/shard_map/all_to_all | solution.py:697
  47.8 17.7 %collective-permute-start.1 = (bf16[144,1152]{1,0:T(8,128)(2,1)}, bf16[144,1152]{1,0:T(8,128)(2,1)}, u32[]{:S(2)}, u32[]{:S(2)}) collective-permute-start(bf16[144,1152]{1,0:T(8,128)(2,1)} %refs_0_.1), channel_id=1, source_target_pairs={{0,8},{4,12},{8,0},{12,4},{16,24},{20,28},{24,16},{28,20},{1,9},{5... | collective-permute-start | bytes 995336 | tf_op jit(solution)/shard_map/ppermute | solution.py:716
  47.8 17.7 %collective-permute-start.2 = (bf16[144,1152]{1,0:T(8,128)(2,1)}, bf16[144,1152]{1,0:T(8,128)(2,1)}, u32[]{:S(2)}, u32[]{:S(2)}) collective-permute-start(bf16[144,1152]{1,0:T(8,128)(2,1)} %refs_0_.1), channel_id=1, source_target_pairs={{0,16},{4,20},{8,24},{12,28},{16,0},{20,4},{24,8},{28,12},{1,17},{... | collective-permute-start | bytes 995336 | tf_op jit(solution)/shard_map/ppermute | solution.py:716
  66.5 10.4 %collective-permute-start.4 = (bf16[80,1152]{1,0:T(8,128)(2,1)S(1)}, bf16[80,1152]{1,0:T(8,128)(2,1)}, u32[]{:S(2)}, u32[]{:S(2)}) collective-permute-start(bf16[80,1152]{1,0:T(8,128)(2,1)S(1)} %slice.107), channel_id=1, source_target_pairs={{0,8},{4,12},{8,0},{12,4},{16,24},{20,28},{24,16},{28,20},{1,9},{5... | collective-permute-start | bytes 552968 | tf_op jit(solution)/shard_map/ppermute | solution.py:716
  70.0 6.0 %collective-permute-start.3 = (bf16[64,1152]{1,0:T(8,128)(2,1)}, bf16[64,1152]{1,0:T(8,128)(2,1)}, u32[]{:S(2)}, u32[]{:S(2)}) collective-permute-start(bf16[64,1152]{1,0:T(8,128)(2,1)} %slice.106), channel_id=1, source_target_pairs={{0,16},{4,20},{8,24},{12,28},{16,0},{20,4},{24,8},{28,12},{1,17},{... | collective-permute-start | bytes 442376 | tf_op jit(solution)/shard_map/ppermute | solution.py:716
  89.9 19.3 %collective-permute-start.10 = (bf16[512,1792]{1,0:T(8,128)(2,1)}, bf16[512,1792]{1,0:T(8,128)(2,1)}, u32[]{:S(2)}, u32[]{:S(2)}) collective-permute-start(bf16[512,1792]{1,0:T(8,128)(2,1)} %get-tuple-element.130), channel_id=1, source_target_pairs={{0,4},{4,0},{8,12},{12,8},{16,20},{20,16},{24,28},{28,24},{1,5},{5... | collective-permute-start | bytes 5505032 | tf_op jit(solution)/shard_map/ppermute | solution.py:682
  90.3 5.1 collective-permute-start.12
  90.6 11.0 %collective-permute-start.5 = (bf16[144,1152]{1,0:T(8,128)(2,1)}, bf16[144,1152]{1,0:T(8,128)(2,1)}, u32[]{:S(2)}, u32[]{:S(2)}) collective-permute-start(bf16[144,1152]{1,0:T(8,128)(2,1)} %refs_0_.1), channel_id=1, source_target_pairs={{0,4},{4,0},{8,12},{12,8},{16,20},{20,16},{24,28},{28,24},{1,5},{5... | collective-permute-start | bytes 995336 | tf_op jit(solution)/shard_map/ppermute | solution.py:716
  91.0 18.2 %collective-permute-start.6 = (bf16[144,1152]{1,0:T(8,128)(2,1)}, bf16[144,1152]{1,0:T(8,128)(2,1)}, u32[]{:S(2)}, u32[]{:S(2)}) collective-permute-start(bf16[144,1152]{1,0:T(8,128)(2,1)} %collective-permute-done.1.refs_1_), channel_id=1, source_target_pairs={{0,4},{4,0},{8,12},{12,8},{16,20},{20,16},{24,28},{28,24},{1,5},{5... | collective-permute-start | bytes 995336 | tf_op jit(solution)/shard_map/ppermute | solution.py:716
  91.3 18.0 %collective-permute-start.7 = (bf16[144,1152]{1,0:T(8,128)(2,1)}, bf16[144,1152]{1,0:T(8,128)(2,1)}, u32[]{:S(2)}, u32[]{:S(2)}) collective-permute-start(bf16[144,1152]{1,0:T(8,128)(2,1)} %collective-permute-done.2.refs_2_), channel_id=1, source_target_pairs={{0,4},{4,0},{8,12},{12,8},{16,20},{20,16},{24,28},{28,24},{1,5},{5... | collective-permute-start | bytes 995336 | tf_op jit(solution)/shard_map/ppermute | solution.py:716
  95.4 13.8 %collective-permute-start.9 = (bf16[80,1152]{1,0:T(8,128)(2,1)}, bf16[80,1152]{1,0:T(8,128)(2,1)S(1)}, u32[]{:S(2)}, u32[]{:S(2)}) collective-permute-start(bf16[80,1152]{1,0:T(8,128)(2,1)} %collective-permute-done.4.refs_4_), channel_id=1, source_target_pairs={{0,4},{4,0},{8,12},{12,8},{16,20},{20,16},{24,28},{28,24},{1,5},{5... | collective-permute-start | bytes 552968 | tf_op jit(solution)/shard_map/ppermute | solution.py:716
  96.9 40.8 %all-to-all-start.2 = ((bf16[4,128,1152]{2,1,0:T(8,128)(2,1)}), bf16[4,128,1152]{2,1,0:T(8,128)(2,1)S(1)}, u32[]{:S(2)}, u32[]{:S(2)}) async-start(bf16[4,128,1152]{2,1,0:T(8,128)(2,1)} %bitcast.107), calls=%async_computation.2 | async-start | bytes 2359296 | tf_op jit(solution)/shard_map/all_to_all | solution.py:697
  101.6 7.6 %collective-permute-start.8 = (bf16[64,1152]{1,0:T(8,128)(2,1)}, bf16[64,1152]{1,0:T(8,128)(2,1)}, u32[]{:S(2)}, u32[]{:S(2)}) collective-permute-start(bf16[64,1152]{1,0:T(8,128)(2,1)} %collective-permute-done.3.refs_3_), channel_id=1, source_target_pairs={{0,4},{4,0},{8,12},{12,8},{16,20},{20,16},{24,28},{28,24},{1,5},{5... | collective-permute-start | bytes 442376 | tf_op jit(solution)/shard_map/ppermute | solution.py:716
  109.0 27.5 %copy-start.1 = (s32[8]{0:T(128)}, s32[8]{0:T(128)S(1)}, u32[]{:S(2)}) copy-start(s32[8]{0:T(128)S(1)} %stack.228.limits) | copy-start | bytes 100
  136.5 4.6 collective-permute-start.11
  139.1 37.3 %collective-permute-start.13 = (bf16[576,1152]{1,0:T(8,128)(2,1)}, bf16[576,1152]{1,0:T(8,128)(2,1)}, u32[]{:S(2)}, u32[]{:S(2)}) collective-permute-start(bf16[576,1152]{1,0:T(8,128)(2,1)} %refs_0_.2), channel_id=1, source_target_pairs={{0,8},{4,12},{8,0},{12,4},{16,24},{20,28},{24,16},{28,20},{1,9},{5... | collective-permute-start | bytes 3981320 | tf_op jit(solution)/shard_map/ppermute | solution.py:716
  139.4 37.0 %collective-permute-start.14 = (bf16[576,1152]{1,0:T(8,128)(2,1)}, bf16[576,1152]{1,0:T(8,128)(2,1)}, u32[]{:S(2)}, u32[]{:S(2)}) collective-permute-start(bf16[576,1152]{1,0:T(8,128)(2,1)} %refs_0_.2), channel_id=1, source_target_pairs={{0,16},{4,20},{8,24},{12,28},{16,0},{20,4},{24,8},{28,12},{1,17},{... | collective-permute-start | bytes 3981320 | tf_op jit(solution)/shard_map/ppermute | solution.py:716
  176.4 44.1 %collective-permute-start.22 = (bf16[4,576,1152]{2,1,0:T(8,128)(2,1)}, bf16[4,576,1152]{2,1,0:T(8,128)(2,1)}, u32[]{:S(2)}, u32[]{:S(2)}) collective-permute-start(bf16[4,576,1152]{2,1,0:T(8,128)(2,1)} %shard_map.250), channel_id=1, source_target_pairs={{0,4},{4,0},{8,12},{12,8},{16,20},{20,16},{24,28},{28,24},{1,5},{5... | collective-permute-start | bytes 15925256 | tf_op jit(solution)/shard_map/ppermute | solution.py:716
  177.6 17.4 %collective-permute-start.15 = (bf16[288,1152]{1,0:T(8,128)(2,1)S(1)}, bf16[288,1152]{1,0:T(8,128)(2,1)S(1)}, u32[]{:S(2)}, u32[]{:S(2)}) collective-permute-start(bf16[288,1152]{1,0:T(8,128)(2,1)S(1)} %slice.116), channel_id=1, source_target_pairs={{0,16},{4,20},{8,24},{12,28},{16,0},{20,4},{24,8},{28,12},{1,17},{... | collective-permute-start | bytes 1990664 | tf_op jit(solution)/shard_map/ppermute | solution.py:716
  179.2 17.2 %collective-permute-start.16 = (bf16[288,1152]{1,0:T(8,128)(2,1)S(1)}, bf16[288,1152]{1,0:T(8,128)(2,1)}, u32[]{:S(2)}, u32[]{:S(2)}) collective-permute-start(bf16[288,1152]{1,0:T(8,128)(2,1)S(1)} %slice.117), channel_id=1, source_target_pairs={{0,8},{4,12},{8,0},{12,4},{16,24},{20,28},{24,16},{28,20},{1,9},{5... | collective-permute-start | bytes 1990664 | tf_op jit(solution)/shard_map/ppermute | solution.py:716
  181.0 16.0 %collective-permute-start.17 = (bf16[576,1152]{1,0:T(8,128)(2,1)}, bf16[576,1152]{1,0:T(8,128)(2,1)}, u32[]{:S(2)}, u32[]{:S(2)}) collective-permute-start(bf16[576,1152]{1,0:T(8,128)(2,1)} %refs_0_.2), channel_id=1, source_target_pairs={{0,4},{4,0},{8,12},{12,8},{16,20},{20,16},{24,28},{28,24},{1,5},{5... | collective-permute-start | bytes 3981320 | tf_op jit(solution)/shard_map/ppermute | solution.py:716
  196.5 7.2 %collective-permute-start.18 = (bf16[576,1152]{1,0:T(8,128)(2,1)}, bf16[576,1152]{1,0:T(8,128)(2,1)}, u32[]{:S(2)}, u32[]{:S(2)}) collective-permute-start(bf16[576,1152]{1,0:T(8,128)(2,1)} %collective-permute-done.13.refs_1_), channel_id=1, source_target_pairs={{0,4},{4,0},{8,12},{12,8},{16,20},{20,16},{24,28},{28,24},{1,5},{5... | collective-permute-start | bytes 3981320 | tf_op jit(solution)/shard_map/ppermute | solution.py:716
  196.5 7.2 %collective-permute-start.19 = (bf16[576,1152]{1,0:T(8,128)(2,1)}, bf16[576,1152]{1,0:T(8,128)(2,1)}, u32[]{:S(2)}, u32[]{:S(2)}) collective-permute-start(bf16[576,1152]{1,0:T(8,128)(2,1)} %collective-permute-done.14.refs_2_), channel_id=1, source_target_pairs={{0,4},{4,0},{8,12},{12,8},{16,20},{20,16},{24,28},{28,24},{1,5},{5... | collective-permute-start | bytes 3981320 | tf_op jit(solution)/shard_map/ppermute | solution.py:716
  197.0 4.6 collective-permute-start.20
  197.0 6.7 %collective-permute-start.21 = (bf16[288,1152]{1,0:T(8,128)(2,1)}, bf16[288,1152]{1,0:T(8,128)(2,1)}, u32[]{:S(2)}, u32[]{:S(2)}) collective-permute-start(bf16[288,1152]{1,0:T(8,128)(2,1)} %collective-permute-done.16.refs_4_), channel_id=1, source_target_pairs={{0,4},{4,0},{8,12},{12,8},{16,20},{20,16},{24,28},{28,24},{1,5},{5... | collective-permute-start | bytes 1990664 | tf_op jit(solution)/shard_map/ppermute | solution.py:716
  231.7 30.8 %collective-permute-start.24 = (bf16[288,1152]{1,0:T(8,128)(2,1)}, bf16[288,1152]{1,0:T(8,128)(2,1)}, u32[]{:S(2)}, u32[]{:S(2)}) collective-permute-start(bf16[288,1152]{1,0:T(8,128)(2,1)} %get-tuple-element.151), channel_id=1, source_target_pairs={{0,8},{4,12},{8,0},{12,4},{16,24},{20,28},{24,16},{28,20},{1,9},{5... | collective-permute-start | bytes 1990664 | tf_op jit(solution)/shard_map/ppermute | solution.py:716
  233.4 29.0 %collective-permute-start.25 = (bf16[288,1152]{1,0:T(8,128)(2,1)}, bf16[288,1152]{1,0:T(8,128)(2,1)}, u32[]{:S(2)}, u32[]{:S(2)}) collective-permute-start(bf16[288,1152]{1,0:T(8,128)(2,1)} %get-tuple-element.152), channel_id=1, source_target_pairs={{0,16},{4,20},{8,24},{12,28},{16,0},{20,4},{24,8},{28,12},{1,17},{... | collective-permute-start | bytes 1990664 | tf_op jit(solution)/shard_map/ppermute | solution.py:716
  256.5 45.6 %collective-permute-start.28 = (bf16[4,144,4608]{2,1,0:T(8,128)(2,1)}, bf16[4,144,4608]{2,1,0:T(8,128)(2,1)}, u32[]{:S(2)}, u32[]{:S(2)}) collective-permute-start(bf16[4,144,4608]{2,1,0:T(8,128)(2,1)} %shard_map.254), channel_id=1, source_target_pairs={{0,4},{4,0},{8,12},{12,8},{16,20},{20,16},{24,28},{28,24},{1,5},{5... | collective-permute-start | bytes 15925256 | tf_op jit(solution)/shard_map/ppermute | solution.py:716
  256.8 34.6 %all-to-all-start.3 = ((bf16[4,128,1152]{2,1,0:T(8,128)(2,1)}), bf16[4,128,1152]{2,1,0:T(8,128)(2,1)S(1)}, u32[]{:S(2)}, u32[]{:S(2)}) async-start(bf16[4,128,1152]{2,1,0:T(8,128)(2,1)} %bitcast.116), calls=%async_computation.3 | async-start | bytes 2359296 | tf_op jit(solution)/shard_map/all_to_all | solution.py:703
  262.4 103.1 %all-reduce.6.cloned.1.call-start = ((), (), s32[]{:S(2)}) async-start(), calls=%async_computation.9 | async-start | bytes 2654208 | tf_op jit(solution)/shard_map/psum | solution.py:801
  266.3 31.3 %collective-permute-start.26 = (bf16[576,1152]{1,0:T(8,128)(2,1)}, bf16[576,1152]{1,0:T(8,128)(2,1)}, u32[]{:S(2)}, u32[]{:S(2)}) collective-permute-start(bf16[576,1152]{1,0:T(8,128)(2,1)} %get-tuple-element.161), channel_id=1, source_target_pairs={{0,8},{4,12},{8,0},{12,4},{16,24},{20,28},{24,16},{28,20},{1,9},{5... | collective-permute-start | bytes 3981320 | tf_op jit(solution)/shard_map/ppermute | solution.py:716
  266.6 31.0 %collective-permute-start.27 = (bf16[576,1152]{1,0:T(8,128)(2,1)}, bf16[576,1152]{1,0:T(8,128)(2,1)}, u32[]{:S(2)}, u32[]{:S(2)}) collective-permute-start(bf16[576,1152]{1,0:T(8,128)(2,1)} %get-tuple-element.162), channel_id=1, source_target_pairs={{0,16},{4,20},{8,24},{12,28},{16,0},{20,4},{24,8},{28,12},{1,17},{... | collective-permute-start | bytes 3981320 | tf_op jit(solution)/shard_map/ppermute | solution.py:716
  285.6 31.7 %collective-permute-start.29 = (bf16[512,640]{1,0:T(8,128)(2,1)}, bf16[512,640]{1,0:T(8,128)(2,1)}, u32[]{:S(2)}, u32[]{:S(2)}) collective-permute-start(bf16[512,640]{1,0:T(8,128)(2,1)} %get-tuple-element.178), channel_id=1, source_target_pairs={{0,4},{4,0},{8,12},{12,8},{16,20},{20,16},{24,28},{28,24},{1,5},{5... | collective-permute-start | bytes 1966088 | tf_op jit(solution)/shard_map/ppermute | solution.py:682
  292.5 8.4 %collective-permute-start.23 = (bf16[2,128,1152]{2,1,0:T(8,128)(2,1)}, bf16[2,128,1152]{2,1,0:T(8,128)(2,1)S(1)}, u32[]{:S(2)}, u32[]{:S(2)}) collective-permute-start(bf16[2,128,1152]{2,1,0:T(8,128)(2,1)} %get-tuple-element.240), channel_id=1, source_target_pairs={{0,4},{4,0},{8,12},{12,8},{16,20},{20,16},{24,28},{28,24},{1,5},{5... | collective-permute-start | bytes 1769480 | tf_op jit(solution)/shard_map/ppermute | solution.py:682
  302.1 171.5 %all-reduce.8.cloned.1.call-start = ((), (), s32[]{:S(2)}) async-start(), calls=%async_computation.10 | async-start | bytes 2654208 | tf_op jit(solution)/shard_map/psum | solution.py:801
  311.2 23.1 %collective-permute-start.30 = (bf16[72,4608]{1,0:T(8,128)(2,1)}, bf16[72,4608]{1,0:T(8,128)(2,1)S(1)}, u32[]{:S(2)}, u32[]{:S(2)}) collective-permute-start(bf16[72,4608]{1,0:T(8,128)(2,1)} %get-tuple-element.173), channel_id=1, source_target_pairs={{0,8},{4,12},{8,0},{12,4},{16,24},{20,28},{24,16},{28,20},{1,9},{5... | collective-permute-start | bytes 1990664 | tf_op jit(solution)/shard_map/ppermute | solution.py:716
  317.1 25.6 %collective-permute-start.32 = (bf16[4,144,1152]{2,1,0:T(8,128)(2,1)}, bf16[4,144,1152]{2,1,0:T(8,128)(2,1)S(1)}, u32[]{:S(2)}, u32[]{:S(2)}) collective-permute-start(bf16[4,144,1152]{2,1,0:T(8,128)(2,1)} %shard_map.258), channel_id=1, source_target_pairs={{0,4},{4,0},{8,12},{12,8},{16,20},{20,16},{24,28},{28,24},{1,5},{5... | collective-permute-start | bytes 3981320 | tf_op jit(solution)/shard_map/ppermute | solution.py:716
  317.1 17.3 %collective-permute-start.31 = (bf16[72,4608]{1,0:T(8,128)(2,1)S(1)}, bf16[72,4608]{1,0:T(8,128)(2,1)S(1)}, u32[]{:S(2)}, u32[]{:S(2)}) collective-permute-start(bf16[72,4608]{1,0:T(8,128)(2,1)S(1)} %copy-done.27), channel_id=1, source_target_pairs={{0,16},{4,20},{8,24},{12,28},{16,0},{20,4},{24,8},{28,12},{1,17},{... | collective-permute-start | bytes 1990664 | tf_op jit(solution)/shard_map/ppermute | solution.py:716
  340.4 31.7 %collective-permute-start.35 = (bf16[144,4608]{1,0:T(8,128)(2,1)}, bf16[144,4608]{1,0:T(8,128)(2,1)}, u32[]{:S(2)}, u32[]{:S(2)}) collective-permute-start(bf16[144,4608]{1,0:T(8,128)(2,1)} %get-tuple-element.184), channel_id=1, source_target_pairs={{0,8},{4,12},{8,0},{12,4},{16,24},{20,28},{24,16},{28,20},{1,9},{5... | collective-permute-start | bytes 3981320 | tf_op jit(solution)/shard_map/ppermute | solution.py:716
  340.7 31.5 %collective-permute-start.36 = (bf16[144,4608]{1,0:T(8,128)(2,1)}, bf16[144,4608]{1,0:T(8,128)(2,1)}, u32[]{:S(2)}, u32[]{:S(2)}) collective-permute-start(bf16[144,4608]{1,0:T(8,128)(2,1)} %get-tuple-element.185), channel_id=1, source_target_pairs={{0,16},{4,20},{8,24},{12,28},{16,0},{20,4},{24,8},{28,12},{1,17},{... | collective-permute-start | bytes 3981320 | tf_op jit(solution)/shard_map/ppermute | solution.py:716
  342.6 32.9 %collective-permute-start.33 = (bf16[512,896]{1,0:T(8,128)(2,1)}, bf16[512,896]{1,0:T(8,128)(2,1)}, u32[]{:S(2)}, u32[]{:S(2)}) collective-permute-start(bf16[512,896]{1,0:T(8,128)(2,1)} %get-tuple-element.181), channel_id=1, source_target_pairs={{0,4},{4,0},{8,12},{12,8},{16,20},{20,16},{24,28},{28,24},{1,5},{5... | collective-permute-start | bytes 2752520 | tf_op jit(solution)/shard_map/ppermute | solution.py:682
  365.0 10.5 %collective-permute-start.34 = (bf16[512,896]{1,0:T(8,128)(2,1)}, bf16[512,896]{1,0:T(8,128)(2,1)}, u32[]{:S(2)}, u32[]{:S(2)}) collective-permute-start(bf16[512,896]{1,0:T(8,128)(2,1)} %get-tuple-element.194), channel_id=1, source_target_pairs={{0,4},{4,0},{8,12},{12,8},{16,20},{20,16},{24,28},{28,24},{1,5},{5... | collective-permute-start | bytes 2752520 | tf_op jit(solution)/shard_map/ppermute | solution.py:682
  387.5 24.8 %collective-permute-start.39 = (bf16[4,144,3456]{2,1,0:T(8,128)(2,1)}, bf16[4,144,3456]{2,1,0:T(8,128)(2,1)}, u32[]{:S(2)}, u32[]{:S(2)}) collective-permute-start(bf16[4,144,3456]{2,1,0:T(8,128)(2,1)} %shard_map.264), channel_id=1, source_target_pairs={{0,4},{4,0},{8,12},{12,8},{16,20},{20,16},{24,28},{28,24},{1,5},{5... | collective-permute-start | bytes 11943944 | tf_op jit(solution)/shard_map/ppermute | solution.py:716
  387.7 7.0 %collective-permute-start.37 = (bf16[72,1152]{1,0:T(8,128)(2,1)}, bf16[72,1152]{1,0:T(8,128)(2,1)}, u32[]{:S(2)}, u32[]{:S(2)}) collective-permute-start(bf16[72,1152]{1,0:T(8,128)(2,1)} %get-tuple-element.190), channel_id=1, source_target_pairs={{0,8},{4,12},{8,0},{12,4},{16,24},{20,28},{24,16},{28,20},{1,9},{5... | collective-permute-start | bytes 497672 | tf_op jit(solution)/shard_map/ppermute | solution.py:716
  389.4 6.5 %collective-permute-start.38 = (bf16[72,1152]{1,0:T(8,128)(2,1)S(1)}, bf16[72,1152]{1,0:T(8,128)(2,1)}, u32[]{:S(2)}, u32[]{:S(2)}) collective-permute-start(bf16[72,1152]{1,0:T(8,128)(2,1)S(1)} %copy-done.29), channel_id=1, source_target_pairs={{0,16},{4,20},{8,24},{12,28},{16,0},{20,4},{24,8},{28,12},{1,17},{... | collective-permute-start | bytes 497672 | tf_op jit(solution)/shard_map/ppermute | solution.py:716
  420.2 1.2 collective-permute-start.41
  421.4 5.8 %collective-permute-start.42 = (bf16[1,6912]{1,0:T(2,128)(2,1)S(1)}, bf16[1,6912]{1,0:T(2,128)(2,1)S(1)}, u32[]{:S(2)}, u32[]{:S(2)}) collective-permute-start(bf16[1,6912]{1,0:T(2,128)(2,1)S(1)} %broadcast_in_dim.38), channel_id=1, source_target_pairs={{0,1},{1,0},{2,3},{3,2},{4,5},{5,4},{6,7},{7,6},{8,9},{9,8},{10,11... | collective-permute-start | bytes 41480 | tf_op jit(solution)/shard_map/ppermute | solution.py:856
  423.8 10.0 %all-to-all-start.5 = ((f32[8,1,1152]{2,1,0:T(1,128)}), f32[8,1,1152]{2,1,0:T(1,128)S(1)}, u32[]{:S(2)}, u32[]{:S(2)}) async-start(f32[8,1,1152]{2,1,0:T(1,128)} %all_to_all.36), calls=%async_computation.5 | async-start | bytes 73728 | tf_op jit(solution)/shard_map/all_to_all | solution.py:1006
  427.3 10.2 %collective-permute-start.43 = (bf16[2,6912]{1,0:T(2,128)(2,1)S(1)}, bf16[2,6912]{1,0:T(2,128)(2,1)S(1)}, u32[]{:S(2)}, u32[]{:S(2)}) collective-permute-start(bf16[2,6912]{1,0:T(2,128)(2,1)S(1)} %pad_maximum_fusion.4), channel_id=1, source_target_pairs={{0,2},{1,3},{2,0},{3,1},{4,6},{5,7},{6,4},{7,5},{8,10},{9,11},{10,... | collective-permute-start | bytes 82952 | tf_op jit(solution)/shard_map/ppermute | solution.py:856
  429.8 45.3 %collective-permute-start.48 = (bf16[144,1152]{1,0:T(8,128)(2,1)}, bf16[144,1152]{1,0:T(8,128)(2,1)}, u32[]{:S(2)}, u32[]{:S(2)}) collective-permute-start(bf16[144,1152]{1,0:T(8,128)(2,1)} %get-tuple-element.200), channel_id=1, source_target_pairs={{0,8},{4,12},{8,0},{12,4},{16,24},{20,28},{24,16},{28,20},{1,9},{5... | collective-permute-start | bytes 995336 | tf_op jit(solution)/shard_map/ppermute | solution.py:716
  431.6 43.5 %collective-permute-start.49 = (bf16[144,1152]{1,0:T(8,128)(2,1)}, bf16[144,1152]{1,0:T(8,128)(2,1)}, u32[]{:S(2)}, u32[]{:S(2)}) collective-permute-start(bf16[144,1152]{1,0:T(8,128)(2,1)} %get-tuple-element.201), channel_id=1, source_target_pairs={{0,16},{4,20},{8,24},{12,28},{16,0},{20,4},{24,8},{28,12},{1,17},{... | collective-permute-start | bytes 995336 | tf_op jit(solution)/shard_map/ppermute | solution.py:716
  433.1 17.4 %collective-permute-start.44 = (bf16[72,3456]{1,0:T(8,128)(2,1)}, bf16[72,3456]{1,0:T(8,128)(2,1)}, u32[]{:S(2)}, u32[]{:S(2)}) collective-permute-start(bf16[72,3456]{1,0:T(8,128)(2,1)} %get-tuple-element.209), channel_id=1, source_target_pairs={{0,8},{4,12},{8,0},{12,4},{16,24},{20,28},{24,16},{28,20},{1,9},{5... | collective-permute-start | bytes 1493000 | tf_op jit(solution)/shard_map/ppermute | solution.py:716
  433.7 18.2 %collective-permute-start.45 = (bf16[72,3456]{1,0:T(8,128)(2,1)}, bf16[72,3456]{1,0:T(8,128)(2,1)}, u32[]{:S(2)}, u32[]{:S(2)}) collective-permute-start(bf16[72,3456]{1,0:T(8,128)(2,1)} %get-tuple-element.210), channel_id=1, source_target_pairs={{0,16},{4,20},{8,24},{12,28},{16,0},{20,4},{24,8},{28,12},{1,17},{... | collective-permute-start | bytes 1493000 | tf_op jit(solution)/shard_map/ppermute | solution.py:716
  433.8 54.3 %all-to-all-start.4 = ((bf16[4,128,1152]{2,1,0:T(8,128)(2,1)}), bf16[4,128,1152]{2,1,0:T(8,128)(2,1)S(1)}, u32[]{:S(2)}, u32[]{:S(2)}) async-start(bf16[4,128,1152]{2,1,0:T(8,128)(2,1)} %bitcast.115), calls=%async_computation.4 | async-start | bytes 2359296 | tf_op jit(solution)/shard_map/all_to_all | solution.py:703
  437.4 110.7 %all-reduce.10.cloned.1.call-start = ((), (), s32[]{:S(2)}) async-start(), calls=%async_computation.11 | async-start | bytes 2764800 | tf_op jit(solution)/shard_map/psum | solution.py:801
  455.8 17.8 %collective-permute-start.46 = (bf16[4,6912]{1,0:T(4,128)(2,1)S(1)}, bf16[4,6912]{1,0:T(4,128)(2,1)S(1)}, u32[]{:S(2)}, u32[]{:S(2)}) collective-permute-start(bf16[4,6912]{1,0:T(4,128)(2,1)S(1)} %pad_maximum_fusion.3), channel_id=1, source_target_pairs={{0,8},{4,12},{8,0},{12,4},{16,24},{20,28},{24,16},{28,20},{1,9},{5... | collective-permute-start | bytes 165896 | tf_op jit(solution)/shard_map/ppermute | solution.py:716
  456.2 28.0 %collective-permute-start.50 = (bf16[144,3456]{1,0:T(8,128)(2,1)}, bf16[144,3456]{1,0:T(8,128)(2,1)}, u32[]{:S(2)}, u32[]{:S(2)}) collective-permute-start(bf16[144,3456]{1,0:T(8,128)(2,1)} %get-tuple-element.221), channel_id=1, source_target_pairs={{0,8},{4,12},{8,0},{12,4},{16,24},{20,28},{24,16},{28,20},{1,9},{5... | collective-permute-start | bytes 2985992 | tf_op jit(solution)/shard_map/ppermute | solution.py:716
  457.9 26.3 %collective-permute-start.51 = (bf16[144,3456]{1,0:T(8,128)(2,1)}, bf16[144,3456]{1,0:T(8,128)(2,1)}, u32[]{:S(2)}, u32[]{:S(2)}) collective-permute-start(bf16[144,3456]{1,0:T(8,128)(2,1)} %get-tuple-element.222), channel_id=1, source_target_pairs={{0,16},{4,20},{8,24},{12,28},{16,0},{20,4},{24,8},{28,12},{1,17},{... | collective-permute-start | bytes 2985992 | tf_op jit(solution)/shard_map/ppermute | solution.py:716
  473.7 8.9 %collective-permute-start.47 = (bf16[8,6912]{1,0:T(8,128)(2,1)S(1)}, bf16[8,6912]{1,0:T(8,128)(2,1)S(1)}, u32[]{:S(2)}, u32[]{:S(2)}) collective-permute-start(bf16[8,6912]{1,0:T(8,128)(2,1)S(1)} %pad_maximum_fusion.2), channel_id=1, source_target_pairs={{0,16},{4,20},{8,24},{12,28},{16,0},{20,4},{24,8},{28,12},{1,17},{... | collective-permute-start | bytes 331784 | tf_op jit(solution)/shard_map/ppermute | solution.py:716
  488.1 12.5 %all-to-all-start.6 = ((f32[8,1,288]{2,1,0:T(1,128)}), f32[8,1,288]{2,1,0:T(1,128)S(1)}, u32[]{:S(2)}, u32[]{:S(2)}) async-start(f32[8,1,288]{2,1,0:T(1,128)} %all_to_all.38), calls=%async_computation.6 | async-start | bytes 24576 | tf_op jit(solution)/shard_map/all_to_all | solution.py:1021
  492.6 9.0 %collective-permute-start.40 = (bf16[2,128,1152]{2,1,0:T(8,128)(2,1)}, bf16[2,128,1152]{2,1,0:T(8,128)(2,1)S(1)}, u32[]{:S(2)}, u32[]{:S(2)}) collective-permute-start(bf16[2,128,1152]{2,1,0:T(8,128)(2,1)} %get-tuple-element.238), channel_id=1, source_target_pairs={{0,4},{4,0},{8,12},{12,8},{16,20},{20,16},{24,28},{28,24},{1,5},{5... | collective-permute-start | bytes 1769480 | tf_op jit(solution)/shard_map/ppermute | solution.py:682
  (29 other events, 225.2 us)
Sparse Core Ops, SparseCore 0:
  9.9 68.1 all-gather.4
  80.0 63.9 all-gather.6
  302.2 61.3 all-reduce.5
  392.0 81.5 all-reduce.7
  487.6 60.4 all-reduce.9

commit v4 on v3

--- a/solution.py
+++ b/solution.py
@@ -437,7 +437,7 @@
         out_specs=(WHOLE, WHOLE, pl.BlockSpec((1, width), lambda i: (0, i))),
         scratch_shapes=[pltpu.VMEM((rows, width), f32)],
         compiler_params=params(48),
-        cost_estimate=lasts(40),
+        cost_estimate=lasts(120),
     )(*in_hbm(d_qkv, matrix, tokens, mods, d_middle))
 
 
@@ -673,7 +673,7 @@
             pltpu.VMEM((total, HEAD), f32),
         ],
         compiler_params=params(VMEM_ATT),
-        cost_estimate=lasts(17),
+        cost_estimate=lasts(4),
     )(limits, *in_hbm(mine, theirs, d_mine, d_theirs, lse))
 
 
@@ -941,6 +941,7 @@
     theirs = pair_swap(away)
     down_hops = Hops(after(down_weight, mine))
     att_mine, att_away, lse = attend(limits, after(mine, out_pieces[1]), theirs)
+    first = down_hops.moving
     down_hops.turn(att_mine)
     down_pieces = down_hops.pieces()
     attended, projected, normed2, factor2, moved2, out_matrix = middle_part(
@@ -951,15 +952,15 @@
     d_lowered = (gate2 * upstream16.astype(f32)).astype(bf16)
     down_offset_grad = jnp.sum(d_lowered.astype(f32), axis=0)
     down_g = Grad(act, d_lowered, True)
-    mark = down_g.away(act)
+    mark = down_g.away(act, first)
+    mark = down_g.stay(mark)
     d_upper, up_sums, down_matrix = slope_part(after(d_lowered, mark), down_pieces, slope)
-    mark = down_g.stay(d_upper)
+    mark = down_g.mix(d_upper)
     output, d_gate2 = down_part(
         after(act, mark), down_matrix, down_offset[None], tokens16, projected, modulation, upstream16
     )
     up_g = Grad(moved2, d_upper)
     mark = up_g.away(output)
-    mark = down_g.mix(mark)
     d_middle, d_projected, d_att_mine, d_att_away, sums2 = middle_back(
         core, after(d_upper, mark), up_matrix, normed2, factor2, projected, upstream16, modulation, out_matrix
     )
@@ -967,7 +968,7 @@
     d_att_theirs = pair_swap(d_att_away)
     output = undeal(output)
     mark, down_total = down_g.finish(d_att_mine)
-    mark = up_g.stay(mark, output)
+    mark = up_g.stay(mark)
     out_g = Grad(attended, d_projected)
     mark = out_g.away(mark)
     heads = HEADS // 2
@@ -983,8 +984,8 @@
         if i == 0:
             mark = up_g.mix(mark)
             mark = out_g.stay(mark)
-    mark, up_total = up_g.finish(mark, down_total)
     d_qkv = join_heads(core, own, got)
+    mark, up_total = up_g.finish(d_qkv, down_total, output)
     qkv_g = Grad(moved, d_qkv)
     mark = qkv_g.away(mark)
     mark = out_g.mix(mark)

time: 569 us -> 555 us (0.975)
  waiting for transfers between devices: 152 us -> 137 us
    ppermute x40, waiting for transfers between devices: 78.3 us -> 56.7 us  [hop(): return lax.ppermute(array, 'batch', [(i, i ^ bits) for i in range(size)])]
    psum x3, waiting for transfers between devices: 59.1 us -> 71.2 us  [finish(): total = lax.psum(part, 'seq')]
    all_to_all x2, waiting for transfers between devices: 5.74 us -> 0.01 us  [undeal(): lax.all_to_all(array.reshape(4, rows // 4, width), 'seq', 0, 0, tiled=True)]
  transfers between devices with their start and end apart: 63 -> 63, of which waited for: 23 -> 18; matrix products, arithmetic and copies ran while one was open for 9% -> 10% of each run, Pallas kernels for 39% -> 41%
where the time goes in v4:
time: 555 us; the launch traced here: 547 us
  Pallas kernels  240 us (43%)
  waiting for transfers between devices  137 us (25%)
  starting transfers between devices  62.7 us (11%)
  other arithmetic  31.3 us (6%)
  local copies, waits for them, and re-layouts  29.9 us (5%)
  blocking collectives  22.5 us (4%)
  between operations  19.9 us (4%)
    psum x3, waiting for transfers between devices, finish(): total = lax.psum(part, 'seq')  71.2 us
    ppermute x40, waiting for transfers between devices, hop(): return lax.ppermute(array, 'batch', [(i, i ^ bits) for i in range(size)])  56.7 us
    pallas_call x6, Pallas kernels, block_grad(): pl.pallas_call(functools.partial(block_grad_kernel, len(gots)), out_shape...  39.5 us
    pallas_call x2, Pallas kernels, attend_back(): pl.pallas_call(functools.partial(back_kernel, heads, first, number), out_...  34 us
    ppermute x40, starting transfers between devices, hop(): return lax.ppermute(array, 'batch', [(i, i ^ bits) for i in range(size)])  31.1 us
    pallas_call x1, Pallas kernels, attend(): pl.pallas_call(functools.partial(attend_kernel, heads), out_shape=(shaped...  27.2 us
    pallas_call x2, Pallas kernels, pair_grad(): pl.pallas_call(functools.partial(pair_grad_kernel, len(gots)), out_shape=...  21 us
    pallas_call x1, Pallas kernels, middle_back(): pl.pallas_call(middle_back_kernel, out_shape=(shaped((rows, width), f32),...  18.9 us
  transfers between devices with their start and end apart: 63, of which 18 were waited for; matrix products, arithmetic and copies ran while one was open for 10% of the time, Pallas kernels for 41%

profile of v4, /device:TPU:0, one launch (start us, length us, event | category | flops | bytes accessed | tf_op | source)
XLA Modules:
  0.0 546.9 jit_solution(16649449408112135934)
XLA Ops:
  10.0 2.8 concatenate.37
  12.8 10.7 %all-gather.1 = bf16[8,1,3584]{2,1,0:T(2,128)(2,1)S(1)} all-gather(bf16[1,1,3584]{2,1,0:T(2,128)(2,1)S(1)} %reshape.215), channel_id=2, replica_groups=mesh['batch'=8,'seq'=4] {'batch'}, dimensions={0}, use_global_device_ids=true | all-gather | bytes 64512 | tf_op jit(solution)/shard_map/all_gather | solution.py:711
  24.7 11.8 %all_to_all.47 = f32[8,1,6912]{2,1,0:T(1,128)S(1)} all-to-all(f32[8,1,6912]{2,1,0:T(1,128)S(1)} %all_to_all.31), channel_id=1, replica_groups=mesh['batch'=8,'seq'=4] {'batch'}, dimensions={0} | all-to-all | bytes 442368 | tf_op jit(solution)/shard_map/all_to_all | solution.py:929
  37.3 2.2 dynamic-slice_bitcast_fusion.7
  39.4 2.2 collective-permute-done
  43.0 4.9 all-to-all-start
  48.9 16.6 %collective-permute-done.1.refs_1_ = bf16[144,1152]{1,0:T(8,128)(2,1)} collective-permute-done((bf16[144,1152]{1,0:T(8,128)(2,1)}, bf16[144,1152]{1,0:T(8,128)(2,1)}, u32[]{:S(2)}, u32[]{:S(2)}) %collective-permute-start.1) | collective-permute-done | bytes 331808 | tf_op jit(solution)/shard_map/ppermute | solution.py:716
  66.5 2.0 collective-permute-start.4
  71.4 4.6 collective-permute-done.3.refs_3_
  78.2 11.7 %shard_map.246 = (bf16[512,1728]{1,0:T(8,128)(2,1)}, bf16[512,1792]{1,0:T(8,128)(2,1)}, bf16[512,1152]{1,0:T(8,128)(2,1)}) custom-call(s32[1]{0:T(128)} %bitcast.core, bf16[512,1152]{1,0:T(8,128)(2,1)} %bitcast.103, f32[1,6912]{1,0:T(1,128)} %broadcast_in_dim.35.mods, f32[1,3456]{1,0:T(1,128)} %broadcast_in_dim.37.offset, ...), custom_call_target="tpu_custom_call" | custom-call | flops 7800000000 | bytes 25740000 | tf_op jit(solution)/shard_map/pallas_call | solution.py:162
  91.5 3.9 collective-permute-done.14
  96.9 4.6 all-to-all-start.2
  109.2 27.2 %shard_map.247 = (bf16[512,576]{1,0:T(8,128)(2,1)}, bf16[512,640]{1,0:T(8,128)(2,1)}, f32[8,1024]{1,0:T(8,128)}) custom-call(s32[8]{0:T(128)S(1)} %stack.228.limits, bf16[512,1728]{1,0:T(8,128)(2,1)} %get-tuple-element.192.mine, bf16[512,1792]{1,0:T(8,128)(2,1)} %collective-permute-done.10.theirs), custom_call_target="tpu_custom_call" | custom-call | flops 16199999488 | bytes 53460000 | tf_op jit(solution)/shard_map/pallas_call | solution.py:608
  139.5 1.6 collective-permute-start.13
  141.1 9.4 %shard_map.248 = (bf16[512,1152]{1,0:T(8,128)(2,1)}, f32[512,1152]{1,0:T(8,128)}, f32[512,1152]{1,0:T(8,128)}, f32[512,1]{1,0:T(8,128)}, bf16[512,1152]{1,0:T(8,128)(2,1)}, /*index=5*/bf16[1152,1152]{1,0:T(8,128)(2,1)}) custom-call(s32[1]{0:T(128)} %bitcast.core, s32[10]{0:T(128)S(1)} %stack.219.spots, bf16[512,576]{1,0:T(8,128)(2,1)} %get-tuple-element.131.own, ...), custom_call_target="tpu_custom_call" | custom-call | flops 5400000000 | bytes 17820000 | tf_op jit(solution)/shard_map/pallas_call | solution.py:213
  150.5 16.3 %shard_map.249 = (bf16[512,4608]{1,0:T(8,128)(2,1)}, f32[512,4608]{1,0:T(8,128)}) custom-call(bf16[512,1152]{1,0:T(8,128)(2,1)} %get-tuple-element.169.moved.left, bf16[1152,4608]{1,0:T(8,128)(2,1)} %all-gather.7.cloned.1.call-done.matrix, f32[1,4608]{1,0:T(1,128)} %reshape.211.offset), custom_call_target="tpu_custom_call" | custom-call | flops 9600000000 | bytes 31680000 | tf_op jit(solution)/shard_map/pallas_call | solution.py:247
  166.8 3.7 collective-permute-done.12.refs_1_
  170.5 9.8 %shard_map.250 = bf16[4,576,1152]{2,1,0:T(8,128)(2,1)} custom-call(s32[2]{0:T(128)S(1)} %pad_add_fusion.1.where, bf16[512,4608]{1,0:T(8,128)(2,1)} %get-tuple-element.157.left.act, bf16[512,1152]{1,0:T(8,128)(2,1)} %multiply_convert_fusion.1.right.grad), custom_call_target="tpu_custom_call" | custom-call | flops 5400000000 | bytes 17820000 | tf_op jit(solution)/shard_map/pallas_call | solution.py:487
  181.5 1.8 collective-permute-start.16
  184.4 1.8 collective-permute-start.17
  186.2 12.7 %collective-permute-done.16.refs_3_ = bf16[288,1152]{1,0:T(8,128)(2,1)S(1)} collective-permute-done((bf16[288,1152]{1,0:T(8,128)(2,1)S(1)}, bf16[288,1152]{1,0:T(8,128)(2,1)S(1)}, u32[]{:S(2)}, u32[]{:S(2)}) %collective-permute-start.16) | collective-permute-done | bytes 663584 | tf_op jit(solution)/shard_map/ppermute | solution.py:716
  198.9 2.6 collective-permute-done.17.refs_4_
  204.4 11.2 %shard_map.251 = (bf16[576,1152]{1,0:T(8,128)(2,1)}, bf16[576,1152]{1,0:T(8,128)(2,1)}, bf16[576,1152]{1,0:T(8,128)(2,1)}, bf16[288,1152]{1,0:T(8,128)(2,1)}, bf16[288,1152]{1,0:T(8,128)(2,1)}) custom-call(s32[2]{0:T(128)S(1)} %pad_add_fusion.where, bf16[512,4608]{1,0:T(8,128)(2,1)} %get-tuple-element.157.left.act, ...), custom_call_target="tpu_custom_call" | custom-call | flops 5400000000 | bytes 17820000 | tf_op jit(solution)/shard_map/pallas_call | solution.py:487
  215.6 1.8 collective-permute-start.23
  217.7 17.2 %shard_map.252 = (bf16[512,4608]{1,0:T(8,128)(2,1)}, f32[1,4608]{1,0:T(1,128)}, bf16[4608,1152]{1,0:T(8,128)(2,1)}) custom-call(s32[10]{0:T(128)S(1)} %stack.251.spots, bf16[512,1152]{1,0:T(8,128)(2,1)} %multiply_convert_fusion.1.right.grad, f32[512,4608]{1,0:T(8,128)} %get-tuple-element.145.slope, bf16[576,1152]{1,0:T(8,128)(2,1)} %refs_0_.2, ...), custom_call_target="tpu_custom_call" | custom-call | flops 24000000000 | bytes 79200000 | tf_op jit(solution)/shard_map/pallas_call | solution.py:288
  236.7 3.8 shard_map.253
  240.7 1.7 collective-permute-start.27
  242.5 13.0 %shard_map.254 = (bf16[512,1152]{1,0:T(8,128)(2,1)}, f32[1,1152]{1,0:T(1,128)}) custom-call(bf16[512,4608]{1,0:T(8,128)(2,1)} %get-tuple-element.157.left.act, bf16[4608,1152]{1,0:T(8,128)(2,1)} %get-tuple-element.158.matrix, f32[1,1152]{1,0:T(1,128)} %reshape.212.offset, bf16[512,1152]{1,0:T(8,128)(2,1)} %bitcast.105, ...), custom_call_target="tpu_custom_call" | custom-call | flops 3600000000 | bytes 11879999 | tf_op jit(solution)/shard_map/pallas_call | solution.py:331
  255.5 7.8 %shard_map.255 = bf16[4,144,4608]{2,1,0:T(8,128)(2,1)} custom-call(s32[4]{0:T(128)S(1)} %pad_add_fusion.2.spots, bf16[512,1152]{1,0:T(8,128)(2,1)} %get-tuple-element.169.moved.left, bf16[512,4608]{1,0:T(8,128)(2,1)} %get-tuple-element.163.right.d_upper), custom_call_target="tpu_custom_call" | custom-call | flops 2400000000 | bytes 7920000 | tf_op jit(solution)/shard_map/pallas_call | solution.py:527
  263.3 5.6 %all-to-all-start.3 = ((bf16[4,128,1152]{2,1,0:T(8,128)(2,1)}), bf16[4,128,1152]{2,1,0:T(8,128)(2,1)S(1)}, u32[]{:S(2)}, u32[]{:S(2)}) async-start(bf16[4,128,1152]{2,1,0:T(8,128)(2,1)} %bitcast.116), calls=%async_computation.3 | async-start | bytes 2359296 | tf_op jit(solution)/shard_map/all_to_all | solution.py:703
  268.9 18.9 %shard_map.256 = (f32[512,1152]{1,0:T(8,128)}, bf16[512,1152]{1,0:T(8,128)(2,1)}, bf16[512,576]{1,0:T(8,128)(2,1)}, bf16[512,640]{1,0:T(8,128)(2,1)}, f32[4,1152]{1,0:T(4,128)}) custom-call(s32[1]{0:T(128)} %bitcast.core, bf16[512,4608]{1,0:T(8,128)(2,1)} %get-tuple-element.163.right.d_upper, bf16[1152,4608]{1,0:T(8,128)(2,1)} %all-gather.7.cloned.1.call-done.matrix, ...), custom_call_target="tpu_custom_call" | custom-call | flops 89999998976 | bytes 297000000 | tf_op jit(solution)/shard_map/pallas_call | solution.py:383
  287.8 3.3 add_convert_fusion.1
  291.2 8.8 %shard_map.257 = (bf16[144,4608]{1,0:T(8,128)(2,1)}, bf16[144,4608]{1,0:T(8,128)(2,1)}, bf16[144,4608]{1,0:T(8,128)(2,1)}, bf16[72,4608]{1,0:T(8,128)(2,1)}, bf16[72,4608]{1,0:T(8,128)(2,1)}) custom-call(s32[4]{0:T(128)S(1)} %pad_add_fusion.3.spots, bf16[512,1152]{1,0:T(8,128)(2,1)} %get-tuple-element.169.moved.left, ...), custom_call_target="tpu_custom_call" | custom-call | flops 2400000000 | bytes 7920000 | tf_op jit(solution)/shard_map/pallas_call | solution.py:527
  300.0 4.0 shard_map.258
  304.6 1.8 collective-permute-start.30
  308.3 17.0 %shard_map.259 = (bf16[512,864]{1,0:T(8,128)(2,1)}, bf16[512,896]{1,0:T(8,128)(2,1)}) custom-call(s32[8]{0:T(128)S(1)} %copy-done.2, bf16[512,1728]{1,0:T(8,128)(2,1)} %get-tuple-element.192.mine, bf16[512,1792]{1,0:T(8,128)(2,1)} %collective-permute-done.10.theirs, bf16[512,576]{1,0:T(8,128)(2,1)} %get-tuple-element.167.d_mine, ...), custom_call_target="tpu_custom_call" | custom-call | flops 2400000000 | bytes 7920000 | tf_op jit(solution)/shard_map/pallas_call | solution.py:661
  325.7 4.4 shard_map.260
  330.1 1.6 collective-permute-start.35
  332.0 4.2 shard_map.261
  336.3 17.0 %shard_map.262 = (bf16[512,864]{1,0:T(8,128)(2,1)}, bf16[512,896]{1,0:T(8,128)(2,1)}) custom-call(s32[8]{0:T(128)S(1)} %copy-done.2, bf16[512,1728]{1,0:T(8,128)(2,1)} %get-tuple-element.192.mine, bf16[512,1792]{1,0:T(8,128)(2,1)} %collective-permute-done.10.theirs, bf16[512,576]{1,0:T(8,128)(2,1)} %get-tuple-element.167.d_mine, ...), custom_call_target="tpu_custom_call" | custom-call | flops 2400000000 | bytes 7920000 | tf_op jit(solution)/shard_map/pallas_call | solution.py:661
  354.1 2.8 maximum_select_fusion.2
  357.0 1.8 collective-permute-start.37
  359.1 5.2 shard_map.263.right.d_qkv
  364.3 4.2 all-reduce.6.cloned.1.call-done
  368.5 3.3 add_convert_fusion
  371.8 6.7 %shard_map.264 = bf16[4,144,3456]{2,1,0:T(8,128)(2,1)} custom-call(s32[4]{0:T(128)S(1)} %pad_add_fusion.2.spots, bf16[512,1152]{1,0:T(8,128)(2,1)} %get-tuple-element.205.left, bf16[512,3456]{1,0:T(8,128)(2,1)} %shard_map.263.right.d_qkv), custom_call_target="tpu_custom_call" | custom-call | flops 1800000000 | bytes 5939999 | tf_op jit(solution)/shard_map/pallas_call | solution.py:527
  378.6 2.1 shard_map.265
  380.7 12.5 %shard_map.266 = (bf16[512,1152]{1,0:T(8,128)(2,1)}, f32[2,1152]{1,0:T(2,128)}, f32[1,3456]{1,0:T(1,128)}) custom-call(bf16[512,3456]{1,0:T(8,128)(2,1)} %shard_map.263.right.d_qkv, bf16[1152,3456]{1,0:T(8,128)(2,1)} %all-gather.5.cloned.1.call-done.matrix, bf16[512,1152]{1,0:T(8,128)(2,1)} %bitcast.106, f32[1,6912]{1,0:T(1,128)} %broadcast_in_dim.35.mods, ...), custom_call_target="tpu_custom_call" | custom-call | flops 71999995904 | bytes 237600000 | tf_op jit(solution)/shard_map/pallas_call | solution.py:431
  394.8 7.9 %shard_map.267 = (bf16[144,3456]{1,0:T(8,128)(2,1)}, bf16[144,3456]{1,0:T(8,128)(2,1)}, bf16[144,3456]{1,0:T(8,128)(2,1)}, bf16[72,3456]{1,0:T(8,128)(2,1)}, bf16[72,3456]{1,0:T(8,128)(2,1)}) custom-call(s32[4]{0:T(128)S(1)} %pad_add_fusion.3.spots, bf16[512,1152]{1,0:T(8,128)(2,1)} %get-tuple-element.205.left, bf16[512,3456]{1,0:T(8,128)(2,1)} %shard_map.263.right.d_qkv, ...), custom_call_target="tpu_custom_call" | custom-call | flops 1800000000 | bytes 5939999 | tf_op jit(solution)/shard_map/pallas_call | solution.py:527
  406.3 3.7 all-to-all-start.5
  411.2 2.0 collective-permute-start.48
  415.3 3.5 all-to-all-start.4
  419.1 13.0 %collective-permute-done.44.got_x = bf16[72,3456]{1,0:T(8,128)(2,1)} collective-permute-done((bf16[72,3456]{1,0:T(8,128)(2,1)}, bf16[72,3456]{1,0:T(8,128)(2,1)}, u32[]{:S(2)}, u32[]{:S(2)}) %collective-permute-start.44) | collective-permute-done | bytes 497696 | tf_op jit(solution)/shard_map/ppermute | solution.py:716
  433.5 3.9 shard_map.268
  437.8 1.7 collective-permute-start.50
  441.0 20.7 %all-reduce.8.cloned.1.call-done = bf16[144,4608]{1,0:T(8,128)(2,1)} async-done(((bf16[144,4608]{1,0:T(8,128)(2,1)}), bf16[144,4608]{1,0:T(8,128)(2,1)}) %all-reduce.8.cloned.1.call-update) | async-done | bytes 1327120 | tf_op jit(solution)/shard_map/psum | solution.py:801
  463.3 2.0 add_convert_fusion.3
  468.2 2.2 add_convert_fusion.2
  472.2 3.7 all-to-all-start.6
  477.5 2.6 fusion.9
  480.1 1.7 convert_element_type.214
  481.9 1.8 convert_element_type.213
  486.0 1.6 fusion
  487.6 46.2 %all-reduce.10.cloned.1.call-done = (bf16[152,3456]{1,0:T(8,128)(2,1)}, bf16[144,1152]{1,0:T(8,128)(2,1)}) async-done(((bf16[152,3456]{1,0:T(8,128)(2,1)}, bf16[144,1152]{1,0:T(8,128)(2,1)}), (bf16[152,3456]{1,0:T(8,128)(2,1)}, bf16[144,1152]{1,0:T(8,128)(2,1)})) %all-reduce.10.cloned.1.call-update) | async-done | bytes 1382416 | tf_op jit(solution)/shard_map/psum | solution.py:801
  (273 shorter events, 62.2 us)
Async XLA Ops:
  7.2 71.0 %all-gather.5.cloned.1.call-start = ((), (), s32[]{:S(2)}) async-start(), calls=%async_computation.7 | async-start | bytes 8957952 | tf_op jit(solution)/shard_map/all_gather | solution.py:711
  7.9 142.6 %all-gather.7.cloned.1.call-start = ((), (), s32[]{:S(2)}) async-start(), calls=%async_computation.8 | async-start | bytes 11943936 | tf_op jit(solution)/shard_map/all_gather | solution.py:711
  39.4 2.2 collective-permute-start
  43.0 33.9 %all-to-all-start = ((bf16[4,128,1152]{2,1,0:T(8,128)(2,1)}), bf16[4,128,1152]{2,1,0:T(8,128)(2,1)S(1)}, u32[]{:S(2)}, u32[]{:S(2)}) async-start(bf16[4,128,1152]{2,1,0:T(8,128)(2,1)} %bitcast.110), calls=%async_computation | async-start | bytes 2359296 | tf_op jit(solution)/shard_map/all_to_all | solution.py:697
  47.8 17.7 %collective-permute-start.1 = (bf16[144,1152]{1,0:T(8,128)(2,1)}, bf16[144,1152]{1,0:T(8,128)(2,1)}, u32[]{:S(2)}, u32[]{:S(2)}) collective-permute-start(bf16[144,1152]{1,0:T(8,128)(2,1)} %refs_0_.1), channel_id=1, source_target_pairs={{0,8},{4,12},{8,0},{12,4},{16,24},{20,28},{24,16},{28,20},{1,9},{5... | collective-permute-start | bytes 995336 | tf_op jit(solution)/shard_map/ppermute | solution.py:716
  47.8 17.7 %collective-permute-start.2 = (bf16[144,1152]{1,0:T(8,128)(2,1)}, bf16[144,1152]{1,0:T(8,128)(2,1)}, u32[]{:S(2)}, u32[]{:S(2)}) collective-permute-start(bf16[144,1152]{1,0:T(8,128)(2,1)} %refs_0_.1), channel_id=1, source_target_pairs={{0,16},{4,20},{8,24},{12,28},{16,0},{20,4},{24,8},{28,12},{1,17},{... | collective-permute-start | bytes 995336 | tf_op jit(solution)/shard_map/ppermute | solution.py:716
  66.5 10.4 %collective-permute-start.4 = (bf16[80,1152]{1,0:T(8,128)(2,1)S(1)}, bf16[80,1152]{1,0:T(8,128)(2,1)}, u32[]{:S(2)}, u32[]{:S(2)}) collective-permute-start(bf16[80,1152]{1,0:T(8,128)(2,1)S(1)} %slice.107), channel_id=1, source_target_pairs={{0,8},{4,12},{8,0},{12,4},{16,24},{20,28},{24,16},{28,20},{1,9},{5... | collective-permute-start | bytes 552968 | tf_op jit(solution)/shard_map/ppermute | solution.py:716
  70.0 6.0 %collective-permute-start.3 = (bf16[64,1152]{1,0:T(8,128)(2,1)}, bf16[64,1152]{1,0:T(8,128)(2,1)}, u32[]{:S(2)}, u32[]{:S(2)}) collective-permute-start(bf16[64,1152]{1,0:T(8,128)(2,1)} %slice.106), channel_id=1, source_target_pairs={{0,16},{4,20},{8,24},{12,28},{16,0},{20,4},{24,8},{28,12},{1,17},{... | collective-permute-start | bytes 442376 | tf_op jit(solution)/shard_map/ppermute | solution.py:716
  89.9 19.3 %collective-permute-start.10 = (bf16[512,1792]{1,0:T(8,128)(2,1)}, bf16[512,1792]{1,0:T(8,128)(2,1)}, u32[]{:S(2)}, u32[]{:S(2)}) collective-permute-start(bf16[512,1792]{1,0:T(8,128)(2,1)} %get-tuple-element.130), channel_id=1, source_target_pairs={{0,4},{4,0},{8,12},{12,8},{16,20},{20,16},{24,28},{28,24},{1,5},{5... | collective-permute-start | bytes 5505032 | tf_op jit(solution)/shard_map/ppermute | solution.py:682
  90.2 5.1 collective-permute-start.14
  90.6 11.0 %collective-permute-start.5 = (bf16[144,1152]{1,0:T(8,128)(2,1)}, bf16[144,1152]{1,0:T(8,128)(2,1)}, u32[]{:S(2)}, u32[]{:S(2)}) collective-permute-start(bf16[144,1152]{1,0:T(8,128)(2,1)} %refs_0_.1), channel_id=1, source_target_pairs={{0,4},{4,0},{8,12},{12,8},{16,20},{20,16},{24,28},{28,24},{1,5},{5... | collective-permute-start | bytes 995336 | tf_op jit(solution)/shard_map/ppermute | solution.py:716
  91.0 18.2 %collective-permute-start.6 = (bf16[144,1152]{1,0:T(8,128)(2,1)}, bf16[144,1152]{1,0:T(8,128)(2,1)}, u32[]{:S(2)}, u32[]{:S(2)}) collective-permute-start(bf16[144,1152]{1,0:T(8,128)(2,1)} %collective-permute-done.1.refs_1_), channel_id=1, source_target_pairs={{0,4},{4,0},{8,12},{12,8},{16,20},{20,16},{24,28},{28,24},{1,5},{5... | collective-permute-start | bytes 995336 | tf_op jit(solution)/shard_map/ppermute | solution.py:716
  91.2 18.0 %collective-permute-start.7 = (bf16[144,1152]{1,0:T(8,128)(2,1)}, bf16[144,1152]{1,0:T(8,128)(2,1)}, u32[]{:S(2)}, u32[]{:S(2)}) collective-permute-start(bf16[144,1152]{1,0:T(8,128)(2,1)} %collective-permute-done.2.refs_2_), channel_id=1, source_target_pairs={{0,4},{4,0},{8,12},{12,8},{16,20},{20,16},{24,28},{28,24},{1,5},{5... | collective-permute-start | bytes 995336 | tf_op jit(solution)/shard_map/ppermute | solution.py:716
  95.4 13.8 %collective-permute-start.9 = (bf16[80,1152]{1,0:T(8,128)(2,1)}, bf16[80,1152]{1,0:T(8,128)(2,1)S(1)}, u32[]{:S(2)}, u32[]{:S(2)}) collective-permute-start(bf16[80,1152]{1,0:T(8,128)(2,1)} %collective-permute-done.4.refs_4_), channel_id=1, source_target_pairs={{0,4},{4,0},{8,12},{12,8},{16,20},{20,16},{24,28},{28,24},{1,5},{5... | collective-permute-start | bytes 552968 | tf_op jit(solution)/shard_map/ppermute | solution.py:716
  96.9 40.8 %all-to-all-start.2 = ((bf16[4,128,1152]{2,1,0:T(8,128)(2,1)}), bf16[4,128,1152]{2,1,0:T(8,128)(2,1)S(1)}, u32[]{:S(2)}, u32[]{:S(2)}) async-start(bf16[4,128,1152]{2,1,0:T(8,128)(2,1)} %bitcast.107), calls=%async_computation.2 | async-start | bytes 2359296 | tf_op jit(solution)/shard_map/all_to_all | solution.py:697
  101.5 7.6 %collective-permute-start.8 = (bf16[64,1152]{1,0:T(8,128)(2,1)}, bf16[64,1152]{1,0:T(8,128)(2,1)}, u32[]{:S(2)}, u32[]{:S(2)}) collective-permute-start(bf16[64,1152]{1,0:T(8,128)(2,1)} %collective-permute-done.3.refs_3_), channel_id=1, source_target_pairs={{0,4},{4,0},{8,12},{12,8},{16,20},{20,16},{24,28},{28,24},{1,5},{5... | collective-permute-start | bytes 442376 | tf_op jit(solution)/shard_map/ppermute | solution.py:716
  109.0 27.5 %copy-start.1 = (s32[8]{0:T(128)}, s32[8]{0:T(128)S(1)}, u32[]{:S(2)}) copy-start(s32[8]{0:T(128)S(1)} %stack.228.limits) | copy-start | bytes 100
  136.5 4.6 collective-permute-start.11
  139.1 31.4 %collective-permute-start.12 = (bf16[576,1152]{1,0:T(8,128)(2,1)}, bf16[576,1152]{1,0:T(8,128)(2,1)}, u32[]{:S(2)}, u32[]{:S(2)}) collective-permute-start(bf16[576,1152]{1,0:T(8,128)(2,1)} %refs_0_.2), channel_id=1, source_target_pairs={{0,8},{4,12},{8,0},{12,4},{16,24},{20,28},{24,16},{28,20},{1,9},{5... | collective-permute-start | bytes 3981320 | tf_op jit(solution)/shard_map/ppermute | solution.py:716
  139.5 31.1 %collective-permute-start.13 = (bf16[576,1152]{1,0:T(8,128)(2,1)}, bf16[576,1152]{1,0:T(8,128)(2,1)}, u32[]{:S(2)}, u32[]{:S(2)}) collective-permute-start(bf16[576,1152]{1,0:T(8,128)(2,1)} %refs_0_.2), channel_id=1, source_target_pairs={{0,16},{4,20},{8,24},{12,28},{16,0},{20,4},{24,8},{28,12},{1,17},{... | collective-permute-start | bytes 3981320 | tf_op jit(solution)/shard_map/ppermute | solution.py:716
  180.3 22.6 %collective-permute-start.15 = (bf16[4,576,1152]{2,1,0:T(8,128)(2,1)}, bf16[4,576,1152]{2,1,0:T(8,128)(2,1)}, u32[]{:S(2)}, u32[]{:S(2)}) collective-permute-start(bf16[4,576,1152]{2,1,0:T(8,128)(2,1)} %shard_map.250), channel_id=1, source_target_pairs={{0,4},{4,0},{8,12},{12,8},{16,20},{20,16},{24,28},{28,24},{1,5},{5... | collective-permute-start | bytes 15925256 | tf_op jit(solution)/shard_map/ppermute | solution.py:716
  181.5 17.4 %collective-permute-start.16 = (bf16[288,1152]{1,0:T(8,128)(2,1)S(1)}, bf16[288,1152]{1,0:T(8,128)(2,1)S(1)}, u32[]{:S(2)}, u32[]{:S(2)}) collective-permute-start(bf16[288,1152]{1,0:T(8,128)(2,1)S(1)} %slice.116), channel_id=1, source_target_pairs={{0,16},{4,20},{8,24},{12,28},{16,0},{20,4},{24,8},{28,12},{1,17},{... | collective-permute-start | bytes 1990664 | tf_op jit(solution)/shard_map/ppermute | solution.py:716
  184.4 17.1 %collective-permute-start.17 = (bf16[288,1152]{1,0:T(8,128)(2,1)S(1)}, bf16[288,1152]{1,0:T(8,128)(2,1)S(1)}, u32[]{:S(2)}, u32[]{:S(2)}) collective-permute-start(bf16[288,1152]{1,0:T(8,128)(2,1)S(1)} %slice.117), channel_id=1, source_target_pairs={{0,8},{4,12},{8,0},{12,4},{16,24},{20,28},{24,16},{28,20},{1,9},{5... | collective-permute-start | bytes 1990664 | tf_op jit(solution)/shard_map/ppermute | solution.py:716
  186.2 29.4 %collective-permute-start.18 = (bf16[576,1152]{1,0:T(8,128)(2,1)}, bf16[576,1152]{1,0:T(8,128)(2,1)}, u32[]{:S(2)}, u32[]{:S(2)}) collective-permute-start(bf16[576,1152]{1,0:T(8,128)(2,1)} %refs_0_.2), channel_id=1, source_target_pairs={{0,4},{4,0},{8,12},{12,8},{16,20},{20,16},{24,28},{28,24},{1,5},{5... | collective-permute-start | bytes 3981320 | tf_op jit(solution)/shard_map/ppermute | solution.py:716
  202.4 15.3 %collective-permute-start.19 = (bf16[576,1152]{1,0:T(8,128)(2,1)}, bf16[576,1152]{1,0:T(8,128)(2,1)}, u32[]{:S(2)}, u32[]{:S(2)}) collective-permute-start(bf16[576,1152]{1,0:T(8,128)(2,1)} %collective-permute-done.12.refs_1_), channel_id=1, source_target_pairs={{0,4},{4,0},{8,12},{12,8},{16,20},{20,16},{24,28},{28,24},{1,5},{5... | collective-permute-start | bytes 3981320 | tf_op jit(solution)/shard_map/ppermute | solution.py:716
  202.4 15.3 %collective-permute-start.20 = (bf16[576,1152]{1,0:T(8,128)(2,1)}, bf16[576,1152]{1,0:T(8,128)(2,1)}, u32[]{:S(2)}, u32[]{:S(2)}) collective-permute-start(bf16[576,1152]{1,0:T(8,128)(2,1)} %collective-permute-done.13.refs_2_), channel_id=1, source_target_pairs={{0,4},{4,0},{8,12},{12,8},{16,20},{20,16},{24,28},{28,24},{1,5},{5... | collective-permute-start | bytes 3981320 | tf_op jit(solution)/shard_map/ppermute | solution.py:716
  203.0 14.4 %collective-permute-start.21 = (bf16[288,1152]{1,0:T(8,128)(2,1)S(1)}, bf16[288,1152]{1,0:T(8,128)(2,1)}, u32[]{:S(2)}, u32[]{:S(2)}) collective-permute-start(bf16[288,1152]{1,0:T(8,128)(2,1)S(1)} %collective-permute-done.16.refs_3_), channel_id=1, source_target_pairs={{0,4},{4,0},{8,12},{12,8},{16,20},{20,16},{24,28},{28,24},{1,5},{5... | collective-permute-start | bytes 1990664 | tf_op jit(solution)/shard_map/ppermute | solution.py:716
  203.0 14.7 %collective-permute-start.22 = (bf16[288,1152]{1,0:T(8,128)(2,1)}, bf16[288,1152]{1,0:T(8,128)(2,1)}, u32[]{:S(2)}, u32[]{:S(2)}) collective-permute-start(bf16[288,1152]{1,0:T(8,128)(2,1)} %copy-done.25), channel_id=1, source_target_pairs={{0,4},{4,0},{8,12},{12,8},{16,20},{20,16},{24,28},{28,24},{1,5},{5... | collective-permute-start | bytes 1990664 | tf_op jit(solution)/shard_map/ppermute | solution.py:716
  215.6 19.4 %collective-permute-start.23 = (bf16[288,1152]{1,0:T(8,128)(2,1)}, bf16[288,1152]{1,0:T(8,128)(2,1)S(1)}, u32[]{:S(2)}, u32[]{:S(2)}) collective-permute-start(bf16[288,1152]{1,0:T(8,128)(2,1)} %get-tuple-element.142), channel_id=1, source_target_pairs={{0,8},{4,12},{8,0},{12,4},{16,24},{20,28},{24,16},{28,20},{1,9},{5... | collective-permute-start | bytes 1990664 | tf_op jit(solution)/shard_map/ppermute | solution.py:716
  217.4 17.6 %collective-permute-start.24 = (bf16[288,1152]{1,0:T(8,128)(2,1)}, bf16[288,1152]{1,0:T(8,128)(2,1)S(1)}, u32[]{:S(2)}, u32[]{:S(2)}) collective-permute-start(bf16[288,1152]{1,0:T(8,128)(2,1)} %get-tuple-element.143), channel_id=1, source_target_pairs={{0,16},{4,20},{8,24},{12,28},{16,0},{20,4},{24,8},{28,12},{1,17},{... | collective-permute-start | bytes 1990664 | tf_op jit(solution)/shard_map/ppermute | solution.py:716
  240.5 47.4 %collective-permute-start.26 = (bf16[576,1152]{1,0:T(8,128)(2,1)}, bf16[576,1152]{1,0:T(8,128)(2,1)}, u32[]{:S(2)}, u32[]{:S(2)}) collective-permute-start(bf16[576,1152]{1,0:T(8,128)(2,1)} %get-tuple-element.155), channel_id=1, source_target_pairs={{0,8},{4,12},{8,0},{12,4},{16,24},{20,28},{24,16},{28,20},{1,9},{5... | collective-permute-start | bytes 3981320 | tf_op jit(solution)/shard_map/ppermute | solution.py:716
  240.7 47.1 %collective-permute-start.27 = (bf16[576,1152]{1,0:T(8,128)(2,1)}, bf16[576,1152]{1,0:T(8,128)(2,1)}, u32[]{:S(2)}, u32[]{:S(2)}) collective-permute-start(bf16[576,1152]{1,0:T(8,128)(2,1)} %get-tuple-element.156), channel_id=1, source_target_pairs={{0,16},{4,20},{8,24},{12,28},{16,0},{20,4},{24,8},{28,12},{1,17},{... | collective-permute-start | bytes 3981320 | tf_op jit(solution)/shard_map/ppermute | solution.py:716
  263.3 27.9 %collective-permute-start.28 = (bf16[4,144,4608]{2,1,0:T(8,128)(2,1)}, bf16[4,144,4608]{2,1,0:T(8,128)(2,1)}, u32[]{:S(2)}, u32[]{:S(2)}) collective-permute-start(bf16[4,144,4608]{2,1,0:T(8,128)(2,1)} %shard_map.255), channel_id=1, source_target_pairs={{0,4},{4,0},{8,12},{12,8},{16,20},{20,16},{24,28},{28,24},{1,5},{5... | collective-permute-start | bytes 15925256 | tf_op jit(solution)/shard_map/ppermute | solution.py:716
  263.3 43.7 %all-to-all-start.3 = ((bf16[4,128,1152]{2,1,0:T(8,128)(2,1)}), bf16[4,128,1152]{2,1,0:T(8,128)(2,1)S(1)}, u32[]{:S(2)}, u32[]{:S(2)}) async-start(bf16[4,128,1152]{2,1,0:T(8,128)(2,1)} %bitcast.116), calls=%async_computation.3 | async-start | bytes 2359296 | tf_op jit(solution)/shard_map/all_to_all | solution.py:703
  268.9 99.6 %all-reduce.6.cloned.1.call-start = ((), (), s32[]{:S(2)}) async-start(), calls=%async_computation.9 | async-start | bytes 2654208 | tf_op jit(solution)/shard_map/psum | solution.py:801
  304.0 28.1 %collective-permute-start.32 = (bf16[4,144,1152]{2,1,0:T(8,128)(2,1)}, bf16[4,144,1152]{2,1,0:T(8,128)(2,1)}, u32[]{:S(2)}, u32[]{:S(2)}) collective-permute-start(bf16[4,144,1152]{2,1,0:T(8,128)(2,1)} %shard_map.258), channel_id=1, source_target_pairs={{0,4},{4,0},{8,12},{12,8},{16,20},{20,16},{24,28},{28,24},{1,5},{5... | collective-permute-start | bytes 3981320 | tf_op jit(solution)/shard_map/ppermute | solution.py:716
  304.2 4.1 collective-permute-start.29
  304.6 21.1 %collective-permute-start.30 = (bf16[72,4608]{1,0:T(8,128)(2,1)}, bf16[72,4608]{1,0:T(8,128)(2,1)}, u32[]{:S(2)}, u32[]{:S(2)}) collective-permute-start(bf16[72,4608]{1,0:T(8,128)(2,1)} %get-tuple-element.173), channel_id=1, source_target_pairs={{0,8},{4,12},{8,0},{12,4},{16,24},{20,28},{24,16},{28,20},{1,9},{5... | collective-permute-start | bytes 1990664 | tf_op jit(solution)/shard_map/ppermute | solution.py:716
  306.4 19.3 %collective-permute-start.31 = (bf16[72,4608]{1,0:T(8,128)(2,1)}, bf16[72,4608]{1,0:T(8,128)(2,1)}, u32[]{:S(2)}, u32[]{:S(2)}) collective-permute-start(bf16[72,4608]{1,0:T(8,128)(2,1)} %get-tuple-element.174), channel_id=1, source_target_pairs={{0,16},{4,20},{8,24},{12,28},{16,0},{20,4},{24,8},{28,12},{1,17},{... | collective-permute-start | bytes 1990664 | tf_op jit(solution)/shard_map/ppermute | solution.py:716
  306.8 154.9 %all-reduce.8.cloned.1.call-start = ((), (), s32[]{:S(2)}) async-start(), calls=%async_computation.10 | async-start | bytes 2654208 | tf_op jit(solution)/shard_map/psum | solution.py:801
  308.2 45.9 %collective-permute-start.25 = (bf16[2,128,1152]{2,1,0:T(8,128)(2,1)}, bf16[2,128,1152]{2,1,0:T(8,128)(2,1)}, u32[]{:S(2)}, u32[]{:S(2)}) collective-permute-start(bf16[2,128,1152]{2,1,0:T(8,128)(2,1)} %get-tuple-element.240), channel_id=1, source_target_pairs={{0,4},{4,0},{8,12},{12,8},{16,20},{20,16},{24,28},{28,24},{1,5},{5... | collective-permute-start | bytes 1769480 | tf_op jit(solution)/shard_map/ppermute | solution.py:682
  325.3 33.4 %collective-permute-start.33 = (bf16[512,896]{1,0:T(8,128)(2,1)}, bf16[512,896]{1,0:T(8,128)(2,1)}, u32[]{:S(2)}, u32[]{:S(2)}) collective-permute-start(bf16[512,896]{1,0:T(8,128)(2,1)} %get-tuple-element.181), channel_id=1, source_target_pairs={{0,4},{4,0},{8,12},{12,8},{16,20},{20,16},{24,28},{28,24},{1,5},{5... | collective-permute-start | bytes 2752520 | tf_op jit(solution)/shard_map/ppermute | solution.py:682
  330.1 38.5 %collective-permute-start.35 = (bf16[144,4608]{1,0:T(8,128)(2,1)}, bf16[144,4608]{1,0:T(8,128)(2,1)}, u32[]{:S(2)}, u32[]{:S(2)}) collective-permute-start(bf16[144,4608]{1,0:T(8,128)(2,1)} %get-tuple-element.184), channel_id=1, source_target_pairs={{0,8},{4,12},{8,0},{12,4},{16,24},{20,28},{24,16},{28,20},{1,9},{5... | collective-permute-start | bytes 3981320 | tf_op jit(solution)/shard_map/ppermute | solution.py:716
  331.7 36.9 %collective-permute-start.36 = (bf16[144,4608]{1,0:T(8,128)(2,1)}, bf16[144,4608]{1,0:T(8,128)(2,1)}, u32[]{:S(2)}, u32[]{:S(2)}) collective-permute-start(bf16[144,4608]{1,0:T(8,128)(2,1)} %get-tuple-element.185), channel_id=1, source_target_pairs={{0,16},{4,20},{8,24},{12,28},{16,0},{20,4},{24,8},{28,12},{1,17},{... | collective-permute-start | bytes 3981320 | tf_op jit(solution)/shard_map/ppermute | solution.py:716
  353.2 5.8 %collective-permute-start.34 = (bf16[512,896]{1,0:T(8,128)(2,1)}, bf16[512,896]{1,0:T(8,128)(2,1)}, u32[]{:S(2)}, u32[]{:S(2)}) collective-permute-start(bf16[512,896]{1,0:T(8,128)(2,1)} %get-tuple-element.194), channel_id=1, source_target_pairs={{0,4},{4,0},{8,12},{12,8},{16,20},{20,16},{24,28},{28,24},{1,5},{5... | collective-permute-start | bytes 2752520 | tf_op jit(solution)/shard_map/ppermute | solution.py:682
  357.0 21.6 %collective-permute-start.37 = (bf16[72,1152]{1,0:T(8,128)(2,1)}, bf16[72,1152]{1,0:T(8,128)(2,1)}, u32[]{:S(2)}, u32[]{:S(2)}) collective-permute-start(bf16[72,1152]{1,0:T(8,128)(2,1)} %get-tuple-element.190), channel_id=1, source_target_pairs={{0,8},{4,12},{8,0},{12,4},{16,24},{20,28},{24,16},{28,20},{1,9},{5... | collective-permute-start | bytes 497672 | tf_op jit(solution)/shard_map/ppermute | solution.py:716
  358.7 19.9 %collective-permute-start.38 = (bf16[72,1152]{1,0:T(8,128)(2,1)}, bf16[72,1152]{1,0:T(8,128)(2,1)}, u32[]{:S(2)}, u32[]{:S(2)}) collective-permute-start(bf16[72,1152]{1,0:T(8,128)(2,1)} %get-tuple-element.191), channel_id=1, source_target_pairs={{0,16},{4,20},{8,24},{12,28},{16,0},{20,4},{24,8},{28,12},{1,17},{... | collective-permute-start | bytes 497672 | tf_op jit(solution)/shard_map/ppermute | solution.py:716
  378.5 16.3 %collective-permute-start.39 = (bf16[4,144,3456]{2,1,0:T(8,128)(2,1)}, bf16[4,144,3456]{2,1,0:T(8,128)(2,1)}, u32[]{:S(2)}, u32[]{:S(2)}) collective-permute-start(bf16[4,144,3456]{2,1,0:T(8,128)(2,1)} %shard_map.264), channel_id=1, source_target_pairs={{0,4},{4,0},{8,12},{12,8},{16,20},{20,16},{24,28},{28,24},{1,5},{5... | collective-permute-start | bytes 11943944 | tf_op jit(solution)/shard_map/ppermute | solution.py:716
  402.7 1.4 collective-permute-start.41
  404.2 5.8 %collective-permute-start.42 = (bf16[1,6912]{1,0:T(2,128)(2,1)S(1)}, bf16[1,6912]{1,0:T(2,128)(2,1)S(1)}, u32[]{:S(2)}, u32[]{:S(2)}) collective-permute-start(bf16[1,6912]{1,0:T(2,128)(2,1)S(1)} %broadcast_in_dim.38), channel_id=1, source_target_pairs={{0,1},{1,0},{2,3},{3,2},{4,5},{5,4},{6,7},{7,6},{8,9},{9,8},{10,11... | collective-permute-start | bytes 41480 | tf_op jit(solution)/shard_map/ppermute | solution.py:856
  406.3 9.0 %all-to-all-start.5 = ((f32[8,1,1152]{2,1,0:T(1,128)}), f32[8,1,1152]{2,1,0:T(1,128)S(1)}, u32[]{:S(2)}, u32[]{:S(2)}) async-start(f32[8,1,1152]{2,1,0:T(1,128)} %all_to_all.36), calls=%async_computation.5 | async-start | bytes 73728 | tf_op jit(solution)/shard_map/all_to_all | solution.py:1007
  410.1 8.9 %collective-permute-start.43 = (bf16[2,6912]{1,0:T(2,128)(2,1)S(1)}, bf16[2,6912]{1,0:T(2,128)(2,1)S(1)}, u32[]{:S(2)}, u32[]{:S(2)}) collective-permute-start(bf16[2,6912]{1,0:T(2,128)(2,1)S(1)} %pad_maximum_fusion.4), channel_id=1, source_target_pairs={{0,2},{1,3},{2,0},{3,1},{4,6},{5,7},{6,4},{7,5},{8,10},{9,11},{10,... | collective-permute-start | bytes 82952 | tf_op jit(solution)/shard_map/ppermute | solution.py:856
  411.2 52.1 %collective-permute-start.48 = (bf16[144,1152]{1,0:T(8,128)(2,1)}, bf16[144,1152]{1,0:T(8,128)(2,1)}, u32[]{:S(2)}, u32[]{:S(2)}) collective-permute-start(bf16[144,1152]{1,0:T(8,128)(2,1)} %get-tuple-element.200), channel_id=1, source_target_pairs={{0,8},{4,12},{8,0},{12,4},{16,24},{20,28},{24,16},{28,20},{1,9},{5... | collective-permute-start | bytes 995336 | tf_op jit(solution)/shard_map/ppermute | solution.py:716
  413.2 50.1 %collective-permute-start.49 = (bf16[144,1152]{1,0:T(8,128)(2,1)}, bf16[144,1152]{1,0:T(8,128)(2,1)}, u32[]{:S(2)}, u32[]{:S(2)}) collective-permute-start(bf16[144,1152]{1,0:T(8,128)(2,1)} %get-tuple-element.201), channel_id=1, source_target_pairs={{0,16},{4,20},{8,24},{12,28},{16,0},{20,4},{24,8},{28,12},{1,17},{... | collective-permute-start | bytes 995336 | tf_op jit(solution)/shard_map/ppermute | solution.py:716
  414.7 17.4 %collective-permute-start.44 = (bf16[72,3456]{1,0:T(8,128)(2,1)}, bf16[72,3456]{1,0:T(8,128)(2,1)}, u32[]{:S(2)}, u32[]{:S(2)}) collective-permute-start(bf16[72,3456]{1,0:T(8,128)(2,1)} %get-tuple-element.209), channel_id=1, source_target_pairs={{0,8},{4,12},{8,0},{12,4},{16,24},{20,28},{24,16},{28,20},{1,9},{5... | collective-permute-start | bytes 1493000 | tf_op jit(solution)/shard_map/ppermute | solution.py:716
  415.2 18.2 %collective-permute-start.45 = (bf16[72,3456]{1,0:T(8,128)(2,1)}, bf16[72,3456]{1,0:T(8,128)(2,1)}, u32[]{:S(2)}, u32[]{:S(2)}) collective-permute-start(bf16[72,3456]{1,0:T(8,128)(2,1)} %get-tuple-element.210), channel_id=1, source_target_pairs={{0,16},{4,20},{8,24},{12,28},{16,0},{20,4},{24,8},{28,12},{1,17},{... | collective-permute-start | bytes 1493000 | tf_op jit(solution)/shard_map/ppermute | solution.py:716
  415.3 56.9 %all-to-all-start.4 = ((bf16[4,128,1152]{2,1,0:T(8,128)(2,1)}), bf16[4,128,1152]{2,1,0:T(8,128)(2,1)S(1)}, u32[]{:S(2)}, u32[]{:S(2)}) async-start(bf16[4,128,1152]{2,1,0:T(8,128)(2,1)} %bitcast.115), calls=%async_computation.4 | async-start | bytes 2359296 | tf_op jit(solution)/shard_map/all_to_all | solution.py:703
  418.8 115.0 %all-reduce.10.cloned.1.call-start = ((), (), s32[]{:S(2)}) async-start(), calls=%async_computation.11 | async-start | bytes 2764800 | tf_op jit(solution)/shard_map/psum | solution.py:801
  437.4 24.3 %collective-permute-start.46 = (bf16[4,6912]{1,0:T(4,128)(2,1)S(1)}, bf16[4,6912]{1,0:T(4,128)(2,1)S(1)}, u32[]{:S(2)}, u32[]{:S(2)}) collective-permute-start(bf16[4,6912]{1,0:T(4,128)(2,1)S(1)} %pad_maximum_fusion.3), channel_id=1, source_target_pairs={{0,8},{4,12},{8,0},{12,4},{16,24},{20,28},{24,16},{28,20},{1,9},{5... | collective-permute-start | bytes 165896 | tf_op jit(solution)/shard_map/ppermute | solution.py:716
  437.8 30.4 %collective-permute-start.50 = (bf16[144,3456]{1,0:T(8,128)(2,1)}, bf16[144,3456]{1,0:T(8,128)(2,1)}, u32[]{:S(2)}, u32[]{:S(2)}) collective-permute-start(bf16[144,3456]{1,0:T(8,128)(2,1)} %get-tuple-element.221), channel_id=1, source_target_pairs={{0,8},{4,12},{8,0},{12,4},{16,24},{20,28},{24,16},{28,20},{1,9},{5... | collective-permute-start | bytes 2985992 | tf_op jit(solution)/shard_map/ppermute | solution.py:716
  439.5 28.7 %collective-permute-start.51 = (bf16[144,3456]{1,0:T(8,128)(2,1)}, bf16[144,3456]{1,0:T(8,128)(2,1)}, u32[]{:S(2)}, u32[]{:S(2)}) collective-permute-start(bf16[144,3456]{1,0:T(8,128)(2,1)} %get-tuple-element.222), channel_id=1, source_target_pairs={{0,16},{4,20},{8,24},{12,28},{16,0},{20,4},{24,8},{28,12},{1,17},{... | collective-permute-start | bytes 2985992 | tf_op jit(solution)/shard_map/ppermute | solution.py:716
  461.7 4.8 collective-permute-start.47
  472.2 13.0 %all-to-all-start.6 = ((f32[8,1,288]{2,1,0:T(1,128)}), f32[8,1,288]{2,1,0:T(1,128)S(1)}, u32[]{:S(2)}, u32[]{:S(2)}) async-start(f32[8,1,288]{2,1,0:T(1,128)} %all_to_all.38), calls=%async_computation.6 | async-start | bytes 24576 | tf_op jit(solution)/shard_map/all_to_all | solution.py:1022
  477.0 9.0 %collective-permute-start.40 = (bf16[2,128,1152]{2,1,0:T(8,128)(2,1)}, bf16[2,128,1152]{2,1,0:T(8,128)(2,1)S(1)}, u32[]{:S(2)}, u32[]{:S(2)}) collective-permute-start(bf16[2,128,1152]{2,1,0:T(8,128)(2,1)} %get-tuple-element.238), channel_id=1, source_target_pairs={{0,4},{4,0},{8,12},{12,8},{16,20},{20,16},{24,28},{28,24},{1,5},{5... | collective-permute-start | bytes 1769480 | tf_op jit(solution)/shard_map/ppermute | solution.py:682
  (26 other events, 223.2 us)
Sparse Core Ops, SparseCore 0:
  9.9 68.1 all-gather.4
  80.0 63.9 all-gather.6
  306.9 61.5 all-reduce.5
  378.7 82.9 all-reduce.7
  471.6 62.2 all-reduce.9

commit v5 on v4

--- a/solution.py
+++ b/solution.py
@@ -935,6 +935,7 @@
 
     limits = [count - (slot_dev * i + half * (c ^ part)) for part in range(2) for i in range(4)]
     limits = jnp.stack(limits).astype(jnp.int32)
+    tokens16 = after(tokens16, limits)
 
     offsets = jnp.concatenate([qv_offset[:width], jnp.zeros((width,), f32), qv_offset[width:]])
     mine, away, moved = project(core, qkv_matrix, tokens16, modulation, offsets[None])

time: 555 us -> 554 us (level)
  transfers between devices with their start and end apart: 63 -> 63, of which waited for: 18 -> 17; matrix products, arithmetic and copies ran while one was open for 10% -> 10% of each run, Pallas kernels for 41% -> 42%
where the time goes in v5:
time: 554 us; the launch traced here: 545 us
  Pallas kernels  240 us (43%)
  waiting for transfers between devices  137 us (25%)
  starting transfers between devices  60.3 us (11%)
  other arithmetic  31.2 us (6%)
  local copies, waits for them, and re-layouts  30.2 us (5%)
  blocking collectives  22.5 us (4%)
  between operations  19.9 us (4%)
    psum x3, waiting for transfers between devices, finish(): total = lax.psum(part, 'seq')  71 us
    ppermute x40, waiting for transfers between devices, hop(): return lax.ppermute(array, 'batch', [(i, i ^ bits) for i in range(size)])  54.1 us
    pallas_call x6, Pallas kernels, block_grad(): pl.pallas_call(functools.partial(block_grad_kernel, len(gots)), out_shape...  39.5 us
    pallas_call x2, Pallas kernels, attend_back(): pl.pallas_call(functools.partial(back_kernel, heads, first, number), out_...  34 us
    ppermute x40, starting transfers between devices, hop(): return lax.ppermute(array, 'batch', [(i, i ^ bits) for i in range(size)])  29.3 us
    pallas_call x1, Pallas kernels, attend(): pl.pallas_call(functools.partial(attend_kernel, heads), out_shape=(shaped...  27.2 us
    pallas_call x2, Pallas kernels, pair_grad(): pl.pallas_call(functools.partial(pair_grad_kernel, len(gots)), out_shape=...  21 us
    pallas_call x1, Pallas kernels, middle_back(): pl.pallas_call(middle_back_kernel, out_shape=(shaped((rows, width), f32),...  18.9 us
  transfers between devices with their start and end apart: 63, of which 17 were waited for; matrix products, arithmetic and copies ran while one was open for 10% of the time, Pallas kernels for 42%

profile of v5, /device:TPU:0, one launch (start us, length us, event | category | flops | bytes accessed | tf_op | source)
XLA Modules:
  0.0 545.3 jit_solution(14990574544061196952)
XLA Ops:
  10.0 2.8 concatenate.37
  12.8 10.7 %all-gather.1 = bf16[8,1,3584]{2,1,0:T(2,128)(2,1)S(1)} all-gather(bf16[1,1,3584]{2,1,0:T(2,128)(2,1)S(1)} %reshape.215), channel_id=2, replica_groups=mesh['batch'=8,'seq'=4] {'batch'}, dimensions={0}, use_global_device_ids=true | all-gather | bytes 64512 | tf_op jit(solution)/shard_map/all_gather | solution.py:711
  24.7 11.8 %all_to_all.47 = f32[8,1,6912]{2,1,0:T(1,128)S(1)} all-to-all(f32[8,1,6912]{2,1,0:T(1,128)S(1)} %all_to_all.31), channel_id=1, replica_groups=mesh['batch'=8,'seq'=4] {'batch'}, dimensions={0} | all-to-all | bytes 442368 | tf_op jit(solution)/shard_map/all_to_all | solution.py:929
  37.3 2.2 dynamic-slice_bitcast_fusion.7
  39.4 2.2 collective-permute-done
  43.0 4.9 all-to-all-start
  49.0 16.6 %collective-permute-done.1.refs_1_ = bf16[144,1152]{1,0:T(8,128)(2,1)} collective-permute-done((bf16[144,1152]{1,0:T(8,128)(2,1)}, bf16[144,1152]{1,0:T(8,128)(2,1)}, u32[]{:S(2)}, u32[]{:S(2)}) %collective-permute-start.1) | collective-permute-done | bytes 331808 | tf_op jit(solution)/shard_map/ppermute | solution.py:716
  66.5 2.0 collective-permute-start.4
  68.4 1.6 slice.106
  78.4 11.7 %shard_map.246 = (bf16[512,1728]{1,0:T(8,128)(2,1)}, bf16[512,1792]{1,0:T(8,128)(2,1)}, bf16[512,1152]{1,0:T(8,128)(2,1)}) custom-call(s32[1]{0:T(128)} %bitcast.core, bf16[512,1152]{1,0:T(8,128)(2,1)} %bitcast.103, f32[1,6912]{1,0:T(1,128)} %broadcast_in_dim.35.mods, f32[1,3456]{1,0:T(1,128)} %broadcast_in_dim.37.offset, ...), custom_call_target="tpu_custom_call" | custom-call | flops 7800000000 | bytes 25740000 | tf_op jit(solution)/shard_map/pallas_call | solution.py:162
  91.5 3.8 collective-permute-done.14
  96.9 5.1 all-to-all-start.2
  103.9 27.2 %shard_map.247 = (bf16[512,576]{1,0:T(8,128)(2,1)}, bf16[512,640]{1,0:T(8,128)(2,1)}, f32[8,1024]{1,0:T(8,128)}) custom-call(s32[8]{0:T(128)S(1)} %stack.228.limits, bf16[512,1728]{1,0:T(8,128)(2,1)} %get-tuple-element.194.mine, bf16[512,1792]{1,0:T(8,128)(2,1)} %collective-permute-done.10.theirs), custom_call_target="tpu_custom_call" | custom-call | flops 16199999488 | bytes 53460000 | tf_op jit(solution)/shard_map/pallas_call | solution.py:608
  135.3 9.5 %shard_map.248 = (bf16[512,1152]{1,0:T(8,128)(2,1)}, f32[512,1152]{1,0:T(8,128)}, f32[512,1152]{1,0:T(8,128)}, f32[512,1]{1,0:T(8,128)}, bf16[512,1152]{1,0:T(8,128)(2,1)}, /*index=5*/bf16[1152,1152]{1,0:T(8,128)(2,1)}) custom-call(s32[1]{0:T(128)} %bitcast.core, s32[10]{0:T(128)S(1)} %stack.219.spots, bf16[512,576]{1,0:T(8,128)(2,1)} %get-tuple-element.133.own, ...), custom_call_target="tpu_custom_call" | custom-call | flops 5400000000 | bytes 17820000 | tf_op jit(solution)/shard_map/pallas_call | solution.py:213
  144.9 4.0 all-gather.7.cloned.1.call-done.matrix
  148.8 16.3 %shard_map.249 = (bf16[512,4608]{1,0:T(8,128)(2,1)}, f32[512,4608]{1,0:T(8,128)}) custom-call(bf16[512,1152]{1,0:T(8,128)(2,1)} %get-tuple-element.171.moved.left, bf16[1152,4608]{1,0:T(8,128)(2,1)} %all-gather.7.cloned.1.call-done.matrix, f32[1,4608]{1,0:T(1,128)} %reshape.211.offset), custom_call_target="tpu_custom_call" | custom-call | flops 9600000000 | bytes 31680000 | tf_op jit(solution)/shard_map/pallas_call | solution.py:247
  165.2 5.3 collective-permute-done.12.refs_1_
  170.4 9.8 %shard_map.250 = bf16[4,576,1152]{2,1,0:T(8,128)(2,1)} custom-call(s32[2]{0:T(128)S(1)} %pad_add_fusion.1.where, bf16[512,4608]{1,0:T(8,128)(2,1)} %get-tuple-element.159.left.act, bf16[512,1152]{1,0:T(8,128)(2,1)} %multiply_convert_fusion.1.right.grad), custom_call_target="tpu_custom_call" | custom-call | flops 5400000000 | bytes 17820000 | tf_op jit(solution)/shard_map/pallas_call | solution.py:487
  181.4 1.5 collective-permute-start.16
  184.7 14.1 %collective-permute-done.16.refs_3_ = bf16[288,1152]{1,0:T(8,128)(2,1)S(1)} collective-permute-done((bf16[288,1152]{1,0:T(8,128)(2,1)S(1)}, bf16[288,1152]{1,0:T(8,128)(2,1)S(1)}, u32[]{:S(2)}, u32[]{:S(2)}) %collective-permute-start.16) | collective-permute-done | bytes 663584 | tf_op jit(solution)/shard_map/ppermute | solution.py:716
  198.8 2.4 collective-permute-done.17.refs_4_
  204.1 11.2 %shard_map.251 = (bf16[576,1152]{1,0:T(8,128)(2,1)}, bf16[576,1152]{1,0:T(8,128)(2,1)}, bf16[576,1152]{1,0:T(8,128)(2,1)}, bf16[288,1152]{1,0:T(8,128)(2,1)}, bf16[288,1152]{1,0:T(8,128)(2,1)}) custom-call(s32[2]{0:T(128)S(1)} %pad_add_fusion.where, bf16[512,4608]{1,0:T(8,128)(2,1)} %get-tuple-element.159.left.act, ...), custom_call_target="tpu_custom_call" | custom-call | flops 5400000000 | bytes 17820000 | tf_op jit(solution)/shard_map/pallas_call | solution.py:487
  217.3 17.2 %shard_map.252 = (bf16[512,4608]{1,0:T(8,128)(2,1)}, f32[1,4608]{1,0:T(1,128)}, bf16[4608,1152]{1,0:T(8,128)(2,1)}) custom-call(s32[10]{0:T(128)S(1)} %stack.251.spots, bf16[512,1152]{1,0:T(8,128)(2,1)} %multiply_convert_fusion.1.right.grad, f32[512,4608]{1,0:T(8,128)} %get-tuple-element.147.slope, bf16[576,1152]{1,0:T(8,128)(2,1)} %refs_0_.2, ...), custom_call_target="tpu_custom_call" | custom-call | flops 24000000000 | bytes 79200000 | tf_op jit(solution)/shard_map/pallas_call | solution.py:288
  236.3 3.8 shard_map.253
  240.6 1.5 collective-permute-start.27
  242.1 13.0 %shard_map.254 = (bf16[512,1152]{1,0:T(8,128)(2,1)}, f32[1,1152]{1,0:T(1,128)}) custom-call(bf16[512,4608]{1,0:T(8,128)(2,1)} %get-tuple-element.159.left.act, bf16[4608,1152]{1,0:T(8,128)(2,1)} %get-tuple-element.160.matrix, f32[1,1152]{1,0:T(1,128)} %reshape.212.offset, bf16[512,1152]{1,0:T(8,128)(2,1)} %bitcast.105, ...), custom_call_target="tpu_custom_call" | custom-call | flops 3600000000 | bytes 11879999 | tf_op jit(solution)/shard_map/pallas_call | solution.py:331
  255.1 7.8 %shard_map.255 = bf16[4,144,4608]{2,1,0:T(8,128)(2,1)} custom-call(s32[4]{0:T(128)S(1)} %pad_add_fusion.2.spots, bf16[512,1152]{1,0:T(8,128)(2,1)} %get-tuple-element.171.moved.left, bf16[512,4608]{1,0:T(8,128)(2,1)} %get-tuple-element.165.right.d_upper), custom_call_target="tpu_custom_call" | custom-call | flops 2400000000 | bytes 7920000 | tf_op jit(solution)/shard_map/pallas_call | solution.py:527
  263.0 4.6 all-to-all-start.3
  267.6 18.9 %shard_map.256 = (f32[512,1152]{1,0:T(8,128)}, bf16[512,1152]{1,0:T(8,128)(2,1)}, bf16[512,576]{1,0:T(8,128)(2,1)}, bf16[512,640]{1,0:T(8,128)(2,1)}, f32[4,1152]{1,0:T(4,128)}) custom-call(s32[1]{0:T(128)} %bitcast.core, bf16[512,4608]{1,0:T(8,128)(2,1)} %get-tuple-element.165.right.d_upper, bf16[1152,4608]{1,0:T(8,128)(2,1)} %all-gather.7.cloned.1.call-done.matrix, ...), custom_call_target="tpu_custom_call" | custom-call | flops 89999998976 | bytes 297000000 | tf_op jit(solution)/shard_map/pallas_call | solution.py:383
  286.5 3.3 add_convert_fusion.1
  289.8 8.8 %shard_map.257 = (bf16[144,4608]{1,0:T(8,128)(2,1)}, bf16[144,4608]{1,0:T(8,128)(2,1)}, bf16[144,4608]{1,0:T(8,128)(2,1)}, bf16[72,4608]{1,0:T(8,128)(2,1)}, bf16[72,4608]{1,0:T(8,128)(2,1)}) custom-call(s32[4]{0:T(128)S(1)} %pad_add_fusion.3.spots, bf16[512,1152]{1,0:T(8,128)(2,1)} %get-tuple-element.171.moved.left, ...), custom_call_target="tpu_custom_call" | custom-call | flops 2400000000 | bytes 7920000 | tf_op jit(solution)/shard_map/pallas_call | solution.py:527
  298.6 4.0 shard_map.258
  303.9 1.5 collective-permute-start.31
  306.9 17.0 %shard_map.259 = (bf16[512,864]{1,0:T(8,128)(2,1)}, bf16[512,896]{1,0:T(8,128)(2,1)}) custom-call(s32[8]{0:T(128)S(1)} %copy-done.2, bf16[512,1728]{1,0:T(8,128)(2,1)} %get-tuple-element.194.mine, bf16[512,1792]{1,0:T(8,128)(2,1)} %collective-permute-done.10.theirs, bf16[512,576]{1,0:T(8,128)(2,1)} %get-tuple-element.169.d_mine, ...), custom_call_target="tpu_custom_call" | custom-call | flops 2400000000 | bytes 7920000 | tf_op jit(solution)/shard_map/pallas_call | solution.py:661
  324.3 4.4 shard_map.260
  329.2 1.5 collective-permute-start.36
  330.7 4.3 shard_map.261
  334.9 17.0 %shard_map.262 = (bf16[512,864]{1,0:T(8,128)(2,1)}, bf16[512,896]{1,0:T(8,128)(2,1)}) custom-call(s32[8]{0:T(128)S(1)} %copy-done.2, bf16[512,1728]{1,0:T(8,128)(2,1)} %get-tuple-element.194.mine, bf16[512,1792]{1,0:T(8,128)(2,1)} %collective-permute-done.10.theirs, bf16[512,576]{1,0:T(8,128)(2,1)} %get-tuple-element.169.d_mine, ...), custom_call_target="tpu_custom_call" | custom-call | flops 2400000000 | bytes 7920000 | tf_op jit(solution)/shard_map/pallas_call | solution.py:661
  352.8 2.8 maximum_select_fusion.2
  356.2 1.5 collective-permute-start.38
  357.7 5.2 shard_map.263.right.d_qkv
  362.9 4.0 all-reduce.6.cloned.1.call-done
  366.9 3.3 add_convert_fusion
  370.2 6.7 %shard_map.264 = bf16[4,144,3456]{2,1,0:T(8,128)(2,1)} custom-call(s32[4]{0:T(128)S(1)} %pad_add_fusion.2.spots, bf16[512,1152]{1,0:T(8,128)(2,1)} %get-tuple-element.207.left, bf16[512,3456]{1,0:T(8,128)(2,1)} %shard_map.263.right.d_qkv), custom_call_target="tpu_custom_call" | custom-call | flops 1800000000 | bytes 5939999 | tf_op jit(solution)/shard_map/pallas_call | solution.py:527
  377.0 2.1 shard_map.265
  379.0 12.5 %shard_map.266 = (bf16[512,1152]{1,0:T(8,128)(2,1)}, f32[2,1152]{1,0:T(2,128)}, f32[1,3456]{1,0:T(1,128)}) custom-call(bf16[512,3456]{1,0:T(8,128)(2,1)} %shard_map.263.right.d_qkv, bf16[1152,3456]{1,0:T(8,128)(2,1)} %all-gather.5.cloned.1.call-done.matrix, bf16[512,1152]{1,0:T(8,128)(2,1)} %bitcast.106, f32[1,6912]{1,0:T(1,128)} %broadcast_in_dim.35.mods, ...), custom_call_target="tpu_custom_call" | custom-call | flops 71999995904 | bytes 237600000 | tf_op jit(solution)/shard_map/pallas_call | solution.py:431
  393.2 7.9 %shard_map.267 = (bf16[144,3456]{1,0:T(8,128)(2,1)}, bf16[144,3456]{1,0:T(8,128)(2,1)}, bf16[144,3456]{1,0:T(8,128)(2,1)}, bf16[72,3456]{1,0:T(8,128)(2,1)}, bf16[72,3456]{1,0:T(8,128)(2,1)}) custom-call(s32[4]{0:T(128)S(1)} %pad_add_fusion.3.spots, bf16[512,1152]{1,0:T(8,128)(2,1)} %get-tuple-element.207.left, bf16[512,3456]{1,0:T(8,128)(2,1)} %shard_map.263.right.d_qkv, ...), custom_call_target="tpu_custom_call" | custom-call | flops 1800000000 | bytes 5939999 | tf_op jit(solution)/shard_map/pallas_call | solution.py:527
  404.7 3.7 all-to-all-start.5
  409.6 2.0 collective-permute-start.48
  413.7 3.5 all-to-all-start.4
  417.4 13.0 %collective-permute-done.44.got_x = bf16[72,3456]{1,0:T(8,128)(2,1)} collective-permute-done((bf16[72,3456]{1,0:T(8,128)(2,1)}, bf16[72,3456]{1,0:T(8,128)(2,1)}, u32[]{:S(2)}, u32[]{:S(2)}) %collective-permute-start.44) | collective-permute-done | bytes 497696 | tf_op jit(solution)/shard_map/ppermute | solution.py:716
  431.9 3.9 shard_map.268
  436.1 1.7 collective-permute-start.50
  437.9 1.5 collective-permute-start.51
  439.3 20.7 %all-reduce.8.cloned.1.call-done = bf16[144,4608]{1,0:T(8,128)(2,1)} async-done(((bf16[144,4608]{1,0:T(8,128)(2,1)}), bf16[144,4608]{1,0:T(8,128)(2,1)}) %all-reduce.8.cloned.1.call-update) | async-done | bytes 1327120 | tf_op jit(solution)/shard_map/psum | solution.py:801
  460.1 1.6 collective-permute-start.47
  461.7 2.0 add_convert_fusion.3
  466.6 2.2 add_convert_fusion.2
  470.5 3.7 all-to-all-start.6
  475.9 2.6 fusion.9
  478.5 1.7 convert_element_type.214
  480.3 1.8 convert_element_type.213
  484.4 1.6 fusion
  486.0 46.2 %all-reduce.10.cloned.1.call-done = (bf16[152,3456]{1,0:T(8,128)(2,1)}, bf16[144,1152]{1,0:T(8,128)(2,1)}) async-done(((bf16[152,3456]{1,0:T(8,128)(2,1)}, bf16[144,1152]{1,0:T(8,128)(2,1)}), (bf16[152,3456]{1,0:T(8,128)(2,1)}, bf16[144,1152]{1,0:T(8,128)(2,1)})) %all-reduce.10.cloned.1.call-update) | async-done | bytes 1382416 | tf_op jit(solution)/shard_map/psum | solution.py:801
  (273 shorter events, 60.9 us)
Async XLA Ops:
  7.2 71.0 %all-gather.5.cloned.1.call-start = ((), (), s32[]{:S(2)}) async-start(), calls=%async_computation.7 | async-start | bytes 8957952 | tf_op jit(solution)/shard_map/all_gather | solution.py:711
  7.9 140.9 %all-gather.7.cloned.1.call-start = ((), (), s32[]{:S(2)}) async-start(), calls=%async_computation.8 | async-start | bytes 11943936 | tf_op jit(solution)/shard_map/all_gather | solution.py:711
  39.4 2.2 collective-permute-start
  43.0 34.5 %all-to-all-start = ((bf16[4,128,1152]{2,1,0:T(8,128)(2,1)}), bf16[4,128,1152]{2,1,0:T(8,128)(2,1)S(1)}, u32[]{:S(2)}, u32[]{:S(2)}) async-start(bf16[4,128,1152]{2,1,0:T(8,128)(2,1)} %bitcast.107), calls=%async_computation | async-start | bytes 2359296 | tf_op jit(solution)/shard_map/all_to_all | solution.py:697
  47.8 17.7 %collective-permute-start.1 = (bf16[144,1152]{1,0:T(8,128)(2,1)}, bf16[144,1152]{1,0:T(8,128)(2,1)}, u32[]{:S(2)}, u32[]{:S(2)}) collective-permute-start(bf16[144,1152]{1,0:T(8,128)(2,1)} %refs_0_.1), channel_id=1, source_target_pairs={{0,8},{4,12},{8,0},{12,4},{16,24},{20,28},{24,16},{28,20},{1,9},{5... | collective-permute-start | bytes 995336 | tf_op jit(solution)/shard_map/ppermute | solution.py:716
  47.8 17.7 %collective-permute-start.2 = (bf16[144,1152]{1,0:T(8,128)(2,1)}, bf16[144,1152]{1,0:T(8,128)(2,1)}, u32[]{:S(2)}, u32[]{:S(2)}) collective-permute-start(bf16[144,1152]{1,0:T(8,128)(2,1)} %refs_0_.1), channel_id=1, source_target_pairs={{0,16},{4,20},{8,24},{12,28},{16,0},{20,4},{24,8},{28,12},{1,17},{... | collective-permute-start | bytes 995336 | tf_op jit(solution)/shard_map/ppermute | solution.py:716
  66.5 10.9 %collective-permute-start.4 = (bf16[80,1152]{1,0:T(8,128)(2,1)S(1)}, bf16[80,1152]{1,0:T(8,128)(2,1)}, u32[]{:S(2)}, u32[]{:S(2)}) collective-permute-start(bf16[80,1152]{1,0:T(8,128)(2,1)S(1)} %slice.107), channel_id=1, source_target_pairs={{0,8},{4,12},{8,0},{12,4},{16,24},{20,28},{24,16},{28,20},{1,9},{5... | collective-permute-start | bytes 552968 | tf_op jit(solution)/shard_map/ppermute | solution.py:716
  70.0 7.4 %collective-permute-start.3 = (bf16[64,1152]{1,0:T(8,128)(2,1)}, bf16[64,1152]{1,0:T(8,128)(2,1)}, u32[]{:S(2)}, u32[]{:S(2)}) collective-permute-start(bf16[64,1152]{1,0:T(8,128)(2,1)} %slice.106), channel_id=1, source_target_pairs={{0,16},{4,20},{8,24},{12,28},{16,0},{20,4},{24,8},{28,12},{1,17},{... | collective-permute-start | bytes 442376 | tf_op jit(solution)/shard_map/ppermute | solution.py:716
  90.2 13.8 %collective-permute-start.10 = (bf16[512,1792]{1,0:T(8,128)(2,1)}, bf16[512,1792]{1,0:T(8,128)(2,1)}, u32[]{:S(2)}, u32[]{:S(2)}) collective-permute-start(bf16[512,1792]{1,0:T(8,128)(2,1)} %get-tuple-element.132), channel_id=1, source_target_pairs={{0,4},{4,0},{8,12},{12,8},{16,20},{20,16},{24,28},{28,24},{1,5},{5... | collective-permute-start | bytes 5505032 | tf_op jit(solution)/shard_map/ppermute | solution.py:682
  90.3 5.0 collective-permute-start.14
  90.8 11.3 %collective-permute-start.5 = (bf16[144,1152]{1,0:T(8,128)(2,1)}, bf16[144,1152]{1,0:T(8,128)(2,1)}, u32[]{:S(2)}, u32[]{:S(2)}) collective-permute-start(bf16[144,1152]{1,0:T(8,128)(2,1)} %refs_0_.1), channel_id=1, source_target_pairs={{0,4},{4,0},{8,12},{12,8},{16,20},{20,16},{24,28},{28,24},{1,5},{5... | collective-permute-start | bytes 995336 | tf_op jit(solution)/shard_map/ppermute | solution.py:716
  91.0 12.9 %collective-permute-start.6 = (bf16[144,1152]{1,0:T(8,128)(2,1)}, bf16[144,1152]{1,0:T(8,128)(2,1)}, u32[]{:S(2)}, u32[]{:S(2)}) collective-permute-start(bf16[144,1152]{1,0:T(8,128)(2,1)} %collective-permute-done.1.refs_1_), channel_id=1, source_target_pairs={{0,4},{4,0},{8,12},{12,8},{16,20},{20,16},{24,28},{28,24},{1,5},{5... | collective-permute-start | bytes 995336 | tf_op jit(solution)/shard_map/ppermute | solution.py:716
  91.4 12.5 %collective-permute-start.7 = (bf16[144,1152]{1,0:T(8,128)(2,1)}, bf16[144,1152]{1,0:T(8,128)(2,1)}, u32[]{:S(2)}, u32[]{:S(2)}) collective-permute-start(bf16[144,1152]{1,0:T(8,128)(2,1)} %collective-permute-done.2.refs_2_), channel_id=1, source_target_pairs={{0,4},{4,0},{8,12},{12,8},{16,20},{20,16},{24,28},{28,24},{1,5},{5... | collective-permute-start | bytes 995336 | tf_op jit(solution)/shard_map/ppermute | solution.py:716
  95.3 8.6 %collective-permute-start.9 = (bf16[80,1152]{1,0:T(8,128)(2,1)}, bf16[80,1152]{1,0:T(8,128)(2,1)S(1)}, u32[]{:S(2)}, u32[]{:S(2)}) collective-permute-start(bf16[80,1152]{1,0:T(8,128)(2,1)} %collective-permute-done.4.refs_4_), channel_id=1, source_target_pairs={{0,4},{4,0},{8,12},{12,8},{16,20},{20,16},{24,28},{28,24},{1,5},{5... | collective-permute-start | bytes 552968 | tf_op jit(solution)/shard_map/ppermute | solution.py:716
  96.9 35.4 %all-to-all-start.2 = ((bf16[4,128,1152]{2,1,0:T(8,128)(2,1)}), bf16[4,128,1152]{2,1,0:T(8,128)(2,1)S(1)}, u32[]{:S(2)}, u32[]{:S(2)}) async-start(bf16[4,128,1152]{2,1,0:T(8,128)(2,1)} %bitcast.110), calls=%async_computation.2 | async-start | bytes 2359296 | tf_op jit(solution)/shard_map/all_to_all | solution.py:697
  102.1 1.8 collective-permute-start.8
  103.9 27.3 %copy-start.26 = (bf16[80,1152]{1,0:T(8,128)(2,1)}, bf16[80,1152]{1,0:T(8,128)(2,1)S(1)}, u32[]{:S(2)}) copy-start(bf16[80,1152]{1,0:T(8,128)(2,1)S(1)} %collective-permute-done.9.refs_9_) | copy-start | bytes 552964
  131.2 4.2 collective-permute-start.11
  133.7 36.7 %collective-permute-start.12 = (bf16[576,1152]{1,0:T(8,128)(2,1)}, bf16[576,1152]{1,0:T(8,128)(2,1)}, u32[]{:S(2)}, u32[]{:S(2)}) collective-permute-start(bf16[576,1152]{1,0:T(8,128)(2,1)} %refs_0_.2), channel_id=1, source_target_pairs={{0,8},{4,12},{8,0},{12,4},{16,24},{20,28},{24,16},{28,20},{1,9},{5... | collective-permute-start | bytes 3981320 | tf_op jit(solution)/shard_map/ppermute | solution.py:716
  134.3 36.1 %collective-permute-start.13 = (bf16[576,1152]{1,0:T(8,128)(2,1)}, bf16[576,1152]{1,0:T(8,128)(2,1)}, u32[]{:S(2)}, u32[]{:S(2)}) collective-permute-start(bf16[576,1152]{1,0:T(8,128)(2,1)} %refs_0_.2), channel_id=1, source_target_pairs={{0,16},{4,20},{8,24},{12,28},{16,0},{20,4},{24,8},{28,12},{1,17},{... | collective-permute-start | bytes 3981320 | tf_op jit(solution)/shard_map/ppermute | solution.py:716
  180.2 22.4 %collective-permute-start.15 = (bf16[4,576,1152]{2,1,0:T(8,128)(2,1)}, bf16[4,576,1152]{2,1,0:T(8,128)(2,1)}, u32[]{:S(2)}, u32[]{:S(2)}) collective-permute-start(bf16[4,576,1152]{2,1,0:T(8,128)(2,1)} %shard_map.250), channel_id=1, source_target_pairs={{0,4},{4,0},{8,12},{12,8},{16,20},{20,16},{24,28},{28,24},{1,5},{5... | collective-permute-start | bytes 15925256 | tf_op jit(solution)/shard_map/ppermute | solution.py:716
  181.4 17.4 %collective-permute-start.16 = (bf16[288,1152]{1,0:T(8,128)(2,1)S(1)}, bf16[288,1152]{1,0:T(8,128)(2,1)S(1)}, u32[]{:S(2)}, u32[]{:S(2)}) collective-permute-start(bf16[288,1152]{1,0:T(8,128)(2,1)S(1)} %slice.116), channel_id=1, source_target_pairs={{0,16},{4,20},{8,24},{12,28},{16,0},{20,4},{24,8},{28,12},{1,17},{... | collective-permute-start | bytes 1990664 | tf_op jit(solution)/shard_map/ppermute | solution.py:716
  184.1 17.1 %collective-permute-start.17 = (bf16[288,1152]{1,0:T(8,128)(2,1)S(1)}, bf16[288,1152]{1,0:T(8,128)(2,1)S(1)}, u32[]{:S(2)}, u32[]{:S(2)}) collective-permute-start(bf16[288,1152]{1,0:T(8,128)(2,1)S(1)} %slice.117), channel_id=1, source_target_pairs={{0,8},{4,12},{8,0},{12,4},{16,24},{20,28},{24,16},{28,20},{1,9},{5... | collective-permute-start | bytes 1990664 | tf_op jit(solution)/shard_map/ppermute | solution.py:716
  184.7 30.5 %collective-permute-start.18 = (bf16[576,1152]{1,0:T(8,128)(2,1)}, bf16[576,1152]{1,0:T(8,128)(2,1)}, u32[]{:S(2)}, u32[]{:S(2)}) collective-permute-start(bf16[576,1152]{1,0:T(8,128)(2,1)} %refs_0_.2), channel_id=1, source_target_pairs={{0,4},{4,0},{8,12},{12,8},{16,20},{20,16},{24,28},{28,24},{1,5},{5... | collective-permute-start | bytes 3981320 | tf_op jit(solution)/shard_map/ppermute | solution.py:716
  202.0 15.3 %collective-permute-start.19 = (bf16[576,1152]{1,0:T(8,128)(2,1)}, bf16[576,1152]{1,0:T(8,128)(2,1)}, u32[]{:S(2)}, u32[]{:S(2)}) collective-permute-start(bf16[576,1152]{1,0:T(8,128)(2,1)} %collective-permute-done.12.refs_1_), channel_id=1, source_target_pairs={{0,4},{4,0},{8,12},{12,8},{16,20},{20,16},{24,28},{28,24},{1,5},{5... | collective-permute-start | bytes 3981320 | tf_op jit(solution)/shard_map/ppermute | solution.py:716
  202.0 15.3 %collective-permute-start.20 = (bf16[576,1152]{1,0:T(8,128)(2,1)}, bf16[576,1152]{1,0:T(8,128)(2,1)}, u32[]{:S(2)}, u32[]{:S(2)}) collective-permute-start(bf16[576,1152]{1,0:T(8,128)(2,1)} %collective-permute-done.13.refs_2_), channel_id=1, source_target_pairs={{0,4},{4,0},{8,12},{12,8},{16,20},{20,16},{24,28},{28,24},{1,5},{5... | collective-permute-start | bytes 3981320 | tf_op jit(solution)/shard_map/ppermute | solution.py:716
  202.6 13.2 %collective-permute-start.21 = (bf16[288,1152]{1,0:T(8,128)(2,1)S(1)}, bf16[288,1152]{1,0:T(8,128)(2,1)}, u32[]{:S(2)}, u32[]{:S(2)}) collective-permute-start(bf16[288,1152]{1,0:T(8,128)(2,1)S(1)} %collective-permute-done.16.refs_3_), channel_id=1, source_target_pairs={{0,4},{4,0},{8,12},{12,8},{16,20},{20,16},{24,28},{28,24},{1,5},{5... | collective-permute-start | bytes 1990664 | tf_op jit(solution)/shard_map/ppermute | solution.py:716
  202.6 14.7 %collective-permute-start.22 = (bf16[288,1152]{1,0:T(8,128)(2,1)}, bf16[288,1152]{1,0:T(8,128)(2,1)}, u32[]{:S(2)}, u32[]{:S(2)}) collective-permute-start(bf16[288,1152]{1,0:T(8,128)(2,1)} %copy-done.25), channel_id=1, source_target_pairs={{0,4},{4,0},{8,12},{12,8},{16,20},{20,16},{24,28},{28,24},{1,5},{5... | collective-permute-start | bytes 1990664 | tf_op jit(solution)/shard_map/ppermute | solution.py:716
  215.2 19.3 %collective-permute-start.23 = (bf16[288,1152]{1,0:T(8,128)(2,1)}, bf16[288,1152]{1,0:T(8,128)(2,1)S(1)}, u32[]{:S(2)}, u32[]{:S(2)}) collective-permute-start(bf16[288,1152]{1,0:T(8,128)(2,1)} %get-tuple-element.144), channel_id=1, source_target_pairs={{0,8},{4,12},{8,0},{12,4},{16,24},{20,28},{24,16},{28,20},{1,9},{5... | collective-permute-start | bytes 1990664 | tf_op jit(solution)/shard_map/ppermute | solution.py:716
  215.9 18.7 %collective-permute-start.24 = (bf16[288,1152]{1,0:T(8,128)(2,1)}, bf16[288,1152]{1,0:T(8,128)(2,1)S(1)}, u32[]{:S(2)}, u32[]{:S(2)}) collective-permute-start(bf16[288,1152]{1,0:T(8,128)(2,1)} %get-tuple-element.145), channel_id=1, source_target_pairs={{0,16},{4,20},{8,24},{12,28},{16,0},{20,4},{24,8},{28,12},{1,17},{... | collective-permute-start | bytes 1990664 | tf_op jit(solution)/shard_map/ppermute | solution.py:716
  240.0 46.4 %collective-permute-start.26 = (bf16[576,1152]{1,0:T(8,128)(2,1)}, bf16[576,1152]{1,0:T(8,128)(2,1)}, u32[]{:S(2)}, u32[]{:S(2)}) collective-permute-start(bf16[576,1152]{1,0:T(8,128)(2,1)} %get-tuple-element.157), channel_id=1, source_target_pairs={{0,8},{4,12},{8,0},{12,4},{16,24},{20,28},{24,16},{28,20},{1,9},{5... | collective-permute-start | bytes 3981320 | tf_op jit(solution)/shard_map/ppermute | solution.py:716
  240.6 45.8 %collective-permute-start.27 = (bf16[576,1152]{1,0:T(8,128)(2,1)}, bf16[576,1152]{1,0:T(8,128)(2,1)}, u32[]{:S(2)}, u32[]{:S(2)}) collective-permute-start(bf16[576,1152]{1,0:T(8,128)(2,1)} %get-tuple-element.158), channel_id=1, source_target_pairs={{0,16},{4,20},{8,24},{12,28},{16,0},{20,4},{24,8},{28,12},{1,17},{... | collective-permute-start | bytes 3981320 | tf_op jit(solution)/shard_map/ppermute | solution.py:716
  262.9 26.9 %collective-permute-start.28 = (bf16[4,144,4608]{2,1,0:T(8,128)(2,1)}, bf16[4,144,4608]{2,1,0:T(8,128)(2,1)}, u32[]{:S(2)}, u32[]{:S(2)}) collective-permute-start(bf16[4,144,4608]{2,1,0:T(8,128)(2,1)} %shard_map.255), channel_id=1, source_target_pairs={{0,4},{4,0},{8,12},{12,8},{16,20},{20,16},{24,28},{28,24},{1,5},{5... | collective-permute-start | bytes 15925256 | tf_op jit(solution)/shard_map/ppermute | solution.py:716
  263.0 42.7 %all-to-all-start.3 = ((bf16[4,128,1152]{2,1,0:T(8,128)(2,1)}), bf16[4,128,1152]{2,1,0:T(8,128)(2,1)S(1)}, u32[]{:S(2)}, u32[]{:S(2)}) async-start(bf16[4,128,1152]{2,1,0:T(8,128)(2,1)} %bitcast.116), calls=%async_computation.3 | async-start | bytes 2359296 | tf_op jit(solution)/shard_map/all_to_all | solution.py:703
  267.6 99.3 %all-reduce.6.cloned.1.call-start = ((), (), s32[]{:S(2)}) async-start(), calls=%async_computation.9 | async-start | bytes 2654208 | tf_op jit(solution)/shard_map/psum | solution.py:801
  302.6 28.1 %collective-permute-start.32 = (bf16[4,144,1152]{2,1,0:T(8,128)(2,1)}, bf16[4,144,1152]{2,1,0:T(8,128)(2,1)}, u32[]{:S(2)}, u32[]{:S(2)}) collective-permute-start(bf16[4,144,1152]{2,1,0:T(8,128)(2,1)} %shard_map.258), channel_id=1, source_target_pairs={{0,4},{4,0},{8,12},{12,8},{16,20},{20,16},{24,28},{28,24},{1,5},{5... | collective-permute-start | bytes 3981320 | tf_op jit(solution)/shard_map/ppermute | solution.py:716
  302.9 4.1 collective-permute-start.29
  303.3 21.0 %collective-permute-start.30 = (bf16[72,4608]{1,0:T(8,128)(2,1)}, bf16[72,4608]{1,0:T(8,128)(2,1)}, u32[]{:S(2)}, u32[]{:S(2)}) collective-permute-start(bf16[72,4608]{1,0:T(8,128)(2,1)} %get-tuple-element.175), channel_id=1, source_target_pairs={{0,8},{4,12},{8,0},{12,4},{16,24},{20,28},{24,16},{28,20},{1,9},{5... | collective-permute-start | bytes 1990664 | tf_op jit(solution)/shard_map/ppermute | solution.py:716
  303.9 20.4 %collective-permute-start.31 = (bf16[72,4608]{1,0:T(8,128)(2,1)}, bf16[72,4608]{1,0:T(8,128)(2,1)}, u32[]{:S(2)}, u32[]{:S(2)}) collective-permute-start(bf16[72,4608]{1,0:T(8,128)(2,1)} %get-tuple-element.176), channel_id=1, source_target_pairs={{0,16},{4,20},{8,24},{12,28},{16,0},{20,4},{24,8},{28,12},{1,17},{... | collective-permute-start | bytes 1990664 | tf_op jit(solution)/shard_map/ppermute | solution.py:716
  305.4 154.6 %all-reduce.8.cloned.1.call-start = ((), (), s32[]{:S(2)}) async-start(), calls=%async_computation.10 | async-start | bytes 2654208 | tf_op jit(solution)/shard_map/psum | solution.py:801
  306.8 46.0 %collective-permute-start.25 = (bf16[2,128,1152]{2,1,0:T(8,128)(2,1)}, bf16[2,128,1152]{2,1,0:T(8,128)(2,1)}, u32[]{:S(2)}, u32[]{:S(2)}) collective-permute-start(bf16[2,128,1152]{2,1,0:T(8,128)(2,1)} %get-tuple-element.242), channel_id=1, source_target_pairs={{0,4},{4,0},{8,12},{12,8},{16,20},{20,16},{24,28},{28,24},{1,5},{5... | collective-permute-start | bytes 1769480 | tf_op jit(solution)/shard_map/ppermute | solution.py:682
  324.0 32.2 %collective-permute-start.33 = (bf16[512,896]{1,0:T(8,128)(2,1)}, bf16[512,896]{1,0:T(8,128)(2,1)}, u32[]{:S(2)}, u32[]{:S(2)}) collective-permute-start(bf16[512,896]{1,0:T(8,128)(2,1)} %get-tuple-element.183), channel_id=1, source_target_pairs={{0,4},{4,0},{8,12},{12,8},{16,20},{20,16},{24,28},{28,24},{1,5},{5... | collective-permute-start | bytes 2752520 | tf_op jit(solution)/shard_map/ppermute | solution.py:682
  328.7 38.2 %collective-permute-start.35 = (bf16[144,4608]{1,0:T(8,128)(2,1)}, bf16[144,4608]{1,0:T(8,128)(2,1)}, u32[]{:S(2)}, u32[]{:S(2)}) collective-permute-start(bf16[144,4608]{1,0:T(8,128)(2,1)} %get-tuple-element.186), channel_id=1, source_target_pairs={{0,8},{4,12},{8,0},{12,4},{16,24},{20,28},{24,16},{28,20},{1,9},{5... | collective-permute-start | bytes 3981320 | tf_op jit(solution)/shard_map/ppermute | solution.py:716
  329.2 37.7 %collective-permute-start.36 = (bf16[144,4608]{1,0:T(8,128)(2,1)}, bf16[144,4608]{1,0:T(8,128)(2,1)}, u32[]{:S(2)}, u32[]{:S(2)}) collective-permute-start(bf16[144,4608]{1,0:T(8,128)(2,1)} %get-tuple-element.187), channel_id=1, source_target_pairs={{0,16},{4,20},{8,24},{12,28},{16,0},{20,4},{24,8},{28,12},{1,17},{... | collective-permute-start | bytes 3981320 | tf_op jit(solution)/shard_map/ppermute | solution.py:716
  351.9 5.7 %collective-permute-start.34 = (bf16[512,896]{1,0:T(8,128)(2,1)}, bf16[512,896]{1,0:T(8,128)(2,1)}, u32[]{:S(2)}, u32[]{:S(2)}) collective-permute-start(bf16[512,896]{1,0:T(8,128)(2,1)} %get-tuple-element.196), channel_id=1, source_target_pairs={{0,4},{4,0},{8,12},{12,8},{16,20},{20,16},{24,28},{28,24},{1,5},{5... | collective-permute-start | bytes 2752520 | tf_op jit(solution)/shard_map/ppermute | solution.py:682
  355.6 21.3 %collective-permute-start.37 = (bf16[72,1152]{1,0:T(8,128)(2,1)}, bf16[72,1152]{1,0:T(8,128)(2,1)}, u32[]{:S(2)}, u32[]{:S(2)}) collective-permute-start(bf16[72,1152]{1,0:T(8,128)(2,1)} %get-tuple-element.192), channel_id=1, source_target_pairs={{0,8},{4,12},{8,0},{12,4},{16,24},{20,28},{24,16},{28,20},{1,9},{5... | collective-permute-start | bytes 497672 | tf_op jit(solution)/shard_map/ppermute | solution.py:716
  356.2 20.8 %collective-permute-start.38 = (bf16[72,1152]{1,0:T(8,128)(2,1)}, bf16[72,1152]{1,0:T(8,128)(2,1)}, u32[]{:S(2)}, u32[]{:S(2)}) collective-permute-start(bf16[72,1152]{1,0:T(8,128)(2,1)} %get-tuple-element.193), channel_id=1, source_target_pairs={{0,16},{4,20},{8,24},{12,28},{16,0},{20,4},{24,8},{28,12},{1,17},{... | collective-permute-start | bytes 497672 | tf_op jit(solution)/shard_map/ppermute | solution.py:716
  376.9 16.3 %collective-permute-start.39 = (bf16[4,144,3456]{2,1,0:T(8,128)(2,1)}, bf16[4,144,3456]{2,1,0:T(8,128)(2,1)}, u32[]{:S(2)}, u32[]{:S(2)}) collective-permute-start(bf16[4,144,3456]{2,1,0:T(8,128)(2,1)} %shard_map.264), channel_id=1, source_target_pairs={{0,4},{4,0},{8,12},{12,8},{16,20},{20,16},{24,28},{28,24},{1,5},{5... | collective-permute-start | bytes 11943944 | tf_op jit(solution)/shard_map/ppermute | solution.py:716
  401.1 1.4 collective-permute-start.41
  402.5 5.9 %collective-permute-start.42 = (bf16[1,6912]{1,0:T(2,128)(2,1)S(1)}, bf16[1,6912]{1,0:T(2,128)(2,1)S(1)}, u32[]{:S(2)}, u32[]{:S(2)}) collective-permute-start(bf16[1,6912]{1,0:T(2,128)(2,1)S(1)} %broadcast_in_dim.38), channel_id=1, source_target_pairs={{0,1},{1,0},{2,3},{3,2},{4,5},{5,4},{6,7},{7,6},{8,9},{9,8},{10,11... | collective-permute-start | bytes 41480 | tf_op jit(solution)/shard_map/ppermute | solution.py:856
  404.7 9.0 %all-to-all-start.5 = ((f32[8,1,1152]{2,1,0:T(1,128)}), f32[8,1,1152]{2,1,0:T(1,128)S(1)}, u32[]{:S(2)}, u32[]{:S(2)}) async-start(f32[8,1,1152]{2,1,0:T(1,128)} %all_to_all.36), calls=%async_computation.5 | async-start | bytes 73728 | tf_op jit(solution)/shard_map/all_to_all | solution.py:1008
  408.4 8.9 %collective-permute-start.43 = (bf16[2,6912]{1,0:T(2,128)(2,1)S(1)}, bf16[2,6912]{1,0:T(2,128)(2,1)S(1)}, u32[]{:S(2)}, u32[]{:S(2)}) collective-permute-start(bf16[2,6912]{1,0:T(2,128)(2,1)S(1)} %pad_maximum_fusion.4), channel_id=1, source_target_pairs={{0,2},{1,3},{2,0},{3,1},{4,6},{5,7},{6,4},{7,5},{8,10},{9,11},{10,... | collective-permute-start | bytes 82952 | tf_op jit(solution)/shard_map/ppermute | solution.py:856
  409.6 52.1 %collective-permute-start.48 = (bf16[144,1152]{1,0:T(8,128)(2,1)}, bf16[144,1152]{1,0:T(8,128)(2,1)}, u32[]{:S(2)}, u32[]{:S(2)}) collective-permute-start(bf16[144,1152]{1,0:T(8,128)(2,1)} %get-tuple-element.202), channel_id=1, source_target_pairs={{0,8},{4,12},{8,0},{12,4},{16,24},{20,28},{24,16},{28,20},{1,9},{5... | collective-permute-start | bytes 995336 | tf_op jit(solution)/shard_map/ppermute | solution.py:716
  411.6 50.1 %collective-permute-start.49 = (bf16[144,1152]{1,0:T(8,128)(2,1)}, bf16[144,1152]{1,0:T(8,128)(2,1)}, u32[]{:S(2)}, u32[]{:S(2)}) collective-permute-start(bf16[144,1152]{1,0:T(8,128)(2,1)} %get-tuple-element.203), channel_id=1, source_target_pairs={{0,16},{4,20},{8,24},{12,28},{16,0},{20,4},{24,8},{28,12},{1,17},{... | collective-permute-start | bytes 995336 | tf_op jit(solution)/shard_map/ppermute | solution.py:716
  413.0 17.4 %collective-permute-start.44 = (bf16[72,3456]{1,0:T(8,128)(2,1)}, bf16[72,3456]{1,0:T(8,128)(2,1)}, u32[]{:S(2)}, u32[]{:S(2)}) collective-permute-start(bf16[72,3456]{1,0:T(8,128)(2,1)} %get-tuple-element.211), channel_id=1, source_target_pairs={{0,8},{4,12},{8,0},{12,4},{16,24},{20,28},{24,16},{28,20},{1,9},{5... | collective-permute-start | bytes 1493000 | tf_op jit(solution)/shard_map/ppermute | solution.py:716
  413.6 18.2 %collective-permute-start.45 = (bf16[72,3456]{1,0:T(8,128)(2,1)}, bf16[72,3456]{1,0:T(8,128)(2,1)}, u32[]{:S(2)}, u32[]{:S(2)}) collective-permute-start(bf16[72,3456]{1,0:T(8,128)(2,1)} %get-tuple-element.212), channel_id=1, source_target_pairs={{0,16},{4,20},{8,24},{12,28},{16,0},{20,4},{24,8},{28,12},{1,17},{... | collective-permute-start | bytes 1493000 | tf_op jit(solution)/shard_map/ppermute | solution.py:716
  413.7 56.9 %all-to-all-start.4 = ((bf16[4,128,1152]{2,1,0:T(8,128)(2,1)}), bf16[4,128,1152]{2,1,0:T(8,128)(2,1)S(1)}, u32[]{:S(2)}, u32[]{:S(2)}) async-start(bf16[4,128,1152]{2,1,0:T(8,128)(2,1)} %bitcast.115), calls=%async_computation.4 | async-start | bytes 2359296 | tf_op jit(solution)/shard_map/all_to_all | solution.py:703
  417.2 115.0 %all-reduce.10.cloned.1.call-start = ((), (), s32[]{:S(2)}) async-start(), calls=%async_computation.11 | async-start | bytes 2764800 | tf_op jit(solution)/shard_map/psum | solution.py:801
  435.8 24.3 %collective-permute-start.46 = (bf16[4,6912]{1,0:T(4,128)(2,1)S(1)}, bf16[4,6912]{1,0:T(4,128)(2,1)S(1)}, u32[]{:S(2)}, u32[]{:S(2)}) collective-permute-start(bf16[4,6912]{1,0:T(4,128)(2,1)S(1)} %pad_maximum_fusion.3), channel_id=1, source_target_pairs={{0,8},{4,12},{8,0},{12,4},{16,24},{20,28},{24,16},{28,20},{1,9},{5... | collective-permute-start | bytes 165896 | tf_op jit(solution)/shard_map/ppermute | solution.py:716
  436.1 30.5 %collective-permute-start.50 = (bf16[144,3456]{1,0:T(8,128)(2,1)}, bf16[144,3456]{1,0:T(8,128)(2,1)}, u32[]{:S(2)}, u32[]{:S(2)}) collective-permute-start(bf16[144,3456]{1,0:T(8,128)(2,1)} %get-tuple-element.223), channel_id=1, source_target_pairs={{0,8},{4,12},{8,0},{12,4},{16,24},{20,28},{24,16},{28,20},{1,9},{5... | collective-permute-start | bytes 2985992 | tf_op jit(solution)/shard_map/ppermute | solution.py:716
  437.9 28.7 %collective-permute-start.51 = (bf16[144,3456]{1,0:T(8,128)(2,1)}, bf16[144,3456]{1,0:T(8,128)(2,1)}, u32[]{:S(2)}, u32[]{:S(2)}) collective-permute-start(bf16[144,3456]{1,0:T(8,128)(2,1)} %get-tuple-element.224), channel_id=1, source_target_pairs={{0,16},{4,20},{8,24},{12,28},{16,0},{20,4},{24,8},{28,12},{1,17},{... | collective-permute-start | bytes 2985992 | tf_op jit(solution)/shard_map/ppermute | solution.py:716
  460.1 4.8 collective-permute-start.47
  470.5 13.0 %all-to-all-start.6 = ((f32[8,1,288]{2,1,0:T(1,128)}), f32[8,1,288]{2,1,0:T(1,128)S(1)}, u32[]{:S(2)}, u32[]{:S(2)}) async-start(f32[8,1,288]{2,1,0:T(1,128)} %all_to_all.38), calls=%async_computation.6 | async-start | bytes 24576 | tf_op jit(solution)/shard_map/all_to_all | solution.py:1023
  475.3 9.0 %collective-permute-start.40 = (bf16[2,128,1152]{2,1,0:T(8,128)(2,1)}, bf16[2,128,1152]{2,1,0:T(8,128)(2,1)S(1)}, u32[]{:S(2)}, u32[]{:S(2)}) collective-permute-start(bf16[2,128,1152]{2,1,0:T(8,128)(2,1)} %get-tuple-element.240), channel_id=1, source_target_pairs={{0,4},{4,0},{8,12},{12,8},{16,20},{20,16},{24,28},{28,24},{1,5},{5... | collective-permute-start | bytes 1769480 | tf_op jit(solution)/shard_map/ppermute | solution.py:682
  (26 other events, 221.1 us)
Sparse Core Ops, SparseCore 0:
  9.9 68.1 all-gather.4
  80.0 68.7 all-gather.6
  305.5 61.3 all-reduce.5
  377.1 82.9 all-reduce.7
  470.0 62.2 all-reduce.9
